TPU v7x, 128 devices: a whole 4x4x4 slice. The times are simulated.
128 devices in a mesh: wide: 16 (over z, x_lo, core), narrow: 8 (over y, x_hi).
Axes of the slice: x: 4 (x_hi: 2, x_lo: 2; x = x_hi * 2 + x_lo), y: 4, z: 4, core: 2. Of those that a mesh axis runs over, the one named last changes fastest.
Arguments:
- signal: bfloat16 [4, 8388608], P(None, ('wide', 'narrow')), may hold values from -6 to 6
- gate: bfloat16 [4, 8388608], P(None, ('wide', 'narrow')), may hold values from -6 to 6
- skip: float32 [4], replicated, may hold values from 0.5 to 2
- spectrum: float32 [2, 4, 256, 256, 256], P(None, None, ('wide', 'narrow')), may hold values from -6 to 6
Outputs:
- mixed: bfloat16 [4, 8388608], P(None, ('wide', 'narrow'))
All inputs are finite; a program needn't handle non-finite values.
Results may differ from a plain program's by a relative error of at most 0.001.
Values may be sent and summed in bfloat16 or wider, within the bound.
No kernel may reach another device: no remote copies, remote signals or barrier semaphores. Data moves between devices by JAX's collectives and lax.ppermute only.
A program may use at most 320 MiB of HBM per device.

v0:
```python
import jax
import jax.numpy as jnp
from jax import lax
from jax.sharding import PartitionSpec as P

F1 = 256
F2 = 256
F3 = 256


full_turn = 6.283185307179586
highest = lax.Precision.HIGHEST


def angle_table(rows, cols, period):
    product = rows[:, None] * cols[None, :] % period
    return full_turn / period * product.astype(jnp.float32)


def rotate(stacked, angle, sign):
    cosine = jnp.cos(angle)
    sine = sign * jnp.sin(angle)
    real = stacked[0]
    imag = stacked[1]
    return jnp.stack([real * cosine - imag * sine, imag * cosine + real * sine])


def pair_table(angle, sign):
    cosine = jnp.cos(angle)
    sine = sign * jnp.sin(angle)
    return jnp.stack([jnp.stack([cosine, sine]), jnp.stack([-sine, cosine])])


def per_device(signal, gate, skip, spectrum):
    wide_count = lax.axis_size("wide")
    narrow_count = lax.axis_size("narrow")
    device_count = wide_count * narrow_count
    place = lax.axis_index("wide") * narrow_count + lax.axis_index("narrow")
    channels = signal.shape[0]
    inner = F2 * F3
    total = F1 * inner
    half_outer = F1 // 2
    rows_local = half_outer // device_count
    cols_local = inner // device_count
    outer_local = F1 // device_count
    blocks = signal.reshape(channels, rows_local, inner)
    spread = lax.all_to_all(blocks, ("wide", "narrow"), split_axis=2, concat_axis=1, tiled=True)
    spread = spread.astype(jnp.float32)
    outer_index = jnp.arange(F1, dtype=jnp.int32)
    half_index = jnp.arange(half_outer, dtype=jnp.int32)
    first_angle = angle_table(half_index, outer_index, F1)
    first_table = jnp.stack([jnp.cos(first_angle), -jnp.sin(first_angle)], axis=1)
    field = jnp.einsum("cnm,npk->pckm", spread, first_table, precision=highest)
    col_global = place * cols_local + jnp.arange(cols_local, dtype=jnp.int32)
    field = rotate(field, angle_table(outer_index, col_global, total), -1.0)
    field = lax.all_to_all(field, ("wide", "narrow"), split_axis=2, concat_axis=3, tiled=True)
    field = field.reshape(2, channels, outer_local, F2, F3)
    middle_index = jnp.arange(F2, dtype=jnp.int32)
    inner_index = jnp.arange(F3, dtype=jnp.int32)
    middle_angle = angle_table(middle_index, middle_index, F2)
    cross_angle = angle_table(middle_index, inner_index, inner)
    inner_angle = angle_table(inner_index, inner_index, F3)
    field = jnp.einsum(
        "pckab,pqae->qckeb", field, pair_table(middle_angle, -1.0), precision=highest
    )
    field = rotate(field, cross_angle, -1.0)
    field = jnp.einsum("pckab,pqbf->qckaf", field, pair_table(inner_angle, -1.0), precision=highest)
    filt_real = spectrum[0]
    filt_imag = spectrum[1]
    field = jnp.stack(
        [field[0] * filt_real - field[1] * filt_imag, field[0] * filt_imag + field[1] * filt_real]
    )
    field = jnp.einsum("pckab,pqbf->qckaf", field, pair_table(inner_angle, 1.0), precision=highest)
    field = rotate(field, cross_angle, 1.0)
    field = jnp.einsum("pckab,pqae->qckeb", field, pair_table(middle_angle, 1.0), precision=highest)
    field = field.reshape(2, channels, outer_local, inner)
    outer_global = place * outer_local + jnp.arange(outer_local, dtype=jnp.int32)
    inner_all = jnp.arange(inner, dtype=jnp.int32)
    field = rotate(field, angle_table(outer_global, inner_all, total), 1.0)
    field = lax.all_to_all(field, ("wide", "narrow"), split_axis=3, concat_axis=2, tiled=True)
    last_angle = angle_table(outer_index, half_index, F1)
    last_table = jnp.stack([jnp.cos(last_angle), -jnp.sin(last_angle)])
    conv = jnp.einsum("pckm,pkn->cnm", field, last_table, precision=highest) / total
    conv = lax.all_to_all(conv, ("wide", "narrow"), split_axis=1, concat_axis=2, tiled=True)
    conv = conv.reshape(channels, rows_local * inner)
    mixed = gate.astype(jnp.float32) * (conv + skip[:, None] * signal.astype(jnp.float32))
    return mixed.astype(jnp.bfloat16)


def solution(mesh):
    in_specs = (
        P(None, ("wide", "narrow")),
        P(None, ("wide", "narrow")),
        P(),
        P(None, None, ("wide", "narrow"), None, None),
    )
    out_specs = P(None, ("wide", "narrow"))
    return jax.shard_map(
        per_device, mesh=mesh, in_specs=in_specs, out_specs=out_specs, check_vma=False
    )
```

profile of v0, /device:TPU:1, one launch (start us, length us, event | category | flops | bytes accessed | tf_op | source)
XLA Modules:
  0.0 1588.8 jit_solution(1187892772403058779)
XLA Ops:
  0.0 57.9 %copy.55 = bf16[4,1,65536]{0,1,2:T(2,128)(2,1)} copy(bf16[4,1,65536]{2,0,1:T(4,128)(2,1)} %bitcast.113) | data formatting | bytes 1048576 | tf_op jit(solution)/shard_map/reshape | solution.py:46
  57.9 0.5 broadcast.677
  58.4 355.9 %reduce = bf16[65536,4]{1,0:T(8,128)(2,1)} reduce(bf16[65536,1,4]{2,1,0:T(2,128)(2,1)} %bitcast.107, bf16[]{:T(256)} %broadcast.677), dimensions={1}, to_apply=%bitcast.94.reduce_sub_computation | reduce | bytes 1048578
  414.3 31.8 %reshape.486 = bf16[128,2,1024]{2,1,0:T(2,128)(2,1)} reshape(bf16[65536,4]{1,0:T(8,128)(2,1)} %reduce) | data formatting | bytes 1048576
  446.1 11.8 all-to-all-start
  458.0 0.5 sine_negate_fusion
  458.5 2.1 fusion.50
  460.6 11.3 all-to-all-done
  471.8 67.1 %reshape.487 = bf16[65536,1,4]{2,1,0:T(2,128)(2,1)} reshape(bf16[128,2,1024]{2,1,0:T(2,128)(2,1)S(1)} %all-to-all-done) | data formatting | bytes 1048576
  538.9 60.9 %copy.56 = bf16[4,1,65536]{2,0,1:T(4,128)(2,1)S(1)} copy(bf16[4,1,65536]{0,1,2:T(2,128)(2,1)} %bitcast.108) | data formatting | bytes 1048576 | tf_op jit(solution)/shard_map/all_to_all | solution.py:47
  599.9 1.9 convolution_bitcast_fusion
  601.7 0.7 multiply_subtract_fusion.4
  602.4 0.4 pad_maximum_fusion
  602.8 4.7 copy.57
  607.5 5.4 all-to-all-start.1
  612.9 9.5 fusion.47
  622.4 4.7 fusion.80
  627.1 1.9 copy.91
  629.0 3.0 copy.92
  632.0 1.0 fusion.72
  633.0 1.7 fusion.61
  634.6 1.0 broadcast_multiply_fusion.1
  635.6 1.0 fusion.66
  636.7 1.7 broadcast_multiply_fusion
  638.4 1.2 fusion.23
  639.6 25.8 %all-to-all-done.1 = f32[2,4,256,512]{3,1,0,2:T(4,128)} async-done(((f32[2,4,256,512]{3,1,0,2:T(4,128)}), f32[2,4,256,512]{3,1,0,2:T(4,128)}, u32[]{:S(2)}, u32[]{:S(2)}) %all-to-all-start.1) | async-done | bytes 4194336 | tf_op jit(solution)/shard_map/all_to_all | solution.py:56
  665.3 6.6 copy.123
  672.0 4.9 reshape.472
  676.9 9.3 convolution_bitcast_fusion.1
  686.1 0.0 copy-done.7
  686.1 0.0 copy-start.1
  686.2 0.0 copy-start.2
  686.2 0.5 multiply_subtract_fusion.3
  686.6 0.5 copy-done.1
  687.2 0.2 copy-done.2
  687.3 7.2 fusion.8
  694.5 0.0 copy-done
  694.5 0.8 multiply_subtract_fusion.2
  695.3 7.6 fusion.11
  702.9 0.0 copy-done.6
  702.9 0.6 multiply_subtract_fusion.1
  703.5 6.8 fusion.14
  710.4 2.4 fusion.79
  712.7 3.2 squeeze.4
  716.0 4.5 squeeze.5
  720.5 4.9 multiply_subtract_fusion
  725.4 2.9 pad_maximum_fusion.3
  728.3 130.0 %copy.71 = f32[2,4,2,65536]{1,2,0,3:T(2,128)} copy(f32[2,4,2,65536]{3,1,2,0:T(4,128)} %pad_maximum_fusion.3) | data formatting | bytes 8388608 | tf_op jit(solution)/shard_map/stack | solution.py:25
  858.3 205.6 %reshape.488 = f32[128,1,8192]{2,1,0:T(1,128)} reshape(f32[65536,2,2,4]{3,2,1,0:T(2,128)} %bitcast.96) | data formatting | bytes 8388608
  1063.9 5.5 all-to-all-start.2
  1069.4 0.5 sine_negate_fusion.1
  1069.9 52.0 %all-to-all-done.2 = f32[128,1,8192]{2,1,0:T(1,128)} async-done(((f32[128,1,8192]{2,1,0:T(1,128)}), f32[128,1,8192]{2,1,0:T(1,128)}, u32[]{:S(2)}, u32[]{:S(2)}) %all-to-all-start.2) | async-done | bytes 4194336 | tf_op jit(solution)/shard_map/all_to_all | solution.py:80
  1122.0 0.5 broadcast.678
  1122.5 13.8 reduce.1
  1136.3 272.1 %reshape.489 = f32[65536,2,2,4]{3,2,1,0:T(2,128)} reshape(f32[128,8192]{1,0:T(8,128)} %reduce.1) | data formatting | bytes 8388608
  1408.4 143.3 %copy.72 = f32[2,4,2,128,512]{4,2,3,0,1:T(2,128)} copy(f32[2,4,2,128,512]{1,2,0,4,3:T(2,128)} %bitcast.35) | data formatting | bytes 8388608 | tf_op jit(solution)/shard_map/all_to_all | solution.py:80
  1551.7 6.2 all_to_all.48
  1557.9 4.6 fusion.18
  1562.5 0.0 copy-start.3
  1562.5 0.0 copy-start.8
  1562.5 0.0 copy-start.9
  1562.5 0.7 copy.73
  1563.2 24.0 %all_to_all.54 = f32[4,128,512]{2,0,1:T(4,128)S(1)} all-to-all(f32[4,128,512]{2,0,1:T(4,128)S(1)} %copy.73), channel_id=1, replica_groups=mesh['wide'=16,'narrow'=8] {'wide','narrow'}, dimensions={1} | all-to-all | bytes 2097152 | tf_op jit(solution)/shard_map/all_to_all | solution.py:84
  1587.3 1.3 multiply_convert_fusion
  (12 shorter events, 0.0 us)
Async XLA Ops:
  446.1 25.7 %all-to-all-start = ((bf16[128,2,1024]{2,1,0:T(2,128)(2,1)}), bf16[128,2,1024]{2,1,0:T(2,128)(2,1)S(1)}, u32[]{:S(2)}, u32[]{:S(2)}) async-start(bf16[128,2,1024]{2,1,0:T(2,128)(2,1)} %reshape.486), calls=%async_computation | async-start | bytes 1048576 | tf_op jit(solution)/shard_map/all_to_all | solution.py:47
  607.5 57.8 %all-to-all-start.1 = ((f32[2,4,256,512]{3,1,0,2:T(4,128)}), f32[2,4,256,512]{3,1,0,2:T(4,128)}, u32[]{:S(2)}, u32[]{:S(2)}) async-start(f32[2,4,256,512]{3,1,0,2:T(4,128)} %copy.57), calls=%async_computation.1 | async-start | bytes 8388608 | tf_op jit(solution)/shard_map/all_to_all | solution.py:56
  676.9 9.3 copy-start.7
  686.1 1.0 copy-start.1
  686.2 1.2 copy-start.2
  687.3 7.2 copy-start
  695.3 7.6 copy-start.6
  716.0 4.5 copy-start.4
  716.0 4.5 copy-start.5
  1063.9 58.1 %all-to-all-start.2 = ((f32[128,1,8192]{2,1,0:T(1,128)}), f32[128,1,8192]{2,1,0:T(1,128)}, u32[]{:S(2)}, u32[]{:S(2)}) async-start(f32[128,1,8192]{2,1,0:T(1,128)} %reshape.488), calls=%async_computation.2 | async-start | bytes 8388608 | tf_op jit(solution)/shard_map/all_to_all | solution.py:80
  1562.5 24.7 %copy-start.3 = (bf16[4,65536]{1,0:T(4,128)(2,1)S(1)}, bf16[4,65536]{1,0:T(4,128)(2,1)}, u32[]{:S(2)}) copy-start(bf16[4,65536]{1,0:T(4,128)(2,1)} %param.4) | copy-start | bytes 1572868
  1562.5 24.7 %copy-start.8 = (bf16[4,65536]{1,0:T(4,128)(2,1)S(1)}, bf16[4,65536]{1,0:T(4,128)(2,1)}, u32[]{:S(2)}) copy-start(bf16[4,65536]{1,0:T(4,128)(2,1)} %param.5) | copy-start | bytes 1572868
  1562.5 24.7 %copy-start.9 = (f32[4]{0:T(128)S(1)}, f32[4]{0:T(128)}, u32[]{:S(2)}) copy-start(f32[4]{0:T(128)} %param.6) | copy-start | bytes 52
where the time goes:
time: 1620 us; the launch traced here: 1590 us
  local copies, waits for them, and re-layouts  1010 us (62%)
  other arithmetic  402 us (25%)
  waiting for transfers between devices  89.1 us (6%)
  matrix products  37.3 us (2%)
  blocking collectives  24 us (1%)
  starting transfers between devices  22.7 us (1%)
    unnamed x27, local copies, waits for them, and re-layouts  583 us
    unnamed x1, other arithmetic  356 us
    all_to_all x3, local copies, waits for them, and re-layouts, per_device(): lax.all_to_all(field, ('wide', 'narrow'), split_axis=3, concat_axis=2, ti...  150 us
    another operation x2, local copies, waits for them, and re-layouts, rotate(): return jnp.stack([real * cosine - imag * sine, imag * cosine + real * sine])  135 us
    all_to_all x1, local copies, waits for them, and re-layouts, per_device(): lax.all_to_all(blocks, ('wide', 'narrow'), split_axis=2, concat_axis=1, t...  60.9 us
    reshape x1, local copies, waits for them, and re-layouts, per_device(): blocks = signal.reshape(channels, rows_local, inner)  57.9 us
    all_to_all x1, waiting for transfers between devices, per_device(): lax.all_to_all(field, ('wide', 'narrow'), split_axis=3, concat_axis=2, ti...  52 us
  transfers between devices with their start and end apart: 3, of which 3 were waited for; matrix products, arithmetic and copies ran while one was open for 2% of the time, Pallas kernels for 0%

commit v1 on v0

v1 whole, which is shorter than its diff:
```python
import jax
import jax.numpy as jnp
import ml_dtypes
import numpy as np
from jax import lax
from jax.experimental import pallas as pl
from jax.experimental.pallas import tpu as pltpu
from jax.sharding import PartitionSpec as P

F = 256
ND = 128
HALF = 32768
AXES = ("wide", "narrow")
bf16 = jnp.bfloat16
f32 = jnp.float32

OFFSET = 120.0 * np.log(2.0)
SPAN = 240.0
FIELD_CODE = (2.0**-8, 15.1)
FILTERED_CODE = (2.0**-11, 22.2)
CONV_CODE = (2.0**-7, 21.7)


def split_np(x):
    hi = x.astype(ml_dtypes.bfloat16)
    lo = (x - hi.astype(np.float64)).astype(ml_dtypes.bfloat16)
    return hi, lo


def outer_forward_table():
    k1 = np.arange(F).reshape(ND, 2)
    n = np.arange(ND)
    ang = 2 * np.pi * (k1[:, :, None] * n % F) / F
    t = np.zeros((ND, 2, 2, 2, 2, ND))
    for c in range(2):
        t[:, :, c, 0, c, :] = np.cos(ang)
        t[:, :, c, 1, c, :] = -np.sin(ang)
    return np.concatenate(split_np(t.reshape(ND * 8, 2 * ND)), axis=1)


def outer_inverse_table():
    k1 = np.arange(F).reshape(ND, 2)
    n = np.arange(ND)
    ang = 2 * np.pi * (n[:, None, None] * k1[None] % F) / F
    t = np.zeros((2, ND, ND, 2, 2, 2))
    for c in range(2):
        t[c, :, :, :, c, 0] = np.cos(ang)
        t[c, :, :, :, c, 1] = -np.sin(ang)
    return np.concatenate(split_np(t.reshape(2 * ND, ND * 8)), axis=1)


def inner_tables():
    i = np.arange(F)
    ang = 2 * np.pi * (i[:, None] * i[None] % F) / F
    c, s = np.cos(ang), np.sin(ang)
    fwd = np.block([[c, -s], [s, c]])
    inv = np.block([[c, s], [-s, c]]) / F
    return np.concatenate(split_np(fwd), axis=0), np.concatenate(split_np(inv), axis=0)


def base_tables():
    i = np.arange(F)
    a0 = 2 * np.pi * (i[:, None] * i[None] % F) / F
    a1 = 2 * np.pi * (i[:, None] * i[None]) / (F * F)
    return np.stack([np.cos(a0), np.sin(a0), np.cos(a1), np.sin(a1)]).astype(np.float32)


def peak_of(peak_ref):
    return jnp.maximum(jnp.max(peak_ref[...], keepdims=True), 1e-30)


def encode(x, peak, code):
    knee, octaves = code
    beta = SPAN / octaves
    z = jnp.abs(x) * (1.0 / (peak * knee))
    y = jnp.exp(jnp.minimum(beta * jnp.log(1.0 + z) - OFFSET, OFFSET))
    return jnp.where(x < 0, -y, y)


def decode(y, peak, code):
    knee, octaves = code
    beta = SPAN / octaves
    z = jnp.exp(jnp.log(jnp.abs(y)) * (1.0 / beta) + OFFSET / beta) - 1.0
    z = z * (peak * knee)
    return jnp.where(y < 0, -z, z)


def split(x):
    hi = x.astype(bf16)
    return hi, (x - hi.astype(f32)).astype(bf16)


def dot(a, b):
    return jnp.dot(a, b, preferred_element_type=f32)


def pack_kernel(sig_ref, out_ref, peak_ref, buf):
    peak_ref[...] = jnp.zeros((8, 128), f32)
    top = jnp.zeros((4, 128), f32)
    for q in range(ND):
        for i in range(4):
            x = sig_ref[:, pl.ds((i // 2) * HALF + q * F + (i % 2) * 128, 128)].astype(f32)
            top = jnp.maximum(top, jnp.abs(x))
            buf[pl.ds(q * 16 + i * 4, 4), :] = x
    peak_ref[pl.ds(0, 4), :] = top
    out_ref[...] = buf[...].reshape(ND, 16, 128).astype(bf16)


def outer_kernel(x_ref, table_ref, peak_ref, out0_ref, out1_ref, buf):
    peak = peak_of(peak_ref)
    buf[...] = x_ref[...].astype(f32).reshape(ND * 16, 128)
    for pair, out_ref in enumerate((out0_ref, out1_ref)):
        rows = []
        for c in range(2):
            parts = [buf[pl.ds(i * 4 + pair * 2 + c, ND, stride=16), :] for i in range(4)]
            rows.append(jnp.concatenate(parts, axis=1).astype(bf16))
        x = jnp.concatenate(rows, axis=0)
        for m in range(4):
            t = table_ref[pl.ds(m * 256, 256), :]
            res = dot(t[:, :256], x) + dot(t[:, 256:], x)
            res = encode(res, peak, FIELD_CODE)
            low = res[:, :F].reshape(32, 8, F)
            high = res[:, F:].reshape(32, 8, F)
            out_ref[pl.ds(m * 32, 32)] = jnp.concatenate([low, high], axis=1).astype(bf16)


def table_kernel(base_ref, lane_ref, sub_ref, mf_ref, mi_ref, cross_ref):
    c0, s0, c1, s1 = (base_ref[i] for i in range(4))
    for r in range(2):
        cb, sb = lane_ref[r, 0], lane_ref[r, 1]
        c, s = c0 * cb - s0 * sb, s0 * cb + c0 * sb
        (ch, cl), (sh, sl) = split(c), split(s)
        for part, (cc, ss) in enumerate(((ch, sh), (cl, sl))):
            lo = part * 512
            mf_ref[r, 0:256, lo : lo + 256] = cc
            mf_ref[r, 0:256, lo + 256 : lo + 512] = ss
            mf_ref[r, 256:512, lo : lo + 256] = -ss
            mf_ref[r, 256:512, lo + 256 : lo + 512] = cc
        cb, sb = sub_ref[r, 0], sub_ref[r, 1]
        c, s = (c0 * cb - s0 * sb) * (1.0 / F), (s0 * cb + c0 * sb) * (1.0 / F)
        (ch, cl), (sh, sl) = split(c), split(s)
        for part, (cc, ss) in enumerate(((ch, sh), (cl, sl))):
            lo = part * 512
            mi_ref[r, 0:256, lo : lo + 256] = cc
            mi_ref[r, 0:256, lo + 256 : lo + 512] = -ss
            mi_ref[r, 256:512, lo : lo + 256] = ss
            mi_ref[r, 256:512, lo + 256 : lo + 512] = cc
        cb, sb = lane_ref[r, 2], lane_ref[r, 3]
        cross_ref[r, 0] = c1 * cb - s1 * sb
        cross_ref[r, 1] = s1 * cb + c1 * sb


def middle_kernel(pair, y_ref, peak_ref, mf_ref, mi_ref, cross_ref, fwd_ref, inv_ref, filt_ref, out_ref, buf, obuf):
    peak = peak_of(peak_ref)
    for m in range(4):
        y = decode(y_ref[pl.ds(m * 32, 32)].astype(f32), peak, FIELD_CODE)
        y = y.reshape(512, F)
        for g in range(2):
            buf[g, pl.ds(m * 512, 512), :] = y[:, g * 128 : (g + 1) * 128]

    for r in range(2):
        cosine, sine = cross_ref[r, 0], cross_ref[r, 1]
        cols = []
        for c in range(2):
            cols.append(
                jnp.concatenate(
                    [
                        jnp.concatenate(
                            [buf[g, pl.ds(h * 8 + r * 4 + c * 2 + ri, ND, stride=16), :] for g in range(2)], axis=1
                        )
                        for ri in range(2)
                        for h in range(2)
                    ],
                    axis=0,
                )
            )
        hi, lo = split(jnp.concatenate(cols, axis=1))
        mf = mf_ref[r]
        z = dot(mf[:, :512], hi) + dot(mf[:, :512], lo) + dot(mf[:, 512:], hi)
        rows = []
        for c in range(2):
            zr, zi = z[:256, c * F : (c + 1) * F], z[256:, c * F : (c + 1) * F]
            rows.append(jnp.concatenate([zr * cosine + zi * sine, zi * cosine - zr * sine], axis=1))
        hi, lo = split(jnp.concatenate(rows, axis=0))
        fh, fl = fwd_ref[0:512, :], fwd_ref[512:1024, :]
        z = dot(hi, fh) + dot(lo, fh) + dot(hi, fl)
        rows = []
        for c in range(2):
            zr, zi = z[c * F : (c + 1) * F, :256], z[c * F : (c + 1) * F, 256:]
            fr, fi = filt_ref[0, c, r], filt_ref[1, c, r]
            rows.append(jnp.concatenate([zr * fr - zi * fi, zi * fr + zr * fi], axis=1))
        hi, lo = split(jnp.concatenate(rows, axis=0))
        fh, fl = inv_ref[0:512, :], inv_ref[512:1024, :]
        z = dot(hi, fh) + dot(lo, fh) + dot(hi, fl)
        cosine, sine = cosine * (1.0 / F), sine * (1.0 / F)
        cols = []
        for c in range(2):
            zr, zi = z[c * F : (c + 1) * F, :256], z[c * F : (c + 1) * F, 256:]
            cols.append(jnp.concatenate([zr * cosine - zi * sine, zi * cosine + zr * sine], axis=0))
        hi, lo = split(jnp.concatenate(cols, axis=1))
        mi = mi_ref[r]
        z = dot(mi[:, :512], hi) + dot(mi[:, :512], lo) + dot(mi[:, 512:], hi)
        for c in range(2):
            for ri in range(2):
                for h in range(2):
                    for g in range(2):
                        obuf[g, pl.ds(h * 8 + r * 4 + c * 2 + ri, ND, stride=16), :] = z[
                            ri * 256 + h * 128 : ri * 256 + (h + 1) * 128, c * F + g * 128 : c * F + (g + 1) * 128
                        ]
    for m in range(4):
        y = jnp.concatenate([obuf[g, pl.ds(m * 512, 512), :] for g in range(2)], axis=1)
        y = encode(y, peak, FILTERED_CODE)
        out_ref[pl.ds(m * 32, 32)] = y.reshape(32, 16, F).astype(bf16)


def last_kernel(y_ref, table_ref, peak_ref, out_ref, buf):
    peak = peak_of(peak_ref)
    for h in range(2):
        acc = jnp.zeros((256, F), f32)
        for m in range(4):
            y = y_ref[pl.ds(m * 32, 32)].astype(f32)[:, h * 8 : (h + 1) * 8, :]
            hi, lo = split(decode(y.reshape(256, F), peak, FILTERED_CODE))
            th = table_ref[:, m * 256 : (m + 1) * 256]
            tl = table_ref[:, 1024 + m * 256 : 1024 + (m + 1) * 256]
            acc = acc + dot(th, hi) + dot(th, lo) + dot(tl, hi)
        for c in range(2):
            for b in range(2):
                buf[pl.ds(h * 4 + b * 2 + c, ND, stride=8), :] = acc[
                    c * ND : (c + 1) * ND, b * 128 : (b + 1) * 128
                ]
    out_ref[...] = encode(buf[...], peak, CONV_CODE).reshape(ND, 8, 128).astype(bf16)


def finish_kernel(y0_ref, y1_ref, sig_ref, gate_ref, skip_ref, peak_ref, out_ref, buf0, buf1, conv):
    peak = peak_of(peak_ref)
    for y_ref, buf in ((y0_ref, buf0), (y1_ref, buf1)):
        buf[...] = decode(y_ref[...].astype(f32).reshape(ND * 8, 128), peak, CONV_CODE)
    for q in range(ND):
        for i in range(4):
            at = pl.ds((i // 2) * HALF + q * F + (i % 2) * 128, 128)
            conv[pl.ds(0, 2), at] = buf0[pl.ds(q * 8 + i * 2, 2), :]
            conv[pl.ds(2, 2), at] = buf1[pl.ds(q * 8 + i * 2, 2), :]
    skip = skip_ref[...]
    for i in range(16):
        at = pl.ds(i * 4096, 4096)
        total = conv[:, at] + skip * sig_ref[:, at].astype(f32)
        out_ref[:, at] = (gate_ref[:, at].astype(f32) * total).astype(bf16)


VMEM = pl.BlockSpec(memory_space=pltpu.VMEM)


def call(kernel, ins, outs, scratch, name, flops=0, limit=48):
    size = sum(int(np.prod(x.shape)) * x.dtype.itemsize for x in (*ins, *outs))
    return pl.pallas_call(
        kernel,
        in_specs=[VMEM] * len(ins),
        out_specs=[VMEM] * len(outs),
        out_shape=outs,
        scratch_shapes=[pltpu.VMEM(s, f32) for s in scratch],
        compiler_params=pltpu.CompilerParams(vmem_limit_bytes=limit * 2**20),
        cost_estimate=pl.CostEstimate(flops=flops, bytes_accessed=size, transcendentals=0),
        name=name,
    )(*ins)


def exchange(x):
    return lax.all_to_all(x, AXES, split_axis=0, concat_axis=0, tiled=True)


def shape(*dims, dtype=bf16):
    return jax.ShapeDtypeStruct(dims, dtype)


def per_device(signal, gate, skip, spectrum):
    place = lax.axis_index("wide") * lax.axis_size("narrow") + lax.axis_index("narrow")
    packed, peak = call(
        pack_kernel, (signal,), [shape(ND, 16, 128), shape(8, 128, dtype=f32)], [(ND * 16, 128)], "pack"
    )
    spread = exchange(packed)
    peak = lax.pmax(peak, AXES)

    k1 = (place * 2 + jnp.arange(2, dtype=jnp.int32))[:, None] * jnp.arange(F, dtype=jnp.int32)
    mid = (2 * np.pi / (F * F)) * (k1 % (F * F)).astype(f32)
    fine = (2 * np.pi / (F * F * F)) * k1.astype(f32)
    lane = jnp.stack([jnp.cos(mid), jnp.sin(mid), jnp.cos(fine), jnp.sin(fine)], axis=1)
    mf, mi, cross = call(
        table_kernel,
        (jnp.asarray(base_tables()), lane[:, :, None, :], lane[:, :2, :, None]),
        [shape(2, 512, 1024), shape(2, 512, 1024), shape(2, 2, F, F, dtype=f32)],
        [],
        "tables",
    )
    inner_fwd, inner_inv = (jnp.asarray(t) for t in inner_tables())

    field = call(
        outer_kernel,
        (spread, jnp.asarray(outer_forward_table()), peak),
        [shape(ND, 16, F)] * 2,
        [(ND * 16, 128)],
        "outer",
        flops=2**30,
    )
    field = [exchange(y) for y in field]
    table = jnp.asarray(outer_inverse_table())
    conv = []
    for pair in range(2):
        (filtered,) = call(
            lambda *refs, pair=pair: middle_kernel(pair, *refs),
            (field[pair], peak, mf, mi, cross, inner_fwd, inner_inv, spectrum[:, 2 * pair : 2 * pair + 2]),
            [shape(ND, 16, F)],
            [(2, ND * 16, 128)] * 2,
            "middle",
            flops=6 * 2**30,
        )
        filtered = exchange(filtered)
        (part,) = call(last_kernel, (filtered, table, peak), [shape(ND, 8, 128)], [(ND * 8, 128)], "last", flops=2**29)
        conv.append(exchange(part))
    (mixed,) = call(
        finish_kernel,
        (*conv, signal, gate, skip[:, None], peak),
        [shape(4, 65536)],
        [(ND * 8, 128), (ND * 8, 128), (4, 65536)],
        "finish",
    )
    return mixed


def solution(mesh):
    split_spec = P(None, AXES)
    return jax.shard_map(
        per_device,
        mesh=mesh,
        in_specs=(split_spec, split_spec, P(), P(None, None, AXES, None, None)),
        out_specs=split_spec,
        check_vma=False,
    )
```

time: 1620 us -> 228 us (0.14); the launches traced: 1590 us -> 227 us
  local copies, waits for them, and re-layouts: 1010 us -> 12.7 us
  other arithmetic: 402 us -> 0.24 us
  blocking collectives: 24 us -> 67.5 us
  Pallas kernels: 0 us -> 41.7 us
  matrix products: 37.3 us -> 0 us
  waiting for transfers between devices: 89.1 us -> 59.5 us
  starting transfers between devices: 22.7 us -> 45.1 us
    unnamed x27 -> x32, local copies, waits for them, and re-layouts: 583 us -> 6.51 us
    unnamed x1 -> x0, other arithmetic: 356 us -> none
    all_to_all x5 -> x0, local copies, waits for them, and re-layouts: 218 us -> none  [the longest x3 150 us: per_device(): lax.all_to_all(field, ('wide', 'narrow'), split_axis=3, concat_axis=2, ti...]
    another operation x2 -> x0, local copies, waits for them, and re-layouts: 135 us -> none  [rotate(): return jnp.stack([real * cosine - imag * sine, imag * cosine + real * sine])]
    pmax x0 -> x1, blocking collectives: none -> 67.5 us  [per_device(): peak = lax.pmax(peak, AXES)]
    reshape x2 -> x0, local copies, waits for them, and re-layouts: 62.8 us -> none  [the longest x1 57.9 us: per_device(): blocks = signal.reshape(channels, rows_local, inner)]
    pallas_call x0 -> x8, Pallas kernels: none -> 41.7 us  [call(): pl.pallas_call(kernel, in_specs=[VMEM] * len(ins), out_specs=[VMEM] * len...]
    dot_general x6 -> x0, matrix products: 37.3 us -> none  [the longest x1 9.25 us: per_device(): jnp.einsum('pckab,pqae->qckeb', field, pair_table(middle_angle, -1.0), pr...]
  transfers between devices with their start and end apart: 3 -> 7, of which waited for: 3 -> 5; matrix products, arithmetic and copies ran while one was open for 2% -> 3% of each run, Pallas kernels for 0% -> 16%
where the time goes in v1:
time: 228 us; the launch traced here: 227 us
  blocking collectives  67.5 us (30%)
  waiting for transfers between devices  59.5 us (26%)
  starting transfers between devices  45.1 us (20%)
  Pallas kernels  41.7 us (18%)
  local copies, waits for them, and re-layouts  12.7 us (6%)
    pmax x1, blocking collectives, per_device(): peak = lax.pmax(peak, AXES)  67.5 us
    all_to_all x7, waiting for transfers between devices, exchange(): return lax.all_to_all(x, AXES, split_axis=0, concat_axis=0, tiled=True)  59.5 us
    all_to_all x7, starting transfers between devices, exchange(): return lax.all_to_all(x, AXES, split_axis=0, concat_axis=0, tiled=True)  45.1 us
    pallas_call x8, Pallas kernels, call(): pl.pallas_call(kernel, in_specs=[VMEM] * len(ins), out_specs=[VMEM] * len...  41.7 us
    unnamed x32, local copies, waits for them, and re-layouts  6.51 us
    slice x1, local copies, waits for them, and re-layouts, per_device(): spectrum[:, 2 * pair:2 * pair + 2]  5.85 us
  transfers between devices with their start and end apart: 7, of which 5 were waited for; matrix products, arithmetic and copies ran while one was open for 3% of the time, Pallas kernels for 16%

profile of v1, /device:TPU:1, one launch (start us, length us, event | category | flops | bytes accessed | tf_op | source)
XLA Modules:
  0.0 226.9 jit_solution(7185997296820864458)
XLA Ops:
  0.0 0.0 copy-start.1
  0.0 1.0 copy-done.1
  1.0 1.3 pack.1
  2.4 11.5 %all-to-all-start = ((bf16[128,16,128]{2,1,0:T(8,128)(2,1)}), bf16[128,16,128]{2,1,0:T(8,128)(2,1)S(1)}, u32[]{:S(2)}, u32[]{:S(2)}) async-start(bf16[128,16,128]{2,1,0:T(8,128)(2,1)} %get-tuple-element.12), calls=%async_computation | async-start | bytes 1048576 | tf_op jit(solution)/shard_map/all_to_all | solution.py:268
  13.9 67.5 %pmax.7.peak_ref.refs_1_ = f32[8,128]{1,0:T(8,128)S(1)} all-reduce(f32[8,128]{1,0:T(8,128)S(1)} %get-tuple-element.13), channel_id=1, replica_groups=mesh['wide'=16,'narrow'=8] {'wide','narrow'}, use_global_device_ids=true, to_apply=%region_0.0 | all-reduce | flops 1024 | bytes 8192 | tf_op jit(solution)/shard_map/pmax | solution.py:281
  81.4 0.0 all-to-all-done.x_ref
  81.4 0.0 copy-start.14
  81.4 1.2 copy-done.14
  82.6 2.7 %outer.1 = (bf16[128,16,256]{2,1,0:T(8,128)(2,1)}, bf16[128,16,256]{2,1,0:T(8,128)(2,1)S(1)}) custom-call(bf16[128,16,128]{2,1,0:T(8,128)(2,1)S(1)} %all-to-all-done.x_ref, bf16[1024,512]{1,0:T(8,128)(2,1)S(1)} %copy-done.14, f32[8,128]{1,0:T(8,128)S(1)} %pmax.7.peak_ref.refs_1_), custom_call_target="tpu_custom_call" | custom-call | flops 1073741824 | bytes 3674112 | tf_op jit(solution)/shard_map/outer/pallas_call | solution.py:255
  85.3 0.0 copy-start.4
  85.3 1.0 copy-done.4
  86.2 0.0 copy-start.3
  86.2 4.7 %all-to-all-start.4 = ((bf16[128,16,256]{2,1,0:T(8,128)(2,1)}), bf16[128,16,256]{2,1,0:T(8,128)(2,1)S(1)}, u32[]{:S(2)}, u32[]{:S(2)}) async-start(bf16[128,16,256]{2,1,0:T(8,128)(2,1)} %copy-done.4), calls=%async_computation.4 | async-start | bytes 2097152 | tf_op jit(solution)/shard_map/all_to_all | solution.py:268
  91.0 0.2 fusion.6
  91.2 19.3 %all-to-all-done.4.refs_0_ = bf16[128,16,256]{2,1,0:T(8,128)(2,1)S(1)} async-done(((bf16[128,16,256]{2,1,0:T(8,128)(2,1)}), bf16[128,16,256]{2,1,0:T(8,128)(2,1)S(1)}, u32[]{:S(2)}, u32[]{:S(2)}) %all-to-all-start.4) | async-done | bytes 1048608 | tf_op jit(solution)/shard_map/all_to_all | solution.py:268
  110.5 4.9 %all-to-all-start.1 = ((bf16[128,16,256]{2,1,0:T(8,128)(2,1)}), bf16[128,16,256]{2,1,0:T(8,128)(2,1)}, u32[]{:S(2)}, u32[]{:S(2)}) async-start(bf16[128,16,256]{2,1,0:T(8,128)(2,1)} %get-tuple-element.14), calls=%async_computation.1 | async-start | bytes 2097152 | tf_op jit(solution)/shard_map/all_to_all | solution.py:268
  115.4 0.2 copy.12.sub_ref
  115.6 0.0 copy-done.3
  115.6 2.0 tables.1
  117.6 0.0 copy-start.7
  117.6 0.0 copy-start.8
  117.6 0.0 copy-start.10
  117.6 0.0 copy-start.12
  117.6 5.8 %fusion.7 = (f32[2,2,2,256,256]{4,3,2,1,0:T(8,128)}, f32[2,2,2,256,256]{4,3,2,1,0:T(8,128)}) fusion(f32[2,4,2,256,256]{4,3,2,1,0:T(8,128)} %param.12), kind=kLoop, calls=%fused_computation.15 | loop fusion | bytes 8388608 | tf_op jit(solution)/shard_map/slice | solution.py:310
  123.5 0.0 copy-done.7
  123.5 0.0 copy-done.8
  123.5 0.0 copy-done.10
  123.5 0.0 copy-done.12
  123.5 14.4 %middle.3 = bf16[128,16,256]{2,1,0:T(8,128)(2,1)} custom-call(bf16[128,16,256]{2,1,0:T(8,128)(2,1)S(1)} %all-to-all-done.4.refs_0_, f32[8,128]{1,0:T(8,128)S(1)} %pmax.7.peak_ref.refs_1_, bf16[2,512,1024]{2,1,0:T(8,128)(2,1)} %copy-done.7, bf16[2,512,1024]{2,1,0:T(8,128)(2,1)} %get-tuple-element.16.refs_3_, ...), custom_call_target="tpu_custom_call" | custom-call | flops 6442450944 | bytes 11538432 | tf_op jit(solution)/shard_map/middle/pallas_call | solution.py:255
  137.9 0.0 copy-start.9
  137.9 0.0 copy-start.11
  137.9 0.0 all-to-all-done.1.refs_0_
  137.9 9.8 %all-to-all-start.5 = ((bf16[128,16,256]{2,1,0:T(8,128)(2,1)}), bf16[128,16,256]{2,1,0:T(8,128)(2,1)S(1)}, u32[]{:S(2)}, u32[]{:S(2)}) async-start(bf16[128,16,256]{2,1,0:T(8,128)(2,1)} %middle.3), calls=%async_computation.5 | async-start | bytes 2097152 | tf_op jit(solution)/shard_map/all_to_all | solution.py:268
  147.7 0.0 copy-done.9
  147.7 0.0 copy-done.11
  147.7 0.0 copy-start.13
  147.7 1.2 copy-done.13
  148.9 13.6 %middle.2 = bf16[128,16,256]{2,1,0:T(8,128)(2,1)S(1)} custom-call(bf16[128,16,256]{2,1,0:T(8,128)(2,1)} %all-to-all-done.1.refs_0_, f32[8,128]{1,0:T(8,128)S(1)} %pmax.7.peak_ref.refs_1_, bf16[2,512,1024]{2,1,0:T(8,128)(2,1)} %copy-done.7, bf16[2,512,1024]{2,1,0:T(8,128)(2,1)} %get-tuple-element.16.refs_3_, f32[2,2,256,256]{3,2,1,0:T(8,128)S(1)} %copy-done.9, ...), custom_call_target="tpu_custom_call" | custom-call | flops 6442450944 | bytes 11538432 | tf_op jit(solution)/shard_map/middle/pallas_call | solution.py:255
  162.5 0.0 copy-start.5
  162.5 1.0 copy-done.5
  163.5 0.0 copy-start
  163.5 3.7 %all-to-all-done.5.y_ref = bf16[128,16,256]{2,1,0:T(8,128)(2,1)S(1)} async-done(((bf16[128,16,256]{2,1,0:T(8,128)(2,1)}), bf16[128,16,256]{2,1,0:T(8,128)(2,1)S(1)}, u32[]{:S(2)}, u32[]{:S(2)}) %all-to-all-start.5) | async-done | bytes 1048608 | tf_op jit(solution)/shard_map/all_to_all | solution.py:268
  167.2 6.1 %all-to-all-start.2 = ((bf16[128,16,256]{2,1,0:T(8,128)(2,1)}), bf16[128,16,256]{2,1,0:T(8,128)(2,1)S(1)}, u32[]{:S(2)}, u32[]{:S(2)}) async-start(bf16[128,16,256]{2,1,0:T(8,128)(2,1)} %copy-done.5), calls=%async_computation.2 | async-start | bytes 2097152 | tf_op jit(solution)/shard_map/all_to_all | solution.py:268
  173.3 0.0 copy-done
  173.3 2.7 %last.3 = bf16[128,8,128]{2,1,0:T(8,128)(2,1)} custom-call(bf16[128,16,256]{2,1,0:T(8,128)(2,1)S(1)} %all-to-all-done.5.y_ref, bf16[256,2048]{1,0:T(8,128)(2,1)S(1)} %copy-done, f32[8,128]{1,0:T(8,128)S(1)} %pmax.7.peak_ref.refs_1_), custom_call_target="tpu_custom_call" | custom-call | flops 536870912 | bytes 2363392 | tf_op jit(solution)/shard_map/last/pallas_call | solution.py:255
  176.0 0.0 copy-start.15
  176.0 0.0 copy-start.2
  176.0 16.8 %all-to-all-done.2.y_ref = bf16[128,16,256]{2,1,0:T(8,128)(2,1)S(1)} async-done(((bf16[128,16,256]{2,1,0:T(8,128)(2,1)}), bf16[128,16,256]{2,1,0:T(8,128)(2,1)S(1)}, u32[]{:S(2)}, u32[]{:S(2)}) %all-to-all-start.2) | async-done | bytes 1048608 | tf_op jit(solution)/shard_map/all_to_all | solution.py:268
  192.8 4.0 %all-to-all-start.6 = ((bf16[128,8,128]{2,1,0:T(8,128)(2,1)}), bf16[128,8,128]{2,1,0:T(8,128)(2,1)S(1)}, u32[]{:S(2)}, u32[]{:S(2)}) async-start(bf16[128,8,128]{2,1,0:T(8,128)(2,1)} %last.3), calls=%async_computation.6 | async-start | bytes 524288 | tf_op jit(solution)/shard_map/all_to_all | solution.py:268
  196.8 2.7 %last.2 = bf16[128,8,128]{2,1,0:T(8,128)(2,1)} custom-call(bf16[128,16,256]{2,1,0:T(8,128)(2,1)S(1)} %all-to-all-done.2.y_ref, bf16[256,2048]{1,0:T(8,128)(2,1)S(1)} %copy-done, f32[8,128]{1,0:T(8,128)S(1)} %pmax.7.peak_ref.refs_1_), custom_call_target="tpu_custom_call" | custom-call | flops 536870912 | bytes 2363392 | tf_op jit(solution)/shard_map/last/pallas_call | solution.py:255
  199.5 8.6 %all-to-all-done.6.y1_ref = bf16[128,8,128]{2,1,0:T(8,128)(2,1)S(1)} async-done(((bf16[128,8,128]{2,1,0:T(8,128)(2,1)}), bf16[128,8,128]{2,1,0:T(8,128)(2,1)S(1)}, u32[]{:S(2)}, u32[]{:S(2)}) %all-to-all-start.6) | async-done | bytes 262176 | tf_op jit(solution)/shard_map/all_to_all | solution.py:268
  208.1 4.2 %all-to-all-start.3 = ((bf16[128,8,128]{2,1,0:T(8,128)(2,1)}), bf16[128,8,128]{2,1,0:T(8,128)(2,1)S(1)}, u32[]{:S(2)}, u32[]{:S(2)}) async-start(bf16[128,8,128]{2,1,0:T(8,128)(2,1)} %last.2), calls=%async_computation.3 | async-start | bytes 524288 | tf_op jit(solution)/shard_map/all_to_all | solution.py:268
  212.2 0.0 copy-done.15
  212.3 0.1 copy.13.skip_ref
  212.4 11.2 %all-to-all-done.3.y0_ref = bf16[128,8,128]{2,1,0:T(8,128)(2,1)S(1)} async-done(((bf16[128,8,128]{2,1,0:T(8,128)(2,1)}), bf16[128,8,128]{2,1,0:T(8,128)(2,1)S(1)}, u32[]{:S(2)}, u32[]{:S(2)}) %all-to-all-start.3) | async-done | bytes 262176 | tf_op jit(solution)/shard_map/all_to_all | solution.py:268
  223.5 0.0 copy-done.2
  223.5 0.0 copy-start.6
  223.5 1.0 copy-done.6
  224.6 2.3 %finish.1 = bf16[4,65536]{1,0:T(4,128)(2,1)} custom-call(bf16[128,8,128]{2,1,0:T(8,128)(2,1)S(1)} %all-to-all-done.3.y0_ref, bf16[128,8,128]{2,1,0:T(8,128)(2,1)S(1)} %all-to-all-done.6.y1_ref, bf16[4,65536]{1,0:T(4,128)(2,1)S(1)} %copy-done.2, bf16[4,65536]{1,0:T(4,128)(2,1)S(1)} %copy-done.6, f32[4,1]{1,0:T(4,128)S(1)} %copy.13.skip_ref, ...), custom_call_target="tpu_custom_call" | custom-call | bytes 2101264 | tf_op jit(solution)/shard_map/finish/pallas_call | solution.py:255
  (4 shorter events, 0.0 us)
Async XLA Ops:
  0.0 1.0 copy-start.1
  2.4 79.0 %all-to-all-start = ((bf16[128,16,128]{2,1,0:T(8,128)(2,1)}), bf16[128,16,128]{2,1,0:T(8,128)(2,1)S(1)}, u32[]{:S(2)}, u32[]{:S(2)}) async-start(bf16[128,16,128]{2,1,0:T(8,128)(2,1)} %get-tuple-element.12), calls=%async_computation | async-start | bytes 1048576 | tf_op jit(solution)/shard_map/all_to_all | solution.py:268
  81.4 1.2 copy-start.14
  85.3 1.0 copy-start.4
  86.2 29.4 %copy-start.3 = (f32[4,256,256]{2,1,0:T(8,128)S(1)}, f32[4,256,256]{2,1,0:T(8,128)}, u32[]{:S(2)}) copy-start(f32[4,256,256]{2,1,0:T(8,128)} %constant.42.clone.base_ref) | copy-start | bytes 3145732
  86.2 24.2 %all-to-all-start.4 = ((bf16[128,16,256]{2,1,0:T(8,128)(2,1)}), bf16[128,16,256]{2,1,0:T(8,128)(2,1)S(1)}, u32[]{:S(2)}, u32[]{:S(2)}) async-start(bf16[128,16,256]{2,1,0:T(8,128)(2,1)} %copy-done.4), calls=%async_computation.4 | async-start | bytes 2097152 | tf_op jit(solution)/shard_map/all_to_all | solution.py:268
  110.5 27.4 %all-to-all-start.1 = ((bf16[128,16,256]{2,1,0:T(8,128)(2,1)}), bf16[128,16,256]{2,1,0:T(8,128)(2,1)}, u32[]{:S(2)}, u32[]{:S(2)}) async-start(bf16[128,16,256]{2,1,0:T(8,128)(2,1)} %get-tuple-element.14), calls=%async_computation.1 | async-start | bytes 2097152 | tf_op jit(solution)/shard_map/all_to_all | solution.py:268
  117.6 5.9 %copy-start.7 = (bf16[2,512,1024]{2,1,0:T(8,128)(2,1)}, bf16[2,512,1024]{2,1,0:T(8,128)(2,1)S(1)}, u32[]{:S(2)}) copy-start(bf16[2,512,1024]{2,1,0:T(8,128)(2,1)S(1)} %get-tuple-element.15.refs_2_) | copy-start | bytes 6291460
  117.6 5.9 %copy-start.8 = (f32[2,2,256,256]{3,2,1,0:T(8,128)}, f32[2,2,256,256]{3,2,1,0:T(8,128)S(1)}, u32[]{:S(2)}) copy-start(f32[2,2,256,256]{3,2,1,0:T(8,128)S(1)} %get-tuple-element.17.refs_4_) | copy-start | bytes 3145732
  117.6 5.9 %copy-start.10 = (bf16[1024,512]{1,0:T(8,128)(2,1)S(1)}, bf16[1024,512]{1,0:T(8,128)(2,1)}, u32[]{:S(2)}) copy-start(bf16[1024,512]{1,0:T(8,128)(2,1)} %constant.43.clone.refs_5_) | copy-start | bytes 3145732
  117.6 5.9 %copy-start.12 = (bf16[1024,512]{1,0:T(8,128)(2,1)S(1)}, bf16[1024,512]{1,0:T(8,128)(2,1)}, u32[]{:S(2)}) copy-start(bf16[1024,512]{1,0:T(8,128)(2,1)} %constant.44.clone.refs_6_) | copy-start | bytes 3145732
  137.9 9.8 %copy-start.9 = (f32[2,2,256,256]{3,2,1,0:T(8,128)S(1)}, f32[2,2,256,256]{3,2,1,0:T(8,128)}, u32[]{:S(2)}) copy-start(f32[2,2,256,256]{3,2,1,0:T(8,128)} %copy-done.8) | copy-start | bytes 3145732
  137.9 9.8 %copy-start.11 = (bf16[1024,512]{1,0:T(8,128)(2,1)S(1)}, bf16[1024,512]{1,0:T(8,128)(2,1)}, u32[]{:S(2)}) copy-start(bf16[1024,512]{1,0:T(8,128)(2,1)} %constant.43.clone.refs_5_) | copy-start | bytes 3145732
  137.9 29.3 %all-to-all-start.5 = ((bf16[128,16,256]{2,1,0:T(8,128)(2,1)}), bf16[128,16,256]{2,1,0:T(8,128)(2,1)S(1)}, u32[]{:S(2)}, u32[]{:S(2)}) async-start(bf16[128,16,256]{2,1,0:T(8,128)(2,1)} %middle.3), calls=%async_computation.5 | async-start | bytes 2097152 | tf_op jit(solution)/shard_map/all_to_all | solution.py:268
  147.7 1.2 copy-start.13
  162.5 1.0 copy-start.5
  163.5 9.8 %copy-start = (bf16[256,2048]{1,0:T(8,128)(2,1)S(1)}, bf16[256,2048]{1,0:T(8,128)(2,1)}, u32[]{:S(2)}) copy-start(bf16[256,2048]{1,0:T(8,128)(2,1)} %constant.46.clone.table_ref) | copy-start | bytes 3145732
  167.2 25.6 %all-to-all-start.2 = ((bf16[128,16,256]{2,1,0:T(8,128)(2,1)}), bf16[128,16,256]{2,1,0:T(8,128)(2,1)S(1)}, u32[]{:S(2)}, u32[]{:S(2)}) async-start(bf16[128,16,256]{2,1,0:T(8,128)(2,1)} %copy-done.5), calls=%async_computation.2 | async-start | bytes 2097152 | tf_op jit(solution)/shard_map/all_to_all | solution.py:268
  176.0 36.3 %copy-start.15 = (f32[4]{0:T(128)S(1)}, f32[4]{0:T(128)}, u32[]{:S(2)}) copy-start(f32[4]{0:T(128)} %param.11) | copy-start | bytes 52
  176.0 47.6 %copy-start.2 = (bf16[4,65536]{1,0:T(4,128)(2,1)S(1)}, bf16[4,65536]{1,0:T(4,128)(2,1)}, u32[]{:S(2)}) copy-start(bf16[4,65536]{1,0:T(4,128)(2,1)} %sig_ref.3) | copy-start | bytes 1572868
  192.8 15.3 %all-to-all-start.6 = ((bf16[128,8,128]{2,1,0:T(8,128)(2,1)}), bf16[128,8,128]{2,1,0:T(8,128)(2,1)S(1)}, u32[]{:S(2)}, u32[]{:S(2)}) async-start(bf16[128,8,128]{2,1,0:T(8,128)(2,1)} %last.3), calls=%async_computation.6 | async-start | bytes 524288 | tf_op jit(solution)/shard_map/all_to_all | solution.py:268
  208.1 15.4 %all-to-all-start.3 = ((bf16[128,8,128]{2,1,0:T(8,128)(2,1)}), bf16[128,8,128]{2,1,0:T(8,128)(2,1)S(1)}, u32[]{:S(2)}, u32[]{:S(2)}) async-start(bf16[128,8,128]{2,1,0:T(8,128)(2,1)} %last.2), calls=%async_computation.3 | async-start | bytes 524288 | tf_op jit(solution)/shard_map/all_to_all | solution.py:268
  223.5 1.0 copy-start.6

commit v2 on v1

v2 whole, which is shorter than its diff:
```python
import jax
import jax.numpy as jnp
import ml_dtypes
import numpy as np
from jax import lax
from jax.experimental import pallas as pl
from jax.experimental.pallas import tpu as pltpu
from jax.sharding import PartitionSpec as P

F = 256
ND = 128
STEPS = 4
ROWS = ND // STEPS
AXES = ("wide", "narrow")
bf16 = jnp.bfloat16
f32 = jnp.float32

OFFSET = 120.0 * np.log(2.0)
SPAN = 240.0
FIELD_CODE = (2.0**-8, 15.1)
FILTERED_CODE = (2.0**-11, 22.2)
CONV_CODE = (2.0**-7, 21.7)


def split_np(x):
    hi = x.astype(ml_dtypes.bfloat16)
    lo = (x - hi.astype(np.float64)).astype(ml_dtypes.bfloat16)
    return hi, lo


def outer_forward_table():
    k1 = np.arange(F).reshape(ND, 2)
    n = np.arange(ND)
    ang = 2 * np.pi * (k1[:, :, None] * n % F) / F
    t = np.zeros((ND, 2, 2, 2, 2, ND))
    for c in range(2):
        t[:, :, c, 0, c, :] = np.cos(ang)
        t[:, :, c, 1, c, :] = -np.sin(ang)
    return np.concatenate(split_np(t.reshape(ND * 8, 2 * ND)), axis=1)


def outer_inverse_table():
    k1 = np.arange(F).reshape(ND, 2)
    n = np.arange(ND)
    ang = 2 * np.pi * (n[:, None, None] * k1[None] % F) / F
    t = np.zeros((2, ND, ND, 2, 2, 2))
    for c in range(2):
        t[c, :, :, :, c, 0] = np.cos(ang)
        t[c, :, :, :, c, 1] = -np.sin(ang)
    hi, lo = (x.reshape(2 * ND, STEPS, -1) for x in split_np(t.reshape(2 * ND, ND * 8)))
    return np.ascontiguousarray(np.concatenate([hi, hi, lo], axis=2).transpose(1, 0, 2))


def inner_tables():
    i = np.arange(F)
    ang = 2 * np.pi * (i[:, None] * i[None] % F) / F
    c, s = np.cos(ang), np.sin(ang)
    fwd = split_np(np.block([[c, -s], [s, c]]))
    inv = split_np(np.block([[c, s], [-s, c]]) / F)
    return tuple(np.concatenate([hi, hi, lo], axis=0) for hi, lo in (fwd, inv))


def base_tables():
    i = np.arange(F)
    half = np.arange(ND)
    a0 = 2 * np.pi * (half[:, None] * half[None] % ND) / ND
    a1 = 2 * np.pi * (i[:, None] * i[None]) / (F * F)
    return (
        np.stack([np.cos(a0), np.sin(a0)]).astype(np.float32),
        np.stack([np.cos(a1), np.sin(a1)]).astype(np.float32),
    )


def peak_of(peak_ref):
    return jnp.maximum(jnp.max(peak_ref[...], keepdims=True), 1e-30)


def encode(x, peak, code):
    knee, octaves = code
    beta = SPAN / octaves
    z = jnp.abs(x) * (1.0 / (peak * knee))
    y = jnp.exp(jnp.minimum(beta * jnp.log(1.0 + z) - OFFSET, OFFSET))
    return jnp.where(x < 0, -y, y)


def decode(y, peak, code):
    knee, octaves = code
    beta = SPAN / octaves
    z = jnp.exp(jnp.log(jnp.abs(y)) * (1.0 / beta) + OFFSET / beta) - 1.0
    z = z * (peak * knee)
    return jnp.where(y < 0, -z, z)


def split(x):
    hi = x.astype(bf16)
    return hi, (x - hi.astype(f32)).astype(bf16)


def dot(a, b):
    return jnp.dot(a, b, preferred_element_type=f32)


def twice(hi, lo, axis):
    return jnp.concatenate([hi, lo, hi], axis=axis)


def pack_kernel(sig_ref, out_ref):
    top = jnp.zeros((4, 128), f32)
    for q in range(ND):
        x = sig_ref[:, pl.ds(q * 512, 512)]
        out_ref[q, :, pl.ds(0, 512)] = x
        x = jnp.abs(x.astype(f32))
        for i in range(4):
            top = jnp.maximum(top, x[:, i * 128 : (i + 1) * 128])
    top = top.astype(bf16)
    for q in range(ND):
        out_ref[q, :, pl.ds(512, 128)] = top


def outer_kernel(x_ref, table_ref, out_ref, peak_ref, buf, xs):
    @pl.when(pl.program_id(0) == 0)
    def _():
        top = jnp.zeros((4, 128), f32)
        for n in range(ND):
            x = x_ref[n].astype(f32)
            top = jnp.maximum(top, x[:, 512:640])
            for i in range(4):
                buf[i, pl.ds(n * 8, 4), :] = x[:, i * 128 : (i + 1) * 128]
        peak_ref[...] = jnp.broadcast_to(jnp.maximum(jnp.max(top, keepdims=True), 1e-30), (8, 128))
        for c in range(4):
            parts = [buf[i, pl.ds(c, ND, stride=8), :] for i in range(4)]
            xs[pl.ds(c * ND, ND), :] = jnp.concatenate(parts, axis=1).astype(bf16)

    peak = peak_ref[0:1, 0:1]
    t = table_ref[...]
    outs = []
    for pair in range(2):
        x = xs[pl.ds(pair * 256, 256), :]
        res = encode(dot(t, jnp.concatenate([x, x], axis=0)), peak, FIELD_CODE)
        outs.append(res[:, :F].reshape(ROWS, 8, F))
        outs.append(res[:, F:].reshape(ROWS, 8, F))
    out_ref[...] = jnp.concatenate(outs, axis=1).astype(bf16)


def table_kernel(base_ref, cross_base_ref, lane_ref, cross_lane_ref, sub_ref, mf_ref, mi_ref, cross_ref):
    c0, s0 = base_ref[0], base_ref[1]
    c1, s1 = cross_base_ref[0], cross_base_ref[1]
    for r in range(2):
        for out_ref, vec_ref, sign in ((mf_ref, lane_ref, 1.0), (mi_ref, sub_ref, -1.0)):
            cb, sb = vec_ref[r, 0], vec_ref[r, 1]
            c, s = c0 * cb - s0 * sb, (s0 * cb + c0 * sb) * sign
            if sign < 0:
                c, s = c * (1.0 / F), s * (1.0 / F)
            (ch, cl), (sh, sl) = split(c), split(s)
            for part, (cc, ss) in enumerate(((ch, sh), (ch, sh), (cl, sl))):
                at = part * 256
                out_ref[r, 0:128, at : at + 128] = cc
                out_ref[r, 0:128, at + 128 : at + 256] = ss
                out_ref[r, 128:256, at : at + 128] = -ss
                out_ref[r, 128:256, at + 128 : at + 256] = cc
        cb, sb = cross_lane_ref[r, 0], cross_lane_ref[r, 1]
        cross_ref[r, 0] = c1 * cb - s1 * sb
        cross_ref[r, 1] = s1 * cb + c1 * sb


def middle_kernel(y_ref, peak_ref, mf_ref, mi_ref, cross_ref, turn_ref, fwd_ref, inv_ref, filt_ref, out_ref, buf, obuf):
    peak = peak_ref[0:1, 0:1]
    for m in range(STEPS):
        y = decode(y_ref[pl.ds(m * ROWS, ROWS)].astype(f32), peak, FIELD_CODE).reshape(ROWS * 16, F)
        for g in range(2):
            buf[g, pl.ds(m * ROWS * 16, ROWS * 16), :] = y[:, g * 128 : (g + 1) * 128]

    for r in range(2):
        tc, ts = turn_ref[r, 0], turn_ref[r, 1]
        parts = []
        for ri in range(2):
            parts.append(
                jnp.concatenate(
                    [
                        buf[g, pl.ds(h * 8 + r * 4 + c * 2 + ri, ND, stride=16), :]
                        for c in range(2)
                        for h in range(2)
                        for g in range(2)
                    ],
                    axis=1,
                )
            )
        hi, lo = split(jnp.concatenate(parts, axis=0))
        z = dot(mf_ref[r], twice(hi, lo, 0))
        rows = []
        for c in range(2):
            at = c * 512
            dr, di = z[:128, at : at + 256], z[128:, at : at + 256]
            er, ei = z[:128, at + 256 : at + 512], z[128:, at + 256 : at + 512]
            pr, pi = er * tc + ei * ts, ei * tc - er * ts
            for zr, zi, e in ((dr + pr, di + pi, 0), (dr - pr, di - pi, 128)):
                cosine, sine = cross_ref[r, 0, e : e + 128], cross_ref[r, 1, e : e + 128]
                rows.append(jnp.concatenate([zr * cosine + zi * sine, zi * cosine - zr * sine], axis=1))
        hi, lo = split(jnp.concatenate(rows, axis=0))
        z = dot(twice(hi, lo, 1), fwd_ref[...])
        rows = []
        for c in range(2):
            zr, zi = z[c * F : (c + 1) * F, :256], z[c * F : (c + 1) * F, 256:]
            fr, fi = filt_ref[0, c, r], filt_ref[1, c, r]
            rows.append(jnp.concatenate([zr * fr - zi * fi, zi * fr + zr * fi], axis=1))
        hi, lo = split(jnp.concatenate(rows, axis=0))
        z = dot(twice(hi, lo, 1), inv_ref[...])
        tops, bottoms = [], []
        for c in range(2):
            both = []
            for e in (0, 128):
                at = c * F + e
                zr, zi = z[at : at + 128, :256], z[at : at + 128, 256:]
                cosine = cross_ref[r, 0, e : e + 128] * (1.0 / F)
                sine = cross_ref[r, 1, e : e + 128] * (1.0 / F)
                both.append((zr * cosine - zi * sine, zi * cosine + zr * sine))
            (ar, ai), (br, bi) = both
            ur, ui = ar - br, ai - bi
            tops += [ar + br, ur * tc - ui * ts]
            bottoms += [ai + bi, ui * tc + ur * ts]
        hi, lo = split(jnp.concatenate([jnp.concatenate(tops, axis=1), jnp.concatenate(bottoms, axis=1)], axis=0))
        z = dot(mi_ref[r], twice(hi, lo, 0))
        for c in range(2):
            for ri in range(2):
                for h in range(2):
                    for g in range(2):
                        at = c * 512 + h * 256 + g * 128
                        obuf[g, pl.ds(h * 8 + r * 4 + c * 2 + ri, ND, stride=16), :] = z[
                            ri * 128 : (ri + 1) * 128, at : at + 128
                        ]
    for m in range(STEPS):
        y = jnp.concatenate([obuf[g, pl.ds(m * ROWS * 16, ROWS * 16), :] for g in range(2)], axis=1)
        out_ref[pl.ds(m * ROWS, ROWS)] = encode(y, peak, FILTERED_CODE).reshape(ROWS, 16, F).astype(bf16)


def last_kernel(y_ref, table_ref, peak_ref, out_ref, acc, buf):
    peak = peak_ref[0:1, 0:1]
    step = pl.program_id(0)

    @pl.when(step == 0)
    def _():
        acc[...] = jnp.zeros(acc.shape, f32)

    y = decode(y_ref[...].astype(f32), peak, FILTERED_CODE)
    t = table_ref[0]
    for pair in range(2):
        for h in range(2):
            at = pair * 16 + h * 8
            hi, lo = split(y[:, at : at + 8, :].reshape(ROWS * 8, F))
            acc[pair, h] += dot(t, twice(hi, lo, 0))

    @pl.when(step == STEPS - 1)
    def _():
        for pair in range(2):
            for h in range(2):
                for c in range(2):
                    for g in range(2):
                        buf[pl.ds(h * 8 + g * 4 + pair * 2 + c, ND, stride=16), :] = acc[
                            pair, h, c * ND : (c + 1) * ND, g * 128 : (g + 1) * 128
                        ]
        out_ref[...] = encode(buf[...], peak, CONV_CODE).reshape(ND, 16, 128).astype(bf16)


def finish_kernel(y_ref, sig_ref, gate_ref, skip_ref, peak_ref, out_ref, buf):
    peak = peak_ref[0:1, 0:1]
    buf[...] = decode(y_ref[...].astype(f32).reshape(ND * 16, 128), peak, CONV_CODE)
    skip = skip_ref[...]
    for q in range(ND):
        at = pl.ds(q * 512, 512)
        conv = jnp.concatenate([buf[pl.ds(q * 16 + i * 4, 4), :] for i in range(4)], axis=1)
        total = conv + skip * sig_ref[:, at].astype(f32)
        out_ref[:, at] = (gate_ref[:, at].astype(f32) * total).astype(bf16)


VMEM = pl.BlockSpec(memory_space=pltpu.VMEM)


def call(kernel, ins, outs, scratch, name, flops=0, limit=48, grid=(), in_specs=None, out_specs=None):
    size = sum(int(np.prod(x.shape)) * x.dtype.itemsize for x in (*ins, *outs))
    return pl.pallas_call(
        kernel,
        grid=grid,
        in_specs=in_specs or [VMEM] * len(ins),
        out_specs=out_specs or [VMEM] * len(outs),
        out_shape=outs,
        scratch_shapes=[pltpu.VMEM(s, d) for s, d in scratch],
        compiler_params=pltpu.CompilerParams(vmem_limit_bytes=limit * 2**20),
        cost_estimate=pl.CostEstimate(flops=flops, bytes_accessed=size, transcendentals=0),
        name=name,
    )(*ins)


def exchange(x):
    return lax.all_to_all(x, AXES, split_axis=0, concat_axis=0, tiled=True)


def shape(*dims, dtype=bf16):
    return jax.ShapeDtypeStruct(dims, dtype)


def per_device(signal, gate, skip, spectrum):
    place = lax.axis_index("wide") * lax.axis_size("narrow") + lax.axis_index("narrow")
    (packed,) = call(pack_kernel, (signal,), [shape(ND, 4, 640)], [], "pack")
    spread = exchange(packed)

    k1 = place * 2 + jnp.arange(2, dtype=jnp.int32)[:, None]
    half = jnp.arange(ND, dtype=jnp.int32)

    def wave(index, period):
        angle = (2 * np.pi / period) * (index % period).astype(f32)
        return jnp.stack([jnp.cos(angle), jnp.sin(angle)], axis=1)

    mid = wave(k1 * half, F * ND)
    fine = wave(k1 * jnp.arange(F, dtype=jnp.int32), F**3)
    turn = wave(k1 + F * half, F * F)
    base, cross_base = (jnp.asarray(t) for t in base_tables())
    mf, mi, cross = call(
        table_kernel,
        (base, cross_base, mid[:, :, None, :], fine[:, :, None, :], mid[:, :, :, None]),
        [shape(2, 256, 768), shape(2, 256, 768), shape(2, 2, F, F, dtype=f32)],
        [],
        "tables",
    )
    inner_fwd, inner_inv = (jnp.asarray(t) for t in inner_tables())

    field, peak = call(
        outer_kernel,
        (spread, jnp.asarray(outer_forward_table())),
        [shape(ND, 32, F), shape(8, 128, dtype=f32)],
        [((4, ND * 8, 128), f32), ((ND * 4, 512), bf16)],
        "outer",
        flops=2**30,
        grid=(STEPS,),
        in_specs=[VMEM, pl.BlockSpec((ROWS * 8, 512), lambda i: (i, 0))],
        out_specs=[pl.BlockSpec((ROWS, 32, F), lambda i: (i, 0, 0)), pl.BlockSpec((8, 128), lambda i: (0, 0))],
    )
    field = exchange(field)
    pair_spec = pl.BlockSpec((ND, 16, F), lambda i: (0, i, 0))
    (filtered,) = call(
        middle_kernel,
        (field, peak, mf, mi, cross, turn[:, :, :, None], inner_fwd, inner_inv, spectrum),
        [shape(ND, 32, F)],
        [((2, ND * 16, 128), f32)] * 2,
        "middle",
        flops=9 * 2**30,
        grid=(2,),
        in_specs=[pair_spec] + [VMEM] * 7 + [pl.BlockSpec((2, 2, 2, F, F), lambda i: (0, i, 0, 0, 0))],
        out_specs=[pair_spec],
    )
    filtered = exchange(filtered)
    (conv,) = call(
        last_kernel,
        (filtered, jnp.asarray(outer_inverse_table()), peak),
        [shape(ND, 16, 128)],
        [((2, 2, 2 * ND, F), f32), ((ND * 16, 128), f32)],
        "last",
        flops=2**30,
        grid=(STEPS,),
        in_specs=[
            pl.BlockSpec((ROWS, 32, F), lambda i: (i, 0, 0)),
            pl.BlockSpec((1, 2 * ND, ROWS * 24), lambda i: (i, 0, 0)),
            VMEM,
        ],
        out_specs=[VMEM],
    )
    conv = exchange(conv)
    (mixed,) = call(
        finish_kernel,
        (conv, signal, gate, skip[:, None], peak),
        [shape(4, 65536)],
        [((ND * 16, 128), f32)],
        "finish",
    )
    return mixed


def solution(mesh):
    split_spec = P(None, AXES)
    return jax.shard_map(
        per_device,
        mesh=mesh,
        in_specs=(split_spec, split_spec, P(), P(None, None, AXES, None, None)),
        out_specs=split_spec,
        check_vma=False,
    )
```

time: 228 us -> 154 us (0.68)
  starting transfers between devices: 45.1 us -> 9.1 us
  waiting for transfers between devices: 59.5 us -> 42 us
  Pallas kernels: 41.7 us -> 33.9 us
  local copies, waits for them, and re-layouts: 12.7 us -> 6.29 us
  blocking collectives: 67.5 us -> 61.9 us
    pmax x1 -> x0, blocking collectives: 67.5 us -> none  [per_device(): peak = lax.pmax(peak, AXES)]
    all_to_all x0 -> x2, blocking collectives: none -> 61.9 us  [exchange(): return lax.all_to_all(x, AXES, split_axis=0, concat_axis=0, tiled=True)]
    all_to_all x7 -> x2, starting transfers between devices: 45.1 us -> 9.1 us  [exchange(): return lax.all_to_all(x, AXES, split_axis=0, concat_axis=0, tiled=True)]
    all_to_all x7 -> x2, waiting for transfers between devices: 59.5 us -> 42 us  [exchange(): return lax.all_to_all(x, AXES, split_axis=0, concat_axis=0, tiled=True)]
    pallas_call x8 -> x6, Pallas kernels: 41.7 us -> 33.9 us  [call(): pl.pallas_call(kernel, grid=grid, in_specs=in_specs or [VMEM] * len(ins),...]
    slice x1 -> x0, local copies, waits for them, and re-layouts: 5.85 us -> none  [per_device(): spectrum[:, 2 * pair:2 * pair + 2]]
    unnamed x32 -> x24, local copies, waits for them, and re-layouts: 6.51 us -> 5.9 us
  transfers between devices with their start and end apart: 7 -> 2, of which waited for: 5 -> 2; matrix products, arithmetic and copies ran while one was open for 3% -> 0% of each run, Pallas kernels for 16% -> 0%
where the time goes in v2:
time: 154 us
  blocking collectives  61.9 us (40%)
  waiting for transfers between devices  42 us (27%)
  Pallas kernels  33.9 us (22%)
  starting transfers between devices  9.1 us (6%)
  local copies, waits for them, and re-layouts  6.29 us (4%)
    all_to_all x2, blocking collectives, exchange(): return lax.all_to_all(x, AXES, split_axis=0, concat_axis=0, tiled=True)  61.9 us
    all_to_all x2, waiting for transfers between devices, exchange(): return lax.all_to_all(x, AXES, split_axis=0, concat_axis=0, tiled=True)  42 us
    pallas_call x6, Pallas kernels, call(): pl.pallas_call(kernel, grid=grid, in_specs=in_specs or [VMEM] * len(ins),...  33.9 us
    all_to_all x2, starting transfers between devices, exchange(): return lax.all_to_all(x, AXES, split_axis=0, concat_axis=0, tiled=True)  9.1 us
    unnamed x24, local copies, waits for them, and re-layouts  5.9 us
  transfers between devices with their start and end apart: 2, of which 2 were waited for; matrix products, arithmetic and copies ran while one was open for 0% of the time, Pallas kernels for 0%

profile of v2, /device:TPU:1, one launch (start us, length us, event | category | flops | bytes accessed | tf_op | source)
XLA Modules:
  0.0 153.7 jit_solution(10043754129552986982)
XLA Ops:
  0.0 0.0 copy-start
  0.0 1.0 copy-done
  1.0 0.0 copy-start.10
  1.0 0.6 pack.1
  1.6 26.7 %all_to_all.20.x_ref = bf16[128,4,640]{2,1,0:T(4,128)(2,1)S(1)} all-to-all(bf16[128,4,640]{2,1,0:T(4,128)(2,1)S(1)} %pack.1), channel_id=1, replica_groups=mesh['wide'=16,'narrow'=8] {'wide','narrow'}, dimensions={0} | all-to-all | bytes 1310720 | tf_op jit(solution)/shard_map/all_to_all | solution.py:294
  28.3 0.0 copy-done.10
  28.3 4.2 %outer.1 = (bf16[128,32,256]{2,1,0:T(8,128)(2,1)}, f32[8,128]{1,0:T(8,128)S(1)}) custom-call(bf16[128,4,640]{2,1,0:T(4,128)(2,1)S(1)} %all_to_all.20.x_ref, bf16[1024,512]{1,0:T(8,128)(2,1)S(1)} %copy-done.10), custom_call_target="tpu_custom_call" | custom-call | flops 1073741824 | bytes 3805184 | tf_op jit(solution)/shard_map/outer/pallas_call | solution.py:280
  32.5 0.0 copy-start.4
  32.5 0.0 copy-start.5
  32.5 4.8 %all-to-all-start.1 = ((bf16[128,32,256]{2,1,0:T(8,128)(2,1)}), bf16[128,32,256]{2,1,0:T(8,128)(2,1)}, u32[]{:S(2)}, u32[]{:S(2)}) async-start(bf16[128,32,256]{2,1,0:T(8,128)(2,1)} %get-tuple-element.10), calls=%async_computation.1 | async-start | bytes 4194304 | tf_op jit(solution)/shard_map/all_to_all | solution.py:294
  37.4 0.2 fusion.10
  37.6 0.2 fusion.14
  37.7 0.1 copy.17.sub_ref
  37.9 0.1 copy.18.turn_ref
  38.1 0.0 copy-done.4
  38.1 0.0 copy-done.5
  38.1 0.5 tables.1
  38.5 0.0 copy-start.6
  38.5 0.9 copy-done.6
  39.4 28.1 %all-to-all-done.1.y_ref = bf16[128,32,256]{2,1,0:T(8,128)(2,1)} async-done(((bf16[128,32,256]{2,1,0:T(8,128)(2,1)}), bf16[128,32,256]{2,1,0:T(8,128)(2,1)}, u32[]{:S(2)}, u32[]{:S(2)}) %all-to-all-start.1) | async-done | bytes 2097184 | tf_op jit(solution)/shard_map/all_to_all | solution.py:294
  67.5 0.0 copy-start.7
  67.5 1.1 copy-done.7
  68.7 0.0 copy-start.8
  68.7 1.4 copy-done.8
  70.1 0.0 copy-start.9
  70.1 1.4 copy-done.9
  71.5 20.6 %middle.1 = bf16[128,32,256]{2,1,0:T(8,128)(2,1)} custom-call(bf16[128,32,256]{2,1,0:T(8,128)(2,1)} %all-to-all-done.1.y_ref, f32[8,128]{1,0:T(8,128)S(1)} %get-tuple-element.11.peak_ref, bf16[2,256,768]{2,1,0:T(8,128)(2,1)S(1)} %get-tuple-element.12.mf_ref, bf16[2,256,768]{2,1,0:T(8,128)(2,1)S(1)} %copy-done.7, ...), custom_call_target="tpu_custom_call" | custom-call | flops 9663676416 | bytes 14161920 | tf_op jit(solution)/shard_map/middle/pallas_call | solution.py:280
  92.1 0.0 copy-start.2
  92.1 35.2 %all_to_all.21.y_ref = bf16[128,32,256]{2,1,0:T(8,128)(2,1)S(1)} all-to-all(bf16[128,32,256]{2,1,0:T(8,128)(2,1)} %middle.1), channel_id=1, replica_groups=mesh['wide'=16,'narrow'=8] {'wide','narrow'}, dimensions={0} | all-to-all | bytes 4194304 | tf_op jit(solution)/shard_map/all_to_all | solution.py:294
  127.4 0.0 copy-done.2
  127.4 0.0 copy-start.11
  127.4 0.0 copy-start.1
  127.4 0.0 copy-start.3
  127.4 6.0 %last.1 = bf16[128,16,128]{2,1,0:T(8,128)(2,1)} custom-call(bf16[128,32,256]{2,1,0:T(8,128)(2,1)S(1)} %all_to_all.21.y_ref, bf16[4,256,768]{2,1,0:T(8,128)(2,1)S(1)} %copy-done.2, f32[8,128]{1,0:T(8,128)S(1)} %get-tuple-element.11.peak_ref), custom_call_target="tpu_custom_call" | custom-call | flops 1073741824 | bytes 4198400 | tf_op jit(solution)/shard_map/last/pallas_call | solution.py:280
  133.4 4.3 %all-to-all-start.3 = ((bf16[128,16,128]{2,1,0:T(8,128)(2,1)}), bf16[128,16,128]{2,1,0:T(8,128)(2,1)S(1)}, u32[]{:S(2)}, u32[]{:S(2)}) async-start(bf16[128,16,128]{2,1,0:T(8,128)(2,1)} %last.1), calls=%async_computation.3 | async-start | bytes 1048576 | tf_op jit(solution)/shard_map/all_to_all | solution.py:294
  137.7 0.0 copy-done.11
  137.7 0.1 copy.19.skip_ref
  137.8 13.9 %all-to-all-done.3.y_ref = bf16[128,16,128]{2,1,0:T(8,128)(2,1)S(1)} async-done(((bf16[128,16,128]{2,1,0:T(8,128)(2,1)}), bf16[128,16,128]{2,1,0:T(8,128)(2,1)S(1)}, u32[]{:S(2)}, u32[]{:S(2)}) %all-to-all-start.3) | async-done | bytes 524320 | tf_op jit(solution)/shard_map/all_to_all | solution.py:294
  151.7 0.0 copy-done.1
  151.7 0.0 copy-done.3
  151.7 2.0 %finish.1 = bf16[4,65536]{1,0:T(4,128)(2,1)} custom-call(bf16[128,16,128]{2,1,0:T(8,128)(2,1)S(1)} %all-to-all-done.3.y_ref, bf16[4,65536]{1,0:T(4,128)(2,1)S(1)} %copy-done.1, bf16[4,65536]{1,0:T(4,128)(2,1)S(1)} %copy-done.3, f32[4,1]{1,0:T(4,128)S(1)} %copy.19.skip_ref, f32[8,128]{1,0:T(8,128)S(1)} %get-tuple-element.11.peak_ref), custom_call_target="tpu_custom_call" | custom-call | bytes 2101264 | tf_op jit(solution)/shard_map/finish/pallas_call | solution.py:280
  (6 shorter events, 0.0 us)
Async XLA Ops:
  0.0 1.0 copy-start
  1.0 27.3 %copy-start.10 = (bf16[1024,512]{1,0:T(8,128)(2,1)S(1)}, bf16[1024,512]{1,0:T(8,128)(2,1)}, u32[]{:S(2)}) copy-start(bf16[1024,512]{1,0:T(8,128)(2,1)} %constant.77.clone.table_ref) | copy-start | bytes 3145732
  32.5 5.6 %copy-start.4 = (f32[2,256,256]{2,1,0:T(8,128)S(1)}, f32[2,256,256]{2,1,0:T(8,128)}, u32[]{:S(2)}) copy-start(f32[2,256,256]{2,1,0:T(8,128)} %constant.74.clone.cross_base_ref) | copy-start | bytes 1572868
  32.5 5.6 %copy-start.5 = (f32[2,128,128]{2,1,0:T(8,128)S(1)}, f32[2,128,128]{2,1,0:T(8,128)}, u32[]{:S(2)}) copy-start(f32[2,128,128]{2,1,0:T(8,128)} %constant.73.clone.base_ref) | copy-start | bytes 393220
  32.5 35.1 %all-to-all-start.1 = ((bf16[128,32,256]{2,1,0:T(8,128)(2,1)}), bf16[128,32,256]{2,1,0:T(8,128)(2,1)}, u32[]{:S(2)}, u32[]{:S(2)}) async-start(bf16[128,32,256]{2,1,0:T(8,128)(2,1)} %get-tuple-element.10), calls=%async_computation.1 | async-start | bytes 4194304 | tf_op jit(solution)/shard_map/all_to_all | solution.py:294
  38.5 0.9 copy-start.6
  67.5 1.1 copy-start.7
  68.7 1.4 copy-start.8
  70.1 1.4 copy-start.9
  92.1 35.2 %copy-start.2 = (bf16[4,256,768]{2,1,0:T(8,128)(2,1)S(1)}, bf16[4,256,768]{2,1,0:T(8,128)(2,1)}, u32[]{:S(2)}) copy-start(bf16[4,256,768]{2,1,0:T(8,128)(2,1)} %constant.78.clone.table_ref) | copy-start | bytes 4718596
  127.4 10.3 %copy-start.11 = (f32[4]{0:T(128)S(1)}, f32[4]{0:T(128)}, u32[]{:S(2)}) copy-start(f32[4]{0:T(128)} %param.12) | copy-start | bytes 52
  127.4 24.3 %copy-start.1 = (bf16[4,65536]{1,0:T(4,128)(2,1)S(1)}, bf16[4,65536]{1,0:T(4,128)(2,1)}, u32[]{:S(2)}) copy-start(bf16[4,65536]{1,0:T(4,128)(2,1)} %sig_ref.3) | copy-start | bytes 1572868
  127.4 24.3 %copy-start.3 = (bf16[4,65536]{1,0:T(4,128)(2,1)S(1)}, bf16[4,65536]{1,0:T(4,128)(2,1)}, u32[]{:S(2)}) copy-start(bf16[4,65536]{1,0:T(4,128)(2,1)} %gate_ref.1) | copy-start | bytes 1572868
  133.4 18.3 %all-to-all-start.3 = ((bf16[128,16,128]{2,1,0:T(8,128)(2,1)}), bf16[128,16,128]{2,1,0:T(8,128)(2,1)S(1)}, u32[]{:S(2)}, u32[]{:S(2)}) async-start(bf16[128,16,128]{2,1,0:T(8,128)(2,1)} %last.1), calls=%async_computation.3 | async-start | bytes 1048576 | tf_op jit(solution)/shard_map/all_to_all | solution.py:294

commit v3 on v2

v3 whole, which is shorter than its diff:
```python
import jax
import jax.numpy as jnp
import ml_dtypes
import numpy as np
from jax import lax
from jax.experimental import pallas as pl
from jax.experimental.pallas import tpu as pltpu
from jax.sharding import PartitionSpec as P

F = 256
ND = 128
STEPS = 4
ROWS = ND // STEPS
AXES = ("wide", "narrow")
bf16 = jnp.bfloat16
f32 = jnp.float32

OFFSET = 120.0 * np.log(2.0)
SPAN = 240.0
FIELD_CODE = (2.0**-8, 15.1)
FILTERED_CODE = (2.0**-11, 22.2)
CONV_CODE = (2.0**-7, 21.7)
FILTER_TOP = 6.02


def split_np(x):
    hi = x.astype(ml_dtypes.bfloat16)
    lo = (x - hi.astype(np.float64)).astype(ml_dtypes.bfloat16)
    return hi, lo


def outer_waves():
    k1 = np.arange(F).reshape(ND, 2)
    ang = 2 * np.pi * (k1[:, :, None] * np.arange(ND) % F) / F
    wave = np.stack([np.cos(ang), -np.sin(ang)], axis=2)
    for p in (0, ND // 2):
        wave[p, 0, 1] = np.cos(np.pi * (1 - p // (ND // 2)) * np.arange(ND))
    return wave


def outer_forward_table():
    t = np.zeros((ND, 2, 2, 2, 2, ND))
    for c in range(2):
        t[:, :, c, :, c, :] = outer_waves()
    return np.concatenate(split_np(t.reshape(ND * 8, 2 * ND)), axis=1)


def outer_inverse_table():
    t = np.zeros((2, ND, ND, 2, 2, 2))
    for c in range(2):
        t[c, :, :, :, c, :] = outer_waves().transpose(3, 0, 1, 2)
    hi, lo = (x.reshape(2 * ND, STEPS, -1) for x in split_np(t.reshape(2 * ND, ND * 8)))
    return np.ascontiguousarray(np.concatenate([hi, hi, lo], axis=2).transpose(1, 0, 2))


def inner_tables():
    low = np.arange(ND)
    out = []
    for odd in range(2):
        ang = 2 * np.pi * (low[:, None] * (2 * low[None] + odd) % F) / F
        c, s = np.cos(ang), np.sin(ang)
        fwd = split_np(np.block([[c, -s], [s, c]]))
        inv = split_np(np.block([[c.T, s.T], [-s.T, c.T]]) / F)
        out.append([np.concatenate([hi, hi, lo], axis=0) for hi, lo in (fwd, inv)])
    return np.stack([out[0][0], out[1][0]]), np.stack([out[0][1], out[1][1]])


def order_tables():
    eye = np.eye(F)
    even_odd = np.concatenate([np.arange(0, F, 2), np.arange(1, F, 2)])
    plain = np.stack([eye, eye[:, even_odd]])
    back = np.stack([eye[::-1], eye[:, 255 - even_odd]])
    return plain.astype(ml_dtypes.bfloat16), back.astype(ml_dtypes.bfloat16)


def base_tables():
    i = np.arange(F)
    half = np.arange(ND)
    a0 = 2 * np.pi * (half[:, None] * half[None] % ND) / ND
    a1 = 2 * np.pi * (i[:, None] * i[None]) / (F * F)
    return (
        np.stack([np.cos(a0), np.sin(a0)]).astype(np.float32),
        np.stack([np.cos(a1), np.sin(a1)]).astype(np.float32),
    )


def peak_of(peak_ref):
    return jnp.maximum(jnp.max(peak_ref[...], keepdims=True), 1e-30)


def encode(x, peak, code):
    knee, octaves = code
    beta = SPAN / octaves
    z = jnp.abs(x) * (1.0 / (peak * knee))
    y = jnp.exp(jnp.minimum(beta * jnp.log(1.0 + z) - OFFSET, OFFSET))
    return jnp.where(x < 0, -y, y)


def decode(y, peak, code):
    knee, octaves = code
    beta = SPAN / octaves
    z = jnp.exp(jnp.log(jnp.abs(y)) * (1.0 / beta) + OFFSET / beta) - 1.0
    z = z * (peak * knee)
    return jnp.where(y < 0, -z, z)


def encode_filter(x):
    y = jnp.exp(jnp.abs(x) * (SPAN * np.log(2.0) / FILTER_TOP) - OFFSET)
    return jnp.where(x < 0, -y, y)


def decode_filter(y):
    z = (jnp.log(jnp.abs(y)) + OFFSET) * (FILTER_TOP / (SPAN * np.log(2.0)))
    return jnp.where(y < 0, -z, z)


def split(x):
    hi = x.astype(bf16)
    return hi, (x - hi.astype(f32)).astype(bf16)


def dot(a, b):
    return jnp.dot(a, b, preferred_element_type=f32)


def twice(hi, lo, axis):
    return jnp.concatenate([hi, lo, hi], axis=axis)


def pack_kernel(sig_ref, out_ref):
    top = jnp.zeros((4, 128), f32)
    for q in range(ND):
        x = sig_ref[:, pl.ds(q * 512, 512)]
        out_ref[q, :, pl.ds(0, 512)] = x
        x = jnp.abs(x.astype(f32))
        for i in range(4):
            top = jnp.maximum(top, x[:, i * 128 : (i + 1) * 128])
    top = top.astype(bf16)
    for q in range(ND):
        out_ref[q, :, pl.ds(512, 128)] = top


def outer_kernel(x_ref, table_ref, out_ref, peak_ref, buf, xs):
    @pl.when(pl.program_id(0) == 0)
    def _():
        top = jnp.zeros((4, 128), f32)
        for n in range(ND):
            x = x_ref[n].astype(f32)
            top = jnp.maximum(top, x[:, 512:640])
            for i in range(4):
                buf[i, pl.ds(n * 8, 4), :] = x[:, i * 128 : (i + 1) * 128]
        peak_ref[...] = jnp.broadcast_to(jnp.maximum(jnp.max(top, keepdims=True), 1e-30), (8, 128))
        for c in range(4):
            parts = [buf[i, pl.ds(c, ND, stride=8), :] for i in range(4)]
            xs[pl.ds(c * ND, ND), :] = jnp.concatenate(parts, axis=1).astype(bf16)

    x = xs[pl.ds(pl.program_id(0) // (STEPS // 2) * 256, 256), :]
    res = encode(dot(table_ref[...], jnp.concatenate([x, x], axis=0)), peak_ref[0:1, 0:1], FIELD_CODE)
    parts = [res[:, h * F : (h + 1) * F].reshape(ROWS, 8, F) for h in range(2)]
    out_ref[...] = jnp.concatenate(parts, axis=1).astype(bf16)


def table_kernel(base_ref, cross_base_ref, lane_ref, cross_lane_ref, sub_ref, mf_ref, mi_ref, cross_ref):
    c0, s0 = base_ref[0], base_ref[1]
    c1, s1 = cross_base_ref[0], cross_base_ref[1]
    for r in range(3):
        for out_ref, vec_ref, sign in ((mf_ref, lane_ref, 1.0), (mi_ref, sub_ref, -1.0)):
            cb, sb = vec_ref[r, 0], vec_ref[r, 1]
            c, s = c0 * cb - s0 * sb, (s0 * cb + c0 * sb) * sign
            if sign < 0:
                c, s = c * (1.0 / F), s * (1.0 / F)
            (ch, cl), (sh, sl) = split(c), split(s)
            for part, (cc, ss) in enumerate(((ch, sh), (ch, sh), (cl, sl))):
                at = part * 256
                out_ref[r, 0:128, at : at + 128] = cc
                out_ref[r, 0:128, at + 128 : at + 256] = ss
                out_ref[r, 128:256, at : at + 128] = -ss
                out_ref[r, 128:256, at + 128 : at + 256] = cc
        cb, sb = cross_lane_ref[r, 0], cross_lane_ref[r, 1]
        cross_ref[r, 0] = c1 * cb - s1 * sb
        cross_ref[r, 1] = s1 * cb + c1 * sb


def give_kernel(half_ref, filt_ref, order_ref, sign_ref, out0_ref, out1_ref):
    del half_ref
    for r, out_ref in enumerate((out0_ref, out1_ref)):
        left, right = order_ref[r, 0], order_ref[r, 1]
        for ri in range(2):
            for c in range(2):
                hi, lo = split(filt_ref[ri, c, r])
                hi, lo = split(dot(hi, right) + dot(lo, right))
                x = dot(left, hi) + dot(left, lo)
                if ri:
                    x = x * sign_ref[r]
                out_ref[ri * 2 + c] = encode_filter(x).astype(bf16)


def combine_kernel(half_ref, filt_ref, order_ref, got0_ref, got1_ref, generic_ref, out_ref, other_ref):
    del half_ref
    for r, got_ref in enumerate((got0_ref, got1_ref)):
        for ri in range(2):
            for c in range(2):
                got = decode_filter(got_ref[ri * 2 + c].astype(f32))
                if r == 0:
                    other_ref[ri, c] = got
                    got = got * generic_ref[0]
                hi, lo = split(filt_ref[ri, c, r])
                out_ref[r, ri, c] = dot(hi, order_ref[1]) + dot(lo, order_ref[1]) + got


def transform(re, im, table, mf_ref, mi_ref, cross_ref, turn_ref, fwd_ref, inv_ref, filt):
    tc, ts = turn_ref[table, 0], turn_ref[table, 1]
    hi, lo = split(jnp.concatenate([re, im], axis=0))
    z = dot(mf_ref[table], twice(hi, lo, 0))
    sums, diffs = [], []
    for c in range(2):
        at = c * 512
        dr, di = z[:128, at : at + 256], z[128:, at : at + 256]
        er, ei = z[:128, at + 256 : at + 512], z[128:, at + 256 : at + 512]
        pr, pi = er * tc + ei * ts, ei * tc - er * ts
        for zr, zi, e in ((dr + pr, di + pi, 0), (dr - pr, di - pi, 128)):
            cosine, sine = cross_ref[table, 0, e : e + 128], cross_ref[table, 1, e : e + 128]
            zr, zi = zr * cosine + zi * sine, zi * cosine - zr * sine
            sums.append(jnp.concatenate([zr[:, :128] + zr[:, 128:], zi[:, :128] + zi[:, 128:]], axis=1))
            diffs.append(jnp.concatenate([zr[:, :128] - zr[:, 128:], zi[:, :128] - zi[:, 128:]], axis=1))
    back = []
    for odd, rows in enumerate((sums, diffs)):
        hi, lo = split(jnp.concatenate(rows, axis=0))
        z = dot(twice(hi, lo, 1), fwd_ref[odd])
        rows = []
        for c in range(2):
            zr, zi = z[c * F : (c + 1) * F, :128], z[c * F : (c + 1) * F, 128:]
            fr, fi = filt(0, c, odd), filt(1, c, odd)
            rows.append(jnp.concatenate([zr * fr - zi * fi, zi * fr + zr * fi], axis=1))
        hi, lo = split(jnp.concatenate(rows, axis=0))
        back.append(dot(twice(hi, lo, 1), inv_ref[odd]))
    even, odd = back
    tops, bottoms = [], []
    for c in range(2):
        both = []
        for e in (0, 128):
            at = c * F + e
            er, ei = even[at : at + 128, :128], even[at : at + 128, 128:]
            dr, di = odd[at : at + 128, :128], odd[at : at + 128, 128:]
            zr = jnp.concatenate([er + dr, er - dr], axis=1)
            zi = jnp.concatenate([ei + di, ei - di], axis=1)
            cosine = cross_ref[table, 0, e : e + 128] * (1.0 / F)
            sine = cross_ref[table, 1, e : e + 128] * (1.0 / F)
            both.append((zr * cosine - zi * sine, zi * cosine + zr * sine))
        (ar, ai), (br, bi) = both
        ur, ui = ar - br, ai - bi
        tops += [ar + br, ur * tc - ui * ts]
        bottoms += [ai + bi, ui * tc + ur * ts]
    hi, lo = split(jnp.concatenate([jnp.concatenate(tops, axis=1), jnp.concatenate(bottoms, axis=1)], axis=0))
    return dot(mi_ref[table], twice(hi, lo, 0))


def middle_kernel(
    y_ref, peak_ref, mf_ref, mi_ref, cross_ref, turn_ref, fwd_ref, inv_ref, filt_ref, other_ref, generic_ref, out_ref, buf, obuf
):
    peak = peak_ref[0:1, 0:1]
    tables = (mf_ref, mi_ref, cross_ref, turn_ref, fwd_ref, inv_ref)
    for m in range(STEPS):
        y = decode(y_ref[pl.ds(m * ROWS, ROWS)].astype(f32), peak, FIELD_CODE).reshape(ROWS * 16, F)
        for g in range(2):
            buf[g, pl.ds(m * ROWS * 16, ROWS * 16), :] = y[:, g * 128 : (g + 1) * 128]

    def field(r, ri):
        return jnp.concatenate(
            [
                buf[g, pl.ds(h * 8 + r * 4 + c * 2 + ri, ND, stride=16), :]
                for c in range(2)
                for h in range(2)
                for g in range(2)
            ],
            axis=1,
        )

    def put(z, r, ri, part):
        for c in range(2):
            for h in range(2):
                for g in range(2):
                    at = c * 512 + h * 256 + g * 128
                    obuf[g, pl.ds(h * 8 + r * 4 + c * 2 + ri, ND, stride=16), :] = z[
                        part * 128 : (part + 1) * 128, at : at + 128
                    ]

    def filt_of(r):
        return lambda ri, c, odd: filt_ref[r, ri, c, :, odd * 128 : (odd + 1) * 128]

    for r in range(2):
        im = field(r, 1)
        if r == 0:
            im = im * generic_ref[0]
        z = transform(field(r, 0), im, r, *tables, filt_of(r))
        put(z, r, 0, 0)
        put(z, r, 1, 1)

    @pl.when(generic_ref[0] < 0.5)
    def _():
        re = field(0, 1)
        z = transform(
            re, jnp.zeros_like(re), 2, *tables, lambda ri, c, odd: other_ref[ri, c, :, odd * 128 : (odd + 1) * 128]
        )
        put(z, 0, 1, 0)

    for m in range(STEPS):
        y = jnp.concatenate([obuf[g, pl.ds(m * ROWS * 16, ROWS * 16), :] for g in range(2)], axis=1)
        out_ref[pl.ds(m * ROWS, ROWS)] = encode(y, peak, FILTERED_CODE).reshape(ROWS, 16, F).astype(bf16)


def last_kernel(y_ref, table_ref, peak_ref, out_ref, acc, buf):
    peak = peak_ref[0:1, 0:1]
    step = pl.program_id(0)

    y = decode(y_ref[...].astype(f32), peak, FILTERED_CODE)
    t = table_ref[0]
    pair = step // (STEPS // 2)
    first = step % (STEPS // 2) == 0
    for h in range(2):
        hi, lo = split(y[:, h * 8 : h * 8 + 8, :].reshape(ROWS * 8, F))
        res = dot(t, twice(hi, lo, 0))
        acc[pair, h] = jnp.where(first, res, acc[pair, h] + res)

    @pl.when(step == STEPS - 1)
    def _():
        for pair in range(2):
            for h in range(2):
                for c in range(2):
                    for g in range(2):
                        buf[pl.ds(h * 8 + g * 4 + pair * 2 + c, ND, stride=16), :] = acc[
                            pair, h, c * ND : (c + 1) * ND, g * 128 : (g + 1) * 128
                        ]
        out_ref[...] = encode(buf[...], peak, CONV_CODE).reshape(ND, 16, 128).astype(bf16)


def finish_kernel(y_ref, sig_ref, gate_ref, skip_ref, peak_ref, out_ref, buf):
    peak = peak_ref[0:1, 0:1]
    buf[...] = decode(y_ref[...].astype(f32).reshape(ND * 16, 128), peak, CONV_CODE)
    skip = skip_ref[...]
    for q in range(ND):
        at = pl.ds(q * 512, 512)
        conv = jnp.concatenate([buf[pl.ds(q * 16 + i * 4, 4), :] for i in range(4)], axis=1)
        total = conv + skip * sig_ref[:, at].astype(f32)
        out_ref[:, at] = (gate_ref[:, at].astype(f32) * total).astype(bf16)


VMEM = pl.BlockSpec(memory_space=pltpu.VMEM)
SMEM = pl.BlockSpec(memory_space=pltpu.SMEM)


def call(kernel, ins, outs, scratch, name, flops=0, limit=16, grid=(), in_specs=None, out_specs=None, scalars=0):
    size = sum(int(np.prod(x.shape)) * x.dtype.itemsize for x in (*ins, *outs))
    return pl.pallas_call(
        kernel,
        grid_spec=pltpu.PrefetchScalarGridSpec(
            num_scalar_prefetch=scalars,
            grid=grid,
            in_specs=in_specs or [VMEM] * len(ins),
            out_specs=out_specs or [VMEM] * len(outs),
            scratch_shapes=[pltpu.VMEM(s, d) for s, d in scratch],
        ),
        out_shape=outs,
        compiler_params=pltpu.CompilerParams(vmem_limit_bytes=limit * 2**20),
        cost_estimate=pl.CostEstimate(flops=flops, bytes_accessed=size, transcendentals=0),
        name=name,
    )(*ins)


def exchange(x):
    return lax.all_to_all(x, AXES, split_axis=0, concat_axis=0, tiled=True)


def shape(*dims, dtype=bf16):
    return jax.ShapeDtypeStruct(dims, dtype)


def per_device(signal, gate, skip, spectrum):
    place = lax.axis_index("wide") * lax.axis_size("narrow") + lax.axis_index("narrow")
    (packed,) = call(pack_kernel, (signal,), [shape(ND, 4, 640)], [], "pack")
    spread = exchange(packed)

    upper = (place >= ND // 2).astype(jnp.int32)
    special = place % (ND // 2) == 0
    generic = jnp.where(special, 0.0, 1.0).astype(f32)[None]
    plain, back = (jnp.asarray(t) for t in order_tables())
    order = jnp.stack([jnp.where(place == 0, plain, back), back])
    sign = jnp.stack([jnp.where(place == 0, 1.0, -1.0), -1.0]).astype(f32)
    block = (2, 2, 2, F, F)
    given = call(
        give_kernel,
        ((1 - upper)[None], spectrum, order, sign),
        [shape(4, F, F)] * 2,
        [],
        "give",
        flops=2**30,
        grid=(1,),
        in_specs=[pl.BlockSpec(block, lambda i, half: (0, half[0], 0, 0, 0)), VMEM, SMEM],
        out_specs=[pl.BlockSpec((4, F, F), lambda i, half: (0, 0, 0))] * 2,
        scalars=1,
    )
    mirror = [(p, (ND // 2 - p) if p % (ND // 2) == 0 else ND - p) for p in range(ND)]
    got = [
        lax.ppermute(given[0], AXES, mirror),
        lax.ppermute(given[1], AXES, [(p, ND - 1 - p) for p in range(ND)]),
    ]

    k1 = jnp.stack([place * 2, place * 2 + 1, ND - place * 2])[:, None] % F
    half = jnp.arange(ND, dtype=jnp.int32)

    def wave(index, period):
        angle = (2 * np.pi / period) * (index % period).astype(f32)
        return jnp.stack([jnp.cos(angle), jnp.sin(angle)], axis=1)

    mid = wave(k1 * half, F * ND)
    fine = wave(k1 * jnp.arange(F, dtype=jnp.int32), F**3)
    turn = wave(k1 + F * half, F * F)
    base, cross_base = (jnp.asarray(t) for t in base_tables())
    mf, mi, cross = call(
        table_kernel,
        (base, cross_base, mid[:, :, None, :], fine[:, :, None, :], mid[:, :, :, None]),
        [shape(3, 256, 768), shape(3, 256, 768), shape(3, 2, F, F, dtype=f32)],
        [],
        "tables",
    )
    inner_fwd, inner_inv = (jnp.asarray(t) for t in inner_tables())

    field, peak = call(
        outer_kernel,
        (spread, jnp.asarray(outer_forward_table())),
        [shape(ND, 16, F), shape(8, 128, dtype=f32)],
        [((4, ND * 8, 128), f32), ((ND * 4, 512), bf16)],
        "outer",
        flops=2**29,
        grid=(STEPS,),
        in_specs=[VMEM, pl.BlockSpec((ROWS * 8, 512), lambda i: (i, 0))],
        out_specs=[pl.BlockSpec((ROWS, 16, F), lambda i: (i, 0, 0)), pl.BlockSpec((8, 128), lambda i: (0, 0))],
    )
    field = exchange(field)
    filt, other = call(
        combine_kernel,
        (upper[None], spectrum, plain, *got, generic),
        [shape(2, 2, 2, F, F, dtype=f32), shape(2, 2, F, F, dtype=f32)],
        [],
        "combine",
        flops=2**29,
        grid=(1,),
        in_specs=[pl.BlockSpec(block, lambda i, half: (0, half[0], 0, 0, 0)), VMEM, VMEM, VMEM, SMEM],
        out_specs=[
            pl.BlockSpec((2, 2, 2, F, F), lambda i, half: (0, 0, 0, 0, 0)),
            pl.BlockSpec((2, 2, F, F), lambda i, half: (0, 0, 0, 0)),
        ],
        scalars=1,
    )
    (filtered,) = call(
        middle_kernel,
        (field, peak, mf, mi, cross, turn[:, :, :, None], inner_fwd, inner_inv, filt, other, generic),
        [shape(ND, 16, F)],
        [((2, ND * 16, 128), f32)] * 2,
        "middle",
        flops=4 * 2**30,
        limit=24,
        in_specs=[VMEM] * 10 + [SMEM],
    )
    filtered = exchange(filtered)
    (conv,) = call(
        last_kernel,
        (filtered, jnp.asarray(outer_inverse_table()), peak),
        [shape(ND, 16, 128)],
        [((2, 2, 2 * ND, F), f32), ((ND * 16, 128), f32)],
        "last",
        flops=2**29,
        grid=(STEPS,),
        in_specs=[
            pl.BlockSpec((ROWS, 16, F), lambda i: (i, 0, 0)),
            pl.BlockSpec((1, 2 * ND, ROWS * 24), lambda i: (i, 0, 0)),
            VMEM,
        ],
        out_specs=[VMEM],
    )
    conv = exchange(conv)
    (mixed,) = call(
        finish_kernel,
        (conv, signal, gate, skip[:, None], peak),
        [shape(4, 65536)],
        [((ND * 16, 128), f32)],
        "finish",
    )
    return mixed


def solution(mesh):
    split_spec = P(None, AXES)
    return jax.shard_map(
        per_device,
        mesh=mesh,
        in_specs=(split_spec, split_spec, P(), P(None, None, AXES, None, None)),
        out_specs=split_spec,
        check_vma=False,
    )
```

time: 154 us -> 137 us (0.89)
  blocking collectives: 61.9 us -> 28.1 us
  starting transfers between devices: 9.1 us -> 27.4 us
  local copies, waits for them, and re-layouts: 6.29 us -> 22.6 us
  waiting for transfers between devices: 42 us -> 32.6 us
  Pallas kernels: 33.9 us -> 24.9 us
    all_to_all x2 -> x1, blocking collectives: 61.9 us -> 28.1 us  [exchange(): return lax.all_to_all(x, AXES, split_axis=0, concat_axis=0, tiled=True)]
    all_to_all x2 -> x3, waiting for transfers between devices: 42 us -> 23.8 us  [exchange(): return lax.all_to_all(x, AXES, split_axis=0, concat_axis=0, tiled=True)]
    unnamed x24 -> x52, local copies, waits for them, and re-layouts: 5.9 us -> 21.3 us
    all_to_all x2 -> x3, starting transfers between devices: 9.1 us -> 19.4 us  [exchange(): return lax.all_to_all(x, AXES, split_axis=0, concat_axis=0, tiled=True)]
    pallas_call x6 -> x8, Pallas kernels: 33.9 us -> 24.9 us  [call(): pl.pallas_call(kernel, grid_spec=pltpu.PrefetchScalarGridSpec(num_scalar_...]
    ppermute x0 -> x2, waiting for transfers between devices: none -> 8.82 us  [the longest x1 8.82 us: per_device(): lax.ppermute(given[1], AXES, [(p, ND - 1 - p) for p in range(ND)])]
    ppermute x0 -> x2, starting transfers between devices: none -> 7.98 us  [the longest x1 4.18 us: per_device(): lax.ppermute(given[0], AXES, mirror)]
  transfers between devices with their start and end apart: 2 -> 5, of which waited for: 2 -> 4; matrix products, arithmetic and copies ran while one was open for 0% -> 1% of each run, Pallas kernels for 0% -> 6%
where the time goes in v3:
time: 137 us; the launch traced here: 136 us
  waiting for transfers between devices  32.6 us (24%)
  blocking collectives  28.1 us (21%)
  starting transfers between devices  27.4 us (20%)
  Pallas kernels  24.9 us (18%)
  local copies, waits for them, and re-layouts  22.6 us (16%)
    all_to_all x1, blocking collectives, exchange(): return lax.all_to_all(x, AXES, split_axis=0, concat_axis=0, tiled=True)  28.1 us
    pallas_call x8, Pallas kernels, call(): pl.pallas_call(kernel, grid_spec=pltpu.PrefetchScalarGridSpec(num_scalar_...  24.9 us
    all_to_all x3, waiting for transfers between devices, exchange(): return lax.all_to_all(x, AXES, split_axis=0, concat_axis=0, tiled=True)  23.8 us
    unnamed x52, local copies, waits for them, and re-layouts  21.3 us
    all_to_all x3, starting transfers between devices, exchange(): return lax.all_to_all(x, AXES, split_axis=0, concat_axis=0, tiled=True)  19.4 us
    ppermute x1, waiting for transfers between devices, per_device(): lax.ppermute(given[1], AXES, [(p, ND - 1 - p) for p in range(ND)])  8.82 us
    ppermute x1, starting transfers between devices, per_device(): lax.ppermute(given[0], AXES, mirror)  4.18 us
    ppermute x1, starting transfers between devices, per_device(): lax.ppermute(given[1], AXES, [(p, ND - 1 - p) for p in range(ND)])  3.8 us
  transfers between devices with their start and end apart: 5, of which 4 were waited for; matrix products, arithmetic and copies ran while one was open for 1% of the time, Pallas kernels for 6%

profile of v3, /device:TPU:1, one launch (start us, length us, event | category | flops | bytes accessed | tf_op | source)
XLA Modules:
  0.0 136.5 jit_solution(16930922151595111360)
XLA Ops:
  0.0 0.0 copy-start.2
  0.0 1.0 copy-done.2
  1.0 0.0 copy-start.5
  1.0 0.0 copy-start.23
  1.0 1.4 %pack.1 = bf16[128,4,640]{2,1,0:T(4,128)(2,1)} custom-call(bf16[4,65536]{1,0:T(4,128)(2,1)S(1)} %copy-done.2), custom_call_target="tpu_custom_call" | custom-call | bytes 1179648 | tf_op jit(solution)/shard_map/pack/pallas_call | solution.py:354
  2.5 11.5 %all-to-all-start = ((bf16[128,4,640]{2,1,0:T(4,128)(2,1)}), bf16[128,4,640]{2,1,0:T(4,128)(2,1)S(1)}, u32[]{:S(2)}, u32[]{:S(2)}) async-start(bf16[128,4,640]{2,1,0:T(4,128)(2,1)} %pack.1), calls=%async_computation | async-start | bytes 1310720 | tf_op jit(solution)/shard_map/all_to_all | solution.py:371
  14.0 0.1 pad_maximum_fusion.3.sign_ref
  14.1 0.0 copy-done.5
  14.1 0.0 copy-done.24
  14.1 0.0 copy-done.23
  14.1 0.1 pad_maximum_fusion.order_ref
  14.2 0.0 copy-start
  14.2 2.2 %copy-done = f32[2,4,2,256,256]{4,3,2,1,0:T(8,128)S(1)} copy-done((f32[2,4,2,256,256]{4,3,2,1,0:T(8,128)S(1)}, f32[2,4,2,256,256]{4,3,2,1,0:T(8,128)}, u32[]{:S(2)}) %copy-start) | copy-done | bytes 4194328
  16.4 3.0 %give.1 = (bf16[4,256,256]{2,1,0:T(8,128)(2,1)}, bf16[4,256,256]{2,1,0:T(8,128)(2,1)}) custom-call(s32[1]{0:T(128)} %bitcast.7.half_ref, f32[2,4,2,256,256]{4,3,2,1,0:T(8,128)S(1)} %copy-done, bf16[2,2,256,256]{3,2,1,0:T(8,128)(2,1)S(1)} %pad_maximum_fusion.order_ref, f32[2]{0:T(128)S(1)} %pad_maximum_fusion.3.sign_ref), custom_call_target="tpu_custom_call" | custom-call | flops 1073741824 | bytes 5767180 | tf_op jit(solution)/shard_map/give/pallas_call | solution.py:354
  19.4 4.2 %collective-permute-start = (bf16[4,256,256]{2,1,0:T(8,128)(2,1)}, bf16[4,256,256]{2,1,0:T(8,128)(2,1)S(1)}, u32[]{:S(2)}, u32[]{:S(2)}) collective-permute-start(bf16[4,256,256]{2,1,0:T(8,128)(2,1)} %get-tuple-element.19), channel_id=1, source_target_pairs={{0,64},{1,127},{2,126},{3,125},{4,124},{5,123},{6,122},{7,121},{8,... | collective-permute-start | bytes 1572872 | tf_op jit(solution)/shard_map/ppermute | solution.py:404
  23.6 3.8 %collective-permute-start.1 = (bf16[4,256,256]{2,1,0:T(8,128)(2,1)}, bf16[4,256,256]{2,1,0:T(8,128)(2,1)S(1)}, u32[]{:S(2)}, u32[]{:S(2)}) collective-permute-start(bf16[4,256,256]{2,1,0:T(8,128)(2,1)} %get-tuple-element.20), channel_id=1, source_target_pairs={{0,127},{1,126},{2,125},{3,124},{4,123},{5,122},{6,121},{7,120},{8... | collective-permute-start | bytes 1572872 | tf_op jit(solution)/shard_map/ppermute | solution.py:405
  27.4 3.5 %all-to-all-done.x_ref = bf16[128,4,640]{2,1,0:T(4,128)(2,1)S(1)} async-done(((bf16[128,4,640]{2,1,0:T(4,128)(2,1)}), bf16[128,4,640]{2,1,0:T(4,128)(2,1)S(1)}, u32[]{:S(2)}, u32[]{:S(2)}) %all-to-all-start) | async-done | bytes 655392 | tf_op jit(solution)/shard_map/all_to_all | solution.py:371
  30.9 0.0 copy-start.20
  30.9 1.2 copy-done.20
  32.1 3.3 %outer.1 = (bf16[128,16,256]{2,1,0:T(8,128)(2,1)}, f32[8,128]{1,0:T(8,128)S(1)}) custom-call(bf16[128,4,640]{2,1,0:T(4,128)(2,1)S(1)} %all-to-all-done.x_ref, bf16[1024,512]{1,0:T(8,128)(2,1)S(1)} %copy-done.20), custom_call_target="tpu_custom_call" | custom-call | flops 536870912 | bytes 2756608 | tf_op jit(solution)/shard_map/outer/pallas_call | solution.py:354
  35.4 0.0 copy-start.7
  35.4 0.0 copy-start.9
  35.4 3.9 %all-to-all-start.1 = ((bf16[128,16,256]{2,1,0:T(8,128)(2,1)}), bf16[128,16,256]{2,1,0:T(8,128)(2,1)S(1)}, u32[]{:S(2)}, u32[]{:S(2)}) async-start(bf16[128,16,256]{2,1,0:T(8,128)(2,1)} %get-tuple-element.14), calls=%async_computation.1 | async-start | bytes 2097152 | tf_op jit(solution)/shard_map/all_to_all | solution.py:371
  39.3 0.1 and_select_fusion.3
  39.4 0.2 fusion.10
  39.6 0.2 fusion.15
  39.8 0.2 copy.19.sub_ref
  40.0 1.0 copy.20.turn_ref
  41.0 0.0 copy-done.7
  41.0 0.0 copy-done.9
  41.0 0.7 tables.1
  41.7 0.0 copy-start.12
  41.7 1.1 copy-done.12
  42.8 0.0 copy-start.14
  42.8 1.0 copy-done.14
  43.9 1.0 copy-done.16
  44.9 0.0 collective-permute-done.got0_ref
  44.9 8.8 %collective-permute-done.1.got1_ref = bf16[4,256,256]{2,1,0:T(8,128)(2,1)S(1)} collective-permute-done((bf16[4,256,256]{2,1,0:T(8,128)(2,1)}, bf16[4,256,256]{2,1,0:T(8,128)(2,1)S(1)}, u32[]{:S(2)}, u32[]{:S(2)}) %collective-permute-start.1) | collective-permute-done | bytes 524320 | tf_op jit(solution)/shard_map/ppermute | solution.py:405
  53.7 2.2 %copy-done.1 = f32[2,4,2,256,256]{4,3,2,1,0:T(8,128)S(1)} copy-done((f32[2,4,2,256,256]{4,3,2,1,0:T(8,128)S(1)}, f32[2,4,2,256,256]{4,3,2,1,0:T(8,128)}, u32[]{:S(2)}) %copy-start.1) | copy-done | bytes 4194328
  55.9 1.1 combine.1
  57.0 0.0 copy-start.10
  57.1 1.3 copy-done.10
  58.4 1.1 copy-done.18
  59.5 6.4 %all-to-all-done.1.y_ref = bf16[128,16,256]{2,1,0:T(8,128)(2,1)S(1)} async-done(((bf16[128,16,256]{2,1,0:T(8,128)(2,1)}), bf16[128,16,256]{2,1,0:T(8,128)(2,1)S(1)}, u32[]{:S(2)}, u32[]{:S(2)}) %all-to-all-start.1) | async-done | bytes 1048608 | tf_op jit(solution)/shard_map/all_to_all | solution.py:371
  65.8 0.0 copy-done.8
  65.8 1.6 %copy-done.11 = f32[2,2,2,256,256]{4,3,2,1,0:T(8,128)S(1)} copy-done((f32[2,2,2,256,256]{4,3,2,1,0:T(8,128)S(1)}, f32[2,2,2,256,256]{4,3,2,1,0:T(8,128)}, u32[]{:S(2)}) %copy-start.11) | copy-done | bytes 2097176
  67.4 1.4 %copy-done.13 = f32[3,2,256,256]{3,2,1,0:T(8,128)S(1)} copy-done((f32[3,2,256,256]{3,2,1,0:T(8,128)S(1)}, f32[3,2,256,256]{3,2,1,0:T(8,128)}, u32[]{:S(2)}) %copy-start.13) | copy-done | bytes 1572888
  68.8 1.3 copy-done.15
  70.1 1.3 copy-done.17
  71.4 1.2 copy-done.19
  72.6 1.1 copy-done.21
  73.7 1.1 copy-done.22
  74.9 8.8 %middle.1 = bf16[128,16,256]{2,1,0:T(8,128)(2,1)S(1)} custom-call(bf16[128,16,256]{2,1,0:T(8,128)(2,1)S(1)} %all-to-all-done.1.y_ref, f32[8,128]{1,0:T(8,128)S(1)} %get-tuple-element.15.peak_ref, bf16[3,256,768]{2,1,0:T(8,128)(2,1)S(1)} %copy-done.15, bf16[3,256,768]{2,1,0:T(8,128)(2,1)S(1)} %copy-done.17, f32[3,2,256,256]{3,2,1,0:T(8,128)S(1)} %copy-done.13, ...), custom_call_target="tpu_custom_call" | custom-call | flops 4294967296 | bytes 10755076 | tf_op jit(solution)/shard_map/middle/pallas_call | solution.py:354
  83.7 0.0 copy-start.4
  83.7 28.1 %all_to_all.20.y_ref = bf16[128,16,256]{2,1,0:T(8,128)(2,1)S(1)} all-to-all(bf16[128,16,256]{2,1,0:T(8,128)(2,1)S(1)} %middle.1), channel_id=1, replica_groups=mesh['wide'=16,'narrow'=8] {'wide','narrow'}, dimensions={0} | all-to-all | bytes 2097152 | tf_op jit(solution)/shard_map/all_to_all | solution.py:371
  111.8 0.0 copy-done.4
  111.8 4.6 %last.1 = bf16[128,16,128]{2,1,0:T(8,128)(2,1)} custom-call(bf16[128,16,256]{2,1,0:T(8,128)(2,1)S(1)} %all_to_all.20.y_ref, bf16[4,256,768]{2,1,0:T(8,128)(2,1)S(1)} %copy-done.4, f32[8,128]{1,0:T(8,128)S(1)} %get-tuple-element.15.peak_ref), custom_call_target="tpu_custom_call" | custom-call | flops 536870912 | bytes 3149824 | tf_op jit(solution)/shard_map/last/pallas_call | solution.py:354
  116.4 4.0 %all-to-all-start.3 = ((bf16[128,16,128]{2,1,0:T(8,128)(2,1)}), bf16[128,16,128]{2,1,0:T(8,128)(2,1)S(1)}, u32[]{:S(2)}, u32[]{:S(2)}) async-start(bf16[128,16,128]{2,1,0:T(8,128)(2,1)} %last.1), calls=%async_computation.3 | async-start | bytes 1048576 | tf_op jit(solution)/shard_map/all_to_all | solution.py:371
  120.4 0.0 copy-done.25
  120.4 0.1 copy.21.skip_ref
  120.5 13.9 %all-to-all-done.3.y_ref = bf16[128,16,128]{2,1,0:T(8,128)(2,1)S(1)} async-done(((bf16[128,16,128]{2,1,0:T(8,128)(2,1)}), bf16[128,16,128]{2,1,0:T(8,128)(2,1)S(1)}, u32[]{:S(2)}, u32[]{:S(2)}) %all-to-all-start.3) | async-done | bytes 524320 | tf_op jit(solution)/shard_map/all_to_all | solution.py:371
  134.5 0.0 copy-done.3
  134.5 0.0 copy-done.6
  134.5 2.0 %finish.1 = bf16[4,65536]{1,0:T(4,128)(2,1)} custom-call(bf16[128,16,128]{2,1,0:T(8,128)(2,1)S(1)} %all-to-all-done.3.y_ref, bf16[4,65536]{1,0:T(4,128)(2,1)S(1)} %copy-done.3, bf16[4,65536]{1,0:T(4,128)(2,1)S(1)} %copy-done.6, f32[4,1]{1,0:T(4,128)S(1)} %copy.21.skip_ref, f32[8,128]{1,0:T(8,128)S(1)} %get-tuple-element.15.peak_ref), custom_call_target="tpu_custom_call" | custom-call | bytes 2101264 | tf_op jit(solution)/shard_map/finish/pallas_call | solution.py:354
  (21 shorter events, 0.1 us)
Async XLA Ops:
  0.0 1.0 copy-start.2
  1.0 13.0 %copy-start.5 = (bf16[2,256,256]{2,1,0:T(8,128)(2,1)S(1)}, bf16[2,256,256]{2,1,0:T(8,128)(2,1)}, u32[]{:S(2)}) copy-start(bf16[2,256,256]{2,1,0:T(8,128)(2,1)} %constant.115.clone.order_ref) | copy-start | bytes 786436
  1.0 13.0 %copy-start.24 = (bf16[2,256,256]{2,1,0:T(8,128)(2,1)S(1)}, bf16[2,256,256]{2,1,0:T(8,128)(2,1)}, u32[]{:S(2)}) copy-start(bf16[2,256,256]{2,1,0:T(8,128)(2,1)} %constant.116.clone) | copy-start | bytes 786436
  1.0 13.1 %copy-start.23 = (bf16[1,2,256,256]{3,2,1,0:T(8,128)(2,1)S(1)}, bf16[1,2,256,256]{3,2,1,0:T(8,128)(2,1)}, u32[]{:S(2)}) copy-start(bf16[1,2,256,256]{3,2,1,0:T(8,128)(2,1)} %constant.124) | copy-start | bytes 786436
  2.5 28.4 %all-to-all-start = ((bf16[128,4,640]{2,1,0:T(4,128)(2,1)}), bf16[128,4,640]{2,1,0:T(4,128)(2,1)S(1)}, u32[]{:S(2)}, u32[]{:S(2)}) async-start(bf16[128,4,640]{2,1,0:T(4,128)(2,1)} %pack.1), calls=%async_computation | async-start | bytes 1310720 | tf_op jit(solution)/shard_map/all_to_all | solution.py:371
  14.2 2.2 %copy-start = (f32[2,4,2,256,256]{4,3,2,1,0:T(8,128)S(1)}, f32[2,4,2,256,256]{4,3,2,1,0:T(8,128)}, u32[]{:S(2)}) copy-start(f32[2,4,2,256,256]{4,3,2,1,0:T(8,128)} %filt_ref.3) | copy-start | bytes 12582916
  19.4 25.5 %collective-permute-start = (bf16[4,256,256]{2,1,0:T(8,128)(2,1)}, bf16[4,256,256]{2,1,0:T(8,128)(2,1)S(1)}, u32[]{:S(2)}, u32[]{:S(2)}) collective-permute-start(bf16[4,256,256]{2,1,0:T(8,128)(2,1)} %get-tuple-element.19), channel_id=1, source_target_pairs={{0,64},{1,127},{2,126},{3,125},{4,124},{5,123},{6,122},{7,121},{8,... | collective-permute-start | bytes 1572872 | tf_op jit(solution)/shard_map/ppermute | solution.py:404
  23.6 30.1 %collective-permute-start.1 = (bf16[4,256,256]{2,1,0:T(8,128)(2,1)}, bf16[4,256,256]{2,1,0:T(8,128)(2,1)S(1)}, u32[]{:S(2)}, u32[]{:S(2)}) collective-permute-start(bf16[4,256,256]{2,1,0:T(8,128)(2,1)} %get-tuple-element.20), channel_id=1, source_target_pairs={{0,127},{1,126},{2,125},{3,124},{4,123},{5,122},{6,121},{7,120},{8... | collective-permute-start | bytes 1572872 | tf_op jit(solution)/shard_map/ppermute | solution.py:405
  30.9 1.2 copy-start.20
  35.4 5.6 %copy-start.7 = (f32[2,256,256]{2,1,0:T(8,128)S(1)}, f32[2,256,256]{2,1,0:T(8,128)}, u32[]{:S(2)}) copy-start(f32[2,256,256]{2,1,0:T(8,128)} %constant.118.clone.cross_base_ref) | copy-start | bytes 1572868
  35.4 5.6 %copy-start.9 = (f32[2,128,128]{2,1,0:T(8,128)S(1)}, f32[2,128,128]{2,1,0:T(8,128)}, u32[]{:S(2)}) copy-start(f32[2,128,128]{2,1,0:T(8,128)} %constant.117.clone.base_ref) | copy-start | bytes 393220
  35.4 30.4 %all-to-all-start.1 = ((bf16[128,16,256]{2,1,0:T(8,128)(2,1)}), bf16[128,16,256]{2,1,0:T(8,128)(2,1)S(1)}, u32[]{:S(2)}, u32[]{:S(2)}) async-start(bf16[128,16,256]{2,1,0:T(8,128)(2,1)} %get-tuple-element.14), calls=%async_computation.1 | async-start | bytes 2097152 | tf_op jit(solution)/shard_map/all_to_all | solution.py:371
  41.7 1.1 copy-start.12
  42.8 1.0 copy-start.14
  43.9 1.0 copy-start.16
  53.7 2.2 %copy-start.1 = (f32[2,4,2,256,256]{4,3,2,1,0:T(8,128)S(1)}, f32[2,4,2,256,256]{4,3,2,1,0:T(8,128)}, u32[]{:S(2)}) copy-start(f32[2,4,2,256,256]{4,3,2,1,0:T(8,128)} %filt_ref.3) | copy-start | bytes 12582916
  55.9 9.9 %copy-start.8 = (f32[3,2,128,1]{3,2,1,0:T(8,128)S(1)}, f32[3,2,128,1]{3,2,1,0:T(8,128)}, u32[]{:S(2)}) copy-start(f32[3,2,128,1]{3,2,1,0:T(8,128)} %copy.20.turn_ref) | copy-start | bytes 9220
  57.0 1.4 copy-start.10
  58.4 1.1 copy-start.18
  65.8 1.6 %copy-start.11 = (f32[2,2,2,256,256]{4,3,2,1,0:T(8,128)S(1)}, f32[2,2,2,256,256]{4,3,2,1,0:T(8,128)}, u32[]{:S(2)}) copy-start(f32[2,2,2,256,256]{4,3,2,1,0:T(8,128)} %copy-done.10) | copy-start | bytes 6291460
  67.4 1.4 %copy-start.13 = (f32[3,2,256,256]{3,2,1,0:T(8,128)S(1)}, f32[3,2,256,256]{3,2,1,0:T(8,128)}, u32[]{:S(2)}) copy-start(f32[3,2,256,256]{3,2,1,0:T(8,128)} %copy-done.12) | copy-start | bytes 4718596
  68.8 1.3 copy-start.15
  70.1 1.3 copy-start.17
  71.4 1.2 copy-start.19
  72.6 1.1 copy-start.21
  73.7 1.1 copy-start.22
  83.7 28.1 %copy-start.4 = (bf16[4,256,768]{2,1,0:T(8,128)(2,1)S(1)}, bf16[4,256,768]{2,1,0:T(8,128)(2,1)}, u32[]{:S(2)}) copy-start(bf16[4,256,768]{2,1,0:T(8,128)(2,1)} %constant.122.clone.table_ref) | copy-start | bytes 4718596
  111.8 8.6 %copy-start.25 = (f32[4]{0:T(128)S(1)}, f32[4]{0:T(128)}, u32[]{:S(2)}) copy-start(f32[4]{0:T(128)} %param.14) | copy-start | bytes 52
  111.8 22.7 %copy-start.3 = (bf16[4,65536]{1,0:T(4,128)(2,1)S(1)}, bf16[4,65536]{1,0:T(4,128)(2,1)}, u32[]{:S(2)}) copy-start(bf16[4,65536]{1,0:T(4,128)(2,1)} %sig_ref.3) | copy-start | bytes 1572868
  111.8 22.7 %copy-start.6 = (bf16[4,65536]{1,0:T(4,128)(2,1)S(1)}, bf16[4,65536]{1,0:T(4,128)(2,1)}, u32[]{:S(2)}) copy-start(bf16[4,65536]{1,0:T(4,128)(2,1)} %gate_ref.1) | copy-start | bytes 1572868
  116.4 18.1 %all-to-all-start.3 = ((bf16[128,16,128]{2,1,0:T(8,128)(2,1)}), bf16[128,16,128]{2,1,0:T(8,128)(2,1)S(1)}, u32[]{:S(2)}, u32[]{:S(2)}) async-start(bf16[128,16,128]{2,1,0:T(8,128)(2,1)} %last.1), calls=%async_computation.3 | async-start | bytes 1048576 | tf_op jit(solution)/shard_map/all_to_all | solution.py:371

commit v4 on v3

--- a/solution.py
+++ b/solution.py
@@ -61,7 +61,7 @@
         c, s = np.cos(ang), np.sin(ang)
         fwd = split_np(np.block([[c, -s], [s, c]]))
         inv = split_np(np.block([[c.T, s.T], [-s.T, c.T]]) / F)
-        out.append([np.concatenate([hi, hi, lo], axis=0) for hi, lo in (fwd, inv)])
+        out.append([np.concatenate(x, axis=0) for x in (fwd, inv)])
     return np.stack([out[0][0], out[1][0]]), np.stack([out[0][1], out[1][1]])
 
 
@@ -125,6 +125,11 @@
 
 def twice(hi, lo, axis):
     return jnp.concatenate([hi, lo, hi], axis=axis)
+
+
+def wide_table(t, axis):
+    hi, lo = jnp.split(t, 2, axis=axis)
+    return jnp.concatenate([hi, hi, lo], axis=axis)
 
 
 def pack_kernel(sig_ref, out_ref):
@@ -160,38 +165,42 @@
     out_ref[...] = jnp.concatenate(parts, axis=1).astype(bf16)
 
 
-def table_kernel(base_ref, cross_base_ref, lane_ref, cross_lane_ref, sub_ref, mf_ref, mi_ref, cross_ref):
+def fill_tables(table, base_ref, cross_base_ref, wave_ref, mf_ref, mi_ref, cross_ref, turn_ref):
+    def wave(row, lanes):
+        return wave_ref[table, row : row + 1, 0:lanes]
+
+    cb, sb = wave(0, ND), wave(1, ND)
     c0, s0 = base_ref[0], base_ref[1]
+    c, s = c0 * cb - s0 * sb, s0 * cb + c0 * sb
+    for out_ref, c, s in ((mf_ref, c, s), (mi_ref, c.T * (1.0 / F), s.T * (-1.0 / F))):
+        (ch, cl), (sh, sl) = split(c), split(s)
+        for part, (cc, ss) in enumerate(((ch, sh), (cl, sl))):
+            at = part * 256
+            out_ref[table, 0:128, at : at + 128] = cc
+            out_ref[table, 0:128, at + 128 : at + 256] = ss
+            out_ref[table, 128:256, at : at + 128] = -ss
+            out_ref[table, 128:256, at + 128 : at + 256] = cc
+    cb, sb = wave(2, F), wave(3, F)
     c1, s1 = cross_base_ref[0], cross_base_ref[1]
-    for r in range(3):
-        for out_ref, vec_ref, sign in ((mf_ref, lane_ref, 1.0), (mi_ref, sub_ref, -1.0)):
-            cb, sb = vec_ref[r, 0], vec_ref[r, 1]
-            c, s = c0 * cb - s0 * sb, (s0 * cb + c0 * sb) * sign
-            if sign < 0:
-                c, s = c * (1.0 / F), s * (1.0 / F)
-            (ch, cl), (sh, sl) = split(c), split(s)
-            for part, (cc, ss) in enumerate(((ch, sh), (ch, sh), (cl, sl))):
-                at = part * 256
-                out_ref[r, 0:128, at : at + 128] = cc
-                out_ref[r, 0:128, at + 128 : at + 256] = ss
-                out_ref[r, 128:256, at : at + 128] = -ss
-                out_ref[r, 128:256, at + 128 : at + 256] = cc
-        cb, sb = cross_lane_ref[r, 0], cross_lane_ref[r, 1]
-        cross_ref[r, 0] = c1 * cb - s1 * sb
-        cross_ref[r, 1] = s1 * cb + c1 * sb
-
-
-def give_kernel(half_ref, filt_ref, order_ref, sign_ref, out0_ref, out1_ref):
-    del half_ref
+    cross_ref[table, 0] = c1 * cb - s1 * sb
+    cross_ref[table, 1] = s1 * cb + c1 * sb
+    for i in range(2):
+        turn_ref[table, i] = jnp.broadcast_to(wave(4 + i, ND), (ND, ND)).T
+
+
+def give_kernel(flag_ref, filt_ref, order_ref, out0_ref, out1_ref):
+    first = flag_ref[1]
     for r, out_ref in enumerate((out0_ref, out1_ref)):
-        left, right = order_ref[r, 0], order_ref[r, 1]
+        kind = first if r == 0 else 0
+        left, right = order_ref[kind, 0], order_ref[kind, 1]
+        sign = (2 * kind - 1) * jnp.float32(1.0)
         for ri in range(2):
             for c in range(2):
                 hi, lo = split(filt_ref[ri, c, r])
                 hi, lo = split(dot(hi, right) + dot(lo, right))
                 x = dot(left, hi) + dot(left, lo)
                 if ri:
-                    x = x * sign_ref[r]
+                    x = x * sign
                 out_ref[ri * 2 + c] = encode_filter(x).astype(bf16)
 
 
@@ -208,10 +217,16 @@
                 out_ref[r, ri, c] = dot(hi, order_ref[1]) + dot(lo, order_ref[1]) + got
 
 
-def transform(re, im, table, mf_ref, mi_ref, cross_ref, turn_ref, fwd_ref, inv_ref, filt):
-    tc, ts = turn_ref[table, 0], turn_ref[table, 1]
-    hi, lo = split(jnp.concatenate([re, im], axis=0))
-    z = dot(mf_ref[table], twice(hi, lo, 0))
+def transform(re, im, table, mf_ref, mi_ref, cross_ref, turn_ref, fwd_ref, inv_ref, filt, arrive):
+    tc, ts = (jnp.concatenate([turn_ref[table, i]] * 2, axis=1) for i in range(2))
+    if im is None:
+        hi, lo = split(re)
+        t = jnp.concatenate([mf_ref[table, :, 0:128], mf_ref[table, :, 256:384]], axis=1)
+    else:
+        hi, lo = split(jnp.concatenate([re, im], axis=0))
+        t = mf_ref[table]
+    z = dot(wide_table(t, 1), twice(hi, lo, 0))
+    yield
     sums, diffs = [], []
     for c in range(2):
         at = c * 512
@@ -223,17 +238,24 @@
             zr, zi = zr * cosine + zi * sine, zi * cosine - zr * sine
             sums.append(jnp.concatenate([zr[:, :128] + zr[:, 128:], zi[:, :128] + zi[:, 128:]], axis=1))
             diffs.append(jnp.concatenate([zr[:, :128] - zr[:, 128:], zi[:, :128] - zi[:, 128:]], axis=1))
-    back = []
+    arrive("fwd")
+    spectra = []
     for odd, rows in enumerate((sums, diffs)):
         hi, lo = split(jnp.concatenate(rows, axis=0))
-        z = dot(twice(hi, lo, 1), fwd_ref[odd])
+        spectra.append(dot(twice(hi, lo, 1), wide_table(fwd_ref[odd], 0)))
+    yield
+    arrive(("filt", table))
+    arrive("inv")
+    back = []
+    for odd, z in enumerate(spectra):
         rows = []
         for c in range(2):
             zr, zi = z[c * F : (c + 1) * F, :128], z[c * F : (c + 1) * F, 128:]
             fr, fi = filt(0, c, odd), filt(1, c, odd)
             rows.append(jnp.concatenate([zr * fr - zi * fi, zi * fr + zr * fi], axis=1))
         hi, lo = split(jnp.concatenate(rows, axis=0))
-        back.append(dot(twice(hi, lo, 1), inv_ref[odd]))
+        back.append(dot(twice(hi, lo, 1), wide_table(inv_ref[odd], 0)))
+    yield
     even, odd = back
     tops, bottoms = [], []
     for c in range(2):
@@ -252,16 +274,46 @@
         tops += [ar + br, ur * tc - ui * ts]
         bottoms += [ai + bi, ui * tc + ur * ts]
     hi, lo = split(jnp.concatenate([jnp.concatenate(tops, axis=1), jnp.concatenate(bottoms, axis=1)], axis=0))
-    return dot(mi_ref[table], twice(hi, lo, 0))
+    t = mi_ref[table] if im is not None else mi_ref[table, 0:128]
+    yield dot(wide_table(t, 1), twice(hi, lo, 0))
 
 
 def middle_kernel(
-    y_ref, peak_ref, mf_ref, mi_ref, cross_ref, turn_ref, fwd_ref, inv_ref, filt_ref, other_ref, generic_ref, out_ref, buf, obuf
+    y_hbm, base_hbm, cross_base_hbm, fwd_hbm, inv_hbm, filt_hbm, other_hbm, peak_ref, wave_ref, generic_ref, out_hbm, buf, obuf, *held
 ):
+    y_ref, base_ref, cross_base_ref, fwd_ref, inv_ref, filt_ref, other_ref = held[:7]
+    mf_ref, mi_ref, cross_ref, turn_ref, out_ref, sem = held[7:]
+    blocks = [pl.ds(m * ROWS, ROWS) for m in range(STEPS)]
+    sources = {"base": (base_hbm, base_ref), "cross": (cross_base_hbm, cross_base_ref)}
+    for m, b in enumerate(blocks):
+        sources["y", m] = (y_hbm.at[b], y_ref.at[b])
+    sources["fwd"] = (fwd_hbm, fwd_ref)
+    for ri in range(2):
+        sources["filt", 0, ri] = (filt_hbm.at[0, ri], filt_ref.at[0, ri])
+    sources["inv"] = (inv_hbm, inv_ref)
+    for ri in range(2):
+        sources["filt", 1, ri] = (filt_hbm.at[1, ri], filt_ref.at[1, ri])
+    sources["filt", 2, 0] = (other_hbm, other_ref)
+    copies = {k: pltpu.make_async_copy(*v, sem.at[i]) for i, (k, v) in enumerate(sources.items())}
+    waiting = set(copies)
+
+    def arrive(key):
+        for k in list(copies):
+            if k in waiting and (k == key or k[:2] == key):
+                waiting.remove(k)
+                copies[k].wait()
+
+    for copy in copies.values():
+        copy.start()
     peak = peak_ref[0:1, 0:1]
     tables = (mf_ref, mi_ref, cross_ref, turn_ref, fwd_ref, inv_ref)
+    arrive("base")
+    arrive("cross")
+    for r in range(2):
+        fill_tables(r, base_ref, cross_base_ref, wave_ref, *tables[:4])
     for m in range(STEPS):
-        y = decode(y_ref[pl.ds(m * ROWS, ROWS)].astype(f32), peak, FIELD_CODE).reshape(ROWS * 16, F)
+        arrive(("y", m))
+        y = decode(y_ref[blocks[m]].astype(f32), peak, FIELD_CODE).reshape(ROWS * 16, F)
         for g in range(2):
             buf[g, pl.ds(m * ROWS * 16, ROWS * 16), :] = y[:, g * 128 : (g + 1) * 128]
 
@@ -288,25 +340,42 @@
     def filt_of(r):
         return lambda ri, c, odd: filt_ref[r, ri, c, :, odd * 128 : (odd + 1) * 128]
 
+    running = []
     for r in range(2):
         im = field(r, 1)
         if r == 0:
             im = im * generic_ref[0]
-        z = transform(field(r, 0), im, r, *tables, filt_of(r))
-        put(z, r, 0, 0)
-        put(z, r, 1, 1)
+        running.append(transform(field(r, 0), im, r, *tables, filt_of(r), arrive))
+    for stage in range(4):
+        for r in range(2):
+            z = next(running[r])
+            if stage == 3:
+                put(z, r, 0, 0)
+                put(z, r, 1, 1)
+
+    arrive(("filt", 2))
 
     @pl.when(generic_ref[0] < 0.5)
     def _():
-        re = field(0, 1)
-        z = transform(
-            re, jnp.zeros_like(re), 2, *tables, lambda ri, c, odd: other_ref[ri, c, :, odd * 128 : (odd + 1) * 128]
+        fill_tables(2, base_ref, cross_base_ref, wave_ref, *tables[:4])
+        *_, z = transform(
+            field(0, 1),
+            None,
+            2,
+            *tables,
+            lambda ri, c, odd: other_ref[ri, c, :, odd * 128 : (odd + 1) * 128],
+            arrive,
         )
         put(z, 0, 1, 0)
 
+    writes = []
     for m in range(STEPS):
         y = jnp.concatenate([obuf[g, pl.ds(m * ROWS * 16, ROWS * 16), :] for g in range(2)], axis=1)
-        out_ref[pl.ds(m * ROWS, ROWS)] = encode(y, peak, FILTERED_CODE).reshape(ROWS, 16, F).astype(bf16)
+        out_ref[blocks[m]] = encode(y, peak, FILTERED_CODE).reshape(ROWS, 16, F).astype(bf16)
+        writes.append(pltpu.make_async_copy(out_ref.at[blocks[m]], out_hbm.at[blocks[m]], sem.at[len(copies) + m]))
+        writes[-1].start()
+    for copy in writes:
+        copy.wait()
 
 
 def last_kernel(y_ref, table_ref, peak_ref, out_ref, acc, buf):
@@ -347,6 +416,7 @@
 
 VMEM = pl.BlockSpec(memory_space=pltpu.VMEM)
 SMEM = pl.BlockSpec(memory_space=pltpu.SMEM)
+ANY = pl.BlockSpec(memory_space=pl.ANY)
 
 
 def call(kernel, ins, outs, scratch, name, flops=0, limit=16, grid=(), in_specs=None, out_specs=None, scalars=0):
@@ -358,7 +428,7 @@
             grid=grid,
             in_specs=in_specs or [VMEM] * len(ins),
             out_specs=out_specs or [VMEM] * len(outs),
-            scratch_shapes=[pltpu.VMEM(s, d) for s, d in scratch],
+            scratch_shapes=[d(s) if d is pltpu.SemaphoreType.DMA else pltpu.VMEM(s, d) for s, d in scratch],
         ),
         out_shape=outs,
         compiler_params=pltpu.CompilerParams(vmem_limit_bytes=limit * 2**20),
@@ -383,22 +453,22 @@
     upper = (place >= ND // 2).astype(jnp.int32)
     special = place % (ND // 2) == 0
     generic = jnp.where(special, 0.0, 1.0).astype(f32)[None]
-    plain, back = (jnp.asarray(t) for t in order_tables())
-    order = jnp.stack([jnp.where(place == 0, plain, back), back])
-    sign = jnp.stack([jnp.where(place == 0, 1.0, -1.0), -1.0]).astype(f32)
+    plain, back = order_tables()
     block = (2, 2, 2, F, F)
     given = call(
         give_kernel,
-        ((1 - upper)[None], spectrum, order, sign),
+        (jnp.stack([1 - upper, (place == 0).astype(jnp.int32)]), spectrum, jnp.asarray(np.stack([back, plain]))),
         [shape(4, F, F)] * 2,
         [],
         "give",
+        limit=58,
         flops=2**30,
         grid=(1,),
-        in_specs=[pl.BlockSpec(block, lambda i, half: (0, half[0], 0, 0, 0)), VMEM, SMEM],
-        out_specs=[pl.BlockSpec((4, F, F), lambda i, half: (0, 0, 0))] * 2,
+        in_specs=[pl.BlockSpec(block, lambda i, flag: (0, flag[0], 0, 0, 0)), VMEM],
+        out_specs=[pl.BlockSpec((4, F, F), lambda i, flag: (0, 0, 0))] * 2,
         scalars=1,
     )
+    spread, *_ = lax.optimization_barrier((spread, *given))
     mirror = [(p, (ND // 2 - p) if p % (ND // 2) == 0 else ND - p) for p in range(ND)]
     got = [
         lax.ppermute(given[0], AXES, mirror),
@@ -406,23 +476,11 @@
     ]
 
     k1 = jnp.stack([place * 2, place * 2 + 1, ND - place * 2])[:, None] % F
-    half = jnp.arange(ND, dtype=jnp.int32)
-
-    def wave(index, period):
-        angle = (2 * np.pi / period) * (index % period).astype(f32)
-        return jnp.stack([jnp.cos(angle), jnp.sin(angle)], axis=1)
-
-    mid = wave(k1 * half, F * ND)
-    fine = wave(k1 * jnp.arange(F, dtype=jnp.int32), F**3)
-    turn = wave(k1 + F * half, F * F)
+    lane = jnp.arange(F, dtype=jnp.int32)
+    turns = jnp.stack([k1 * lane % (F * ND) * (F * 2), k1 * lane, (k1 + F * lane) % (F * F) * F], axis=1)
+    angle = (2 * np.pi / F**3) * turns.astype(f32)
+    wave = jnp.stack([jnp.cos(angle), jnp.sin(angle)], axis=2).reshape(3, 6, F)
     base, cross_base = (jnp.asarray(t) for t in base_tables())
-    mf, mi, cross = call(
-        table_kernel,
-        (base, cross_base, mid[:, :, None, :], fine[:, :, None, :], mid[:, :, :, None]),
-        [shape(3, 256, 768), shape(3, 256, 768), shape(3, 2, F, F, dtype=f32)],
-        [],
-        "tables",
-    )
     inner_fwd, inner_inv = (jnp.asarray(t) for t in inner_tables())
 
     field, peak = call(
@@ -439,11 +497,12 @@
     field = exchange(field)
     filt, other = call(
         combine_kernel,
-        (upper[None], spectrum, plain, *got, generic),
+        (upper[None], spectrum, jnp.asarray(plain), *got, generic),
         [shape(2, 2, 2, F, F, dtype=f32), shape(2, 2, F, F, dtype=f32)],
         [],
         "combine",
-        flops=2**29,
+        limit=58,
+        flops=2**34,
         grid=(1,),
         in_specs=[pl.BlockSpec(block, lambda i, half: (0, half[0], 0, 0, 0)), VMEM, VMEM, VMEM, SMEM],
         out_specs=[
@@ -452,15 +511,21 @@
         ],
         scalars=1,
     )
+    loads = (field, base, cross_base, inner_fwd, inner_inv, filt, other)
     (filtered,) = call(
         middle_kernel,
-        (field, peak, mf, mi, cross, turn[:, :, :, None], inner_fwd, inner_inv, filt, other, generic),
+        (*loads, peak, wave, generic),
         [shape(ND, 16, F)],
-        [((2, ND * 16, 128), f32)] * 2,
+        [((2, ND * 16, 128), f32)] * 2
+        + [(x.shape, x.dtype) for x in loads]
+        + [((3, 256, 512), bf16)] * 2
+        + [((3, 2, F, F), f32), ((3, 2, ND, ND), f32), ((ND, 16, F), bf16)]
+        + [((9 + 2 * STEPS,), pltpu.SemaphoreType.DMA)],
         "middle",
         flops=4 * 2**30,
-        limit=24,
-        in_specs=[VMEM] * 10 + [SMEM],
+        limit=58,
+        in_specs=[ANY] * 7 + [VMEM, VMEM, SMEM],
+        out_specs=[ANY],
     )
     filtered = exchange(filtered)
     (conv,) = call(

time: 137 us -> 131 us (0.956)
  local copies, waits for them, and re-layouts: 22.6 us -> 4.39 us
  Pallas kernels: 24.9 us -> 31.6 us
  waiting for transfers between devices: 32.6 us -> 37.1 us
    unnamed x52 -> x22, local copies, waits for them, and re-layouts: 21.3 us -> 3.42 us
    pallas_call x8 -> x7, Pallas kernels: 24.9 us -> 31.6 us  [call(): pl.pallas_call(kernel, grid_spec=pltpu.PrefetchScalarGridSpec(num_scalar_...]
    ppermute x1, waiting for transfers between devices: 0.01 us -> 2.86 us  [per_device(): lax.ppermute(given[0], AXES, mirror)]
    ppermute x1, waiting for transfers between devices: 8.82 us -> 11 us  [per_device(): lax.ppermute(given[1], AXES, [(p, ND - 1 - p) for p in range(ND)])]
  transfers between devices with their start and end apart: 5 -> 5, of which waited for: 4 -> 5; matrix products, arithmetic and copies ran while one was open for 1% -> 2% of each run, Pallas kernels for 6% -> 10%
where the time goes in v4:
time: 131 us
  waiting for transfers between devices  37.1 us (28%)
  Pallas kernels  31.6 us (24%)
  blocking collectives  28.4 us (22%)
  starting transfers between devices  28.3 us (22%)
  local copies, waits for them, and re-layouts  4.39 us (3%)
    pallas_call x7, Pallas kernels, call(): pl.pallas_call(kernel, grid_spec=pltpu.PrefetchScalarGridSpec(num_scalar_...  31.6 us
    all_to_all x1, blocking collectives, exchange(): return lax.all_to_all(x, AXES, split_axis=0, concat_axis=0, tiled=True)  28.4 us
    all_to_all x3, waiting for transfers between devices, exchange(): return lax.all_to_all(x, AXES, split_axis=0, concat_axis=0, tiled=True)  23.2 us
    all_to_all x3, starting transfers between devices, exchange(): return lax.all_to_all(x, AXES, split_axis=0, concat_axis=0, tiled=True)  20.3 us
    ppermute x1, waiting for transfers between devices, per_device(): lax.ppermute(given[1], AXES, [(p, ND - 1 - p) for p in range(ND)])  11 us
    ppermute x1, starting transfers between devices, per_device(): lax.ppermute(given[0], AXES, mirror)  4.17 us
    ppermute x1, starting transfers between devices, per_device(): lax.ppermute(given[1], AXES, [(p, ND - 1 - p) for p in range(ND)])  3.8 us
    unnamed x22, local copies, waits for them, and re-layouts  3.42 us
  transfers between devices with their start and end apart: 5, of which 5 were waited for; matrix products, arithmetic and copies ran while one was open for 2% of the time, Pallas kernels for 10%

profile of v4, /device:TPU:1, one launch (start us, length us, event | category | flops | bytes accessed | tf_op | source)
XLA Modules:
  0.0 131.0 jit_solution(3337438517206708519)
XLA Ops:
  0.0 0.0 copy-start
  0.0 1.0 copy-done
  1.0 1.4 %pack.1 = bf16[128,4,640]{2,1,0:T(4,128)(2,1)} custom-call(bf16[4,65536]{1,0:T(4,128)(2,1)S(1)} %copy-done), custom_call_target="tpu_custom_call" | custom-call | bytes 1179648 | tf_op jit(solution)/shard_map/pack/pallas_call | solution.py:424
  2.5 11.5 %all-to-all-start = ((bf16[128,4,640]{2,1,0:T(4,128)(2,1)}), bf16[128,4,640]{2,1,0:T(4,128)(2,1)S(1)}, u32[]{:S(2)}, u32[]{:S(2)}) async-start(bf16[128,4,640]{2,1,0:T(4,128)(2,1)} %pack.1), calls=%async_computation | async-start | bytes 1310720 | tf_op jit(solution)/shard_map/all_to_all | solution.py:441
  14.0 0.6 pad_add_fusion.flag_ref
  14.6 0.0 copy-start.6
  14.6 4.9 %give.1 = (bf16[4,256,256]{2,1,0:T(8,128)(2,1)}, bf16[4,256,256]{2,1,0:T(8,128)(2,1)}) custom-call(s32[2]{0:T(128)} %pad_add_fusion.flag_ref, f32[2,4,2,256,256]{4,3,2,1,0:T(8,128)} %filt_ref.3, bf16[2,2,256,256]{3,2,1,0:T(8,128)(2,1)} %constant.96.clone.order_ref), custom_call_target="tpu_custom_call" | custom-call | flops 1073741824 | bytes 5767176 | tf_op jit(solution)/shard_map/give/pallas_call | solution.py:424
  19.5 4.2 %collective-permute-start = (bf16[4,256,256]{2,1,0:T(8,128)(2,1)}, bf16[4,256,256]{2,1,0:T(8,128)(2,1)S(1)}, u32[]{:S(2)}, u32[]{:S(2)}) collective-permute-start(bf16[4,256,256]{2,1,0:T(8,128)(2,1)} %get-tuple-element.12), channel_id=1, source_target_pairs={{0,64},{1,127},{2,126},{3,125},{4,124},{5,123},{6,122},{7,121},{8,... | collective-permute-start | bytes 1572872 | tf_op jit(solution)/shard_map/ppermute | solution.py:474
  23.7 3.8 %collective-permute-start.1 = (bf16[4,256,256]{2,1,0:T(8,128)(2,1)}, bf16[4,256,256]{2,1,0:T(8,128)(2,1)S(1)}, u32[]{:S(2)}, u32[]{:S(2)}) collective-permute-start(bf16[4,256,256]{2,1,0:T(8,128)(2,1)} %get-tuple-element.13), channel_id=1, source_target_pairs={{0,127},{1,126},{2,125},{3,124},{4,123},{5,122},{6,121},{7,120},{8... | collective-permute-start | bytes 1572872 | tf_op jit(solution)/shard_map/ppermute | solution.py:475
  27.5 0.1 and_select_fusion.2
  27.6 0.1 fusion.5
  27.7 0.3 fusion.9
  27.9 0.2 sin.10
  28.2 0.6 reshape.294.wave_ref
  28.9 2.1 %all-to-all-done.x_ref = bf16[128,4,640]{2,1,0:T(4,128)(2,1)S(1)} async-done(((bf16[128,4,640]{2,1,0:T(4,128)(2,1)}), bf16[128,4,640]{2,1,0:T(4,128)(2,1)S(1)}, u32[]{:S(2)}, u32[]{:S(2)}) %all-to-all-start) | async-done | bytes 655392 | tf_op jit(solution)/shard_map/all_to_all | solution.py:441
  30.9 0.0 copy-done.6
  30.9 3.3 %outer.1 = (bf16[128,16,256]{2,1,0:T(8,128)(2,1)}, f32[8,128]{1,0:T(8,128)S(1)}) custom-call(bf16[128,4,640]{2,1,0:T(4,128)(2,1)S(1)} %all-to-all-done.x_ref, bf16[1024,512]{1,0:T(8,128)(2,1)S(1)} %copy-done.6), custom_call_target="tpu_custom_call" | custom-call | flops 536870912 | bytes 2756608 | tf_op jit(solution)/shard_map/outer/pallas_call | solution.py:424
  34.2 0.0 copy-start.4
  34.2 0.6 copy-done.4
  34.8 4.8 %all-to-all-start.1 = ((bf16[128,16,256]{2,1,0:T(8,128)(2,1)}), bf16[128,16,256]{2,1,0:T(8,128)(2,1)S(1)}, u32[]{:S(2)}, u32[]{:S(2)}) async-start(bf16[128,16,256]{2,1,0:T(8,128)(2,1)} %get-tuple-element.15), calls=%async_computation.1 | async-start | bytes 2097152 | tf_op jit(solution)/shard_map/all_to_all | solution.py:441
  39.6 2.9 %collective-permute-done.got0_ref = bf16[4,256,256]{2,1,0:T(8,128)(2,1)S(1)} collective-permute-done((bf16[4,256,256]{2,1,0:T(8,128)(2,1)}, bf16[4,256,256]{2,1,0:T(8,128)(2,1)S(1)}, u32[]{:S(2)}, u32[]{:S(2)}) %collective-permute-start) | collective-permute-done | bytes 524320 | tf_op jit(solution)/shard_map/ppermute | solution.py:474
  42.5 0.0 copy-start.9
  42.5 11.0 %collective-permute-done.1.got1_ref = bf16[4,256,256]{2,1,0:T(8,128)(2,1)S(1)} collective-permute-done((bf16[4,256,256]{2,1,0:T(8,128)(2,1)}, bf16[4,256,256]{2,1,0:T(8,128)(2,1)S(1)}, u32[]{:S(2)}, u32[]{:S(2)}) %collective-permute-start.1) | collective-permute-done | bytes 524320 | tf_op jit(solution)/shard_map/ppermute | solution.py:475
  53.5 0.0 copy-start.10
  53.5 0.0 copy-done.9
  53.5 0.8 copy-done.10
  54.3 4.4 %combine.1 = (f32[2,2,2,256,256]{4,3,2,1,0:T(8,128)}, f32[2,2,256,256]{3,2,1,0:T(8,128)}) custom-call(s32[1]{0:T(128)} %bitcast.2.half_ref, f32[2,4,2,256,256]{4,3,2,1,0:T(8,128)} %filt_ref.3, bf16[2,256,256]{2,1,0:T(8,128)(2,1)} %constant.102.clone.order_ref, bf16[4,256,256]{2,1,0:T(8,128)(2,1)} %copy-done.9, bf16[4,256,256]{2,1,0:T(8,128)(2,1)} %copy-done.10, ...), custom_call_target="tpu_custom_call" | custom-call | flops 17179869184 | bytes 8650760 | tf_op jit(solution)/shard_map/combine/pallas_call | solution.py:424
  58.7 7.2 %all-to-all-done.1.y_hbm = bf16[128,16,256]{2,1,0:T(8,128)(2,1)S(1)} async-done(((bf16[128,16,256]{2,1,0:T(8,128)(2,1)}), bf16[128,16,256]{2,1,0:T(8,128)(2,1)S(1)}, u32[]{:S(2)}, u32[]{:S(2)}) %all-to-all-start.1) | async-done | bytes 1048608 | tf_op jit(solution)/shard_map/all_to_all | solution.py:441
  65.9 0.0 copy-start.7
  65.9 1.0 copy-done.7
  66.9 11.0 %middle.1 = bf16[128,16,256]{2,1,0:T(8,128)(2,1)} custom-call(bf16[128,16,256]{2,1,0:T(8,128)(2,1)} %copy-done.7, f32[2,128,128]{2,1,0:T(8,128)} %constant.97.clone.base_hbm, f32[2,256,256]{2,1,0:T(8,128)} %constant.98.clone.cross_base_hbm, bf16[2,512,256]{2,1,0:T(8,128)(2,1)} %constant.99.clone.fwd_hbm, bf16[2,512,256]{2,1,0:T(8,128)(2,1)} %constant.100.clone.inv_hbm, ...), custom_call_target="tpu_custom_call" | custom-call | flops 4294967296 | bytes 6969348 | tf_op jit(solution)/shard_map/middle/pallas_call | solution.py:424
  77.9 0.0 copy-start.2
  77.9 0.0 copy-start.5
  77.9 28.4 %all_to_all.20.y_ref = bf16[128,16,256]{2,1,0:T(8,128)(2,1)S(1)} all-to-all(bf16[128,16,256]{2,1,0:T(8,128)(2,1)} %middle.1), channel_id=1, replica_groups=mesh['wide'=16,'narrow'=8] {'wide','narrow'}, dimensions={0} | all-to-all | bytes 2097152 | tf_op jit(solution)/shard_map/all_to_all | solution.py:441
  106.3 0.0 copy-done.2
  106.3 0.0 copy-done.5
  106.3 0.0 copy-start.8
  106.3 0.0 copy-start.1
  106.3 0.0 copy-start.3
  106.4 4.6 %last.1 = bf16[128,16,128]{2,1,0:T(8,128)(2,1)} custom-call(bf16[128,16,256]{2,1,0:T(8,128)(2,1)S(1)} %all_to_all.20.y_ref, bf16[4,256,768]{2,1,0:T(8,128)(2,1)S(1)} %copy-done.2, f32[8,128]{1,0:T(8,128)S(1)} %copy-done.5), custom_call_target="tpu_custom_call" | custom-call | flops 536870912 | bytes 3149824 | tf_op jit(solution)/shard_map/last/pallas_call | solution.py:424
  110.9 4.0 %all-to-all-start.3 = ((bf16[128,16,128]{2,1,0:T(8,128)(2,1)}), bf16[128,16,128]{2,1,0:T(8,128)(2,1)S(1)}, u32[]{:S(2)}, u32[]{:S(2)}) async-start(bf16[128,16,128]{2,1,0:T(8,128)(2,1)} %last.1), calls=%async_computation.3 | async-start | bytes 1048576 | tf_op jit(solution)/shard_map/all_to_all | solution.py:441
  115.0 0.0 copy-done.8
  115.0 0.1 copy.15.skip_ref
  115.1 13.9 %all-to-all-done.3.y_ref = bf16[128,16,128]{2,1,0:T(8,128)(2,1)S(1)} async-done(((bf16[128,16,128]{2,1,0:T(8,128)(2,1)}), bf16[128,16,128]{2,1,0:T(8,128)(2,1)S(1)}, u32[]{:S(2)}, u32[]{:S(2)}) %all-to-all-start.3) | async-done | bytes 524320 | tf_op jit(solution)/shard_map/all_to_all | solution.py:441
  129.0 0.0 copy-done.1
  129.0 0.0 copy-done.3
  129.0 2.0 %finish.1 = bf16[4,65536]{1,0:T(4,128)(2,1)} custom-call(bf16[128,16,128]{2,1,0:T(8,128)(2,1)S(1)} %all-to-all-done.3.y_ref, bf16[4,65536]{1,0:T(4,128)(2,1)S(1)} %copy-done.1, bf16[4,65536]{1,0:T(4,128)(2,1)S(1)} %copy-done.3, f32[4,1]{1,0:T(4,128)S(1)} %copy.15.skip_ref, f32[8,128]{1,0:T(8,128)S(1)} %copy-done.5), custom_call_target="tpu_custom_call" | custom-call | bytes 2101264 | tf_op jit(solution)/shard_map/finish/pallas_call | solution.py:424
  (2 shorter events, 0.0 us)
Async XLA Ops:
  0.0 1.0 copy-start
  2.5 28.4 %all-to-all-start = ((bf16[128,4,640]{2,1,0:T(4,128)(2,1)}), bf16[128,4,640]{2,1,0:T(4,128)(2,1)S(1)}, u32[]{:S(2)}, u32[]{:S(2)}) async-start(bf16[128,4,640]{2,1,0:T(4,128)(2,1)} %pack.1), calls=%async_computation | async-start | bytes 1310720 | tf_op jit(solution)/shard_map/all_to_all | solution.py:441
  14.6 16.3 %copy-start.6 = (bf16[1024,512]{1,0:T(8,128)(2,1)S(1)}, bf16[1024,512]{1,0:T(8,128)(2,1)}, u32[]{:S(2)}) copy-start(bf16[1024,512]{1,0:T(8,128)(2,1)} %constant.101.clone.table_ref) | copy-start | bytes 3145732
  19.5 22.9 %collective-permute-start = (bf16[4,256,256]{2,1,0:T(8,128)(2,1)}, bf16[4,256,256]{2,1,0:T(8,128)(2,1)S(1)}, u32[]{:S(2)}, u32[]{:S(2)}) collective-permute-start(bf16[4,256,256]{2,1,0:T(8,128)(2,1)} %get-tuple-element.12), channel_id=1, source_target_pairs={{0,64},{1,127},{2,126},{3,125},{4,124},{5,123},{6,122},{7,121},{8,... | collective-permute-start | bytes 1572872 | tf_op jit(solution)/shard_map/ppermute | solution.py:474
  23.7 29.8 %collective-permute-start.1 = (bf16[4,256,256]{2,1,0:T(8,128)(2,1)}, bf16[4,256,256]{2,1,0:T(8,128)(2,1)S(1)}, u32[]{:S(2)}, u32[]{:S(2)}) collective-permute-start(bf16[4,256,256]{2,1,0:T(8,128)(2,1)} %get-tuple-element.13), channel_id=1, source_target_pairs={{0,127},{1,126},{2,125},{3,124},{4,123},{5,122},{6,121},{7,120},{8... | collective-permute-start | bytes 1572872 | tf_op jit(solution)/shard_map/ppermute | solution.py:475
  34.2 0.6 copy-start.4
  34.8 31.1 %all-to-all-start.1 = ((bf16[128,16,256]{2,1,0:T(8,128)(2,1)}), bf16[128,16,256]{2,1,0:T(8,128)(2,1)S(1)}, u32[]{:S(2)}, u32[]{:S(2)}) async-start(bf16[128,16,256]{2,1,0:T(8,128)(2,1)} %get-tuple-element.15), calls=%async_computation.1 | async-start | bytes 2097152 | tf_op jit(solution)/shard_map/all_to_all | solution.py:441
  42.5 11.0 %copy-start.9 = (bf16[4,256,256]{2,1,0:T(8,128)(2,1)}, bf16[4,256,256]{2,1,0:T(8,128)(2,1)S(1)}, u32[]{:S(2)}) copy-start(bf16[4,256,256]{2,1,0:T(8,128)(2,1)S(1)} %collective-permute-done.got0_ref) | copy-start | bytes 1572868
  53.5 0.8 copy-start.10
  65.9 1.0 copy-start.7
  77.9 28.5 %copy-start.2 = (bf16[4,256,768]{2,1,0:T(8,128)(2,1)S(1)}, bf16[4,256,768]{2,1,0:T(8,128)(2,1)}, u32[]{:S(2)}) copy-start(bf16[4,256,768]{2,1,0:T(8,128)(2,1)} %constant.103.clone.table_ref) | copy-start | bytes 4718596
  77.9 28.5 %copy-start.5 = (f32[8,128]{1,0:T(8,128)S(1)}, f32[8,128]{1,0:T(8,128)}, u32[]{:S(2)}) copy-start(f32[8,128]{1,0:T(8,128)} %copy-done.4) | copy-start | bytes 12292
  106.3 8.6 %copy-start.8 = (f32[4]{0:T(128)S(1)}, f32[4]{0:T(128)}, u32[]{:S(2)}) copy-start(f32[4]{0:T(128)} %param.14) | copy-start | bytes 52
  106.3 22.7 %copy-start.1 = (bf16[4,65536]{1,0:T(4,128)(2,1)S(1)}, bf16[4,65536]{1,0:T(4,128)(2,1)}, u32[]{:S(2)}) copy-start(bf16[4,65536]{1,0:T(4,128)(2,1)} %sig_ref.3) | copy-start | bytes 1572868
  106.3 22.6 %copy-start.3 = (bf16[4,65536]{1,0:T(4,128)(2,1)S(1)}, bf16[4,65536]{1,0:T(4,128)(2,1)}, u32[]{:S(2)}) copy-start(bf16[4,65536]{1,0:T(4,128)(2,1)} %gate_ref.1) | copy-start | bytes 1572868
  110.9 18.1 %all-to-all-start.3 = ((bf16[128,16,128]{2,1,0:T(8,128)(2,1)}), bf16[128,16,128]{2,1,0:T(8,128)(2,1)S(1)}, u32[]{:S(2)}, u32[]{:S(2)}) async-start(bf16[128,16,128]{2,1,0:T(8,128)(2,1)} %last.1), calls=%async_computation.3 | async-start | bytes 1048576 | tf_op jit(solution)/shard_map/all_to_all | solution.py:441

commit v5 on v4

--- a/solution.py
+++ b/solution.py
@@ -170,7 +170,7 @@
         return wave_ref[table, row : row + 1, 0:lanes]
 
     cb, sb = wave(0, ND), wave(1, ND)
-    c0, s0 = base_ref[0], base_ref[1]
+    c0, s0 = base_ref[0:128, 0:128], base_ref[128:256, 0:128]
     c, s = c0 * cb - s0 * sb, s0 * cb + c0 * sb
     for out_ref, c, s in ((mf_ref, c, s), (mi_ref, c.T * (1.0 / F), s.T * (-1.0 / F))):
         (ch, cl), (sh, sl) = split(c), split(s)
@@ -188,36 +188,57 @@
         turn_ref[table, i] = jnp.broadcast_to(wave(4 + i, ND), (ND, ND)).T
 
 
-def give_kernel(flag_ref, filt_ref, order_ref, out0_ref, out1_ref):
-    first = flag_ref[1]
-    for r, out_ref in enumerate((out0_ref, out1_ref)):
-        kind = first if r == 0 else 0
-        left, right = order_ref[kind, 0], order_ref[kind, 1]
-        sign = (2 * kind - 1) * jnp.float32(1.0)
-        for ri in range(2):
-            for c in range(2):
-                hi, lo = split(filt_ref[ri, c, r])
-                hi, lo = split(dot(hi, right) + dot(lo, right))
-                x = dot(left, hi) + dot(left, lo)
-                if ri:
-                    x = x * sign
-                out_ref[ri * 2 + c] = encode_filter(x).astype(bf16)
-
-
-def combine_kernel(half_ref, filt_ref, order_ref, got0_ref, got1_ref, generic_ref, out_ref, other_ref):
-    del half_ref
+def place_of():
+    return lax.axis_index("wide") * lax.axis_size("narrow") + lax.axis_index("narrow")
+
+
+def fetch_filter(r, pair, filt_hbm, held, sem):
+    copies = []
+    for i in range(4):
+        source = filt_hbm.at[i // 2, pair * 2 + i % 2, r]
+        copies.append(pltpu.make_async_copy(source, held.at[r, i], sem.at[r, i]))
+        copies[-1].start()
+    return copies
+
+
+def give_kernel(r, order_ref, filt_hbm, out_ref, held, sem):
+    place = place_of()
+    copies = fetch_filter(r, 1 - place // (ND // 2), filt_hbm, held, sem)
+    kind = jnp.where(place == 0, 1, 0) if r == 0 else 0
+    left, right = order_ref[kind, 0], order_ref[kind, 1]
+    sign = (2 * kind - 1) * jnp.float32(1.0)
+    for copy in copies:
+        copy.wait()
+    for i in range(4):
+        hi, lo = split(held[r, i])
+        hi, lo = split(dot(hi, right) + dot(lo, right))
+        x = dot(left, hi) + dot(left, lo)
+        if i >= 2:
+            x = x * sign
+        out_ref[i] = encode_filter(x).astype(bf16)
+
+
+def combine_kernel(filt_hbm, order_ref, cross_base_ref, base_ref, got0_ref, got1_ref, out_ref, held, sem):
+    place = place_of()
+    copies = [fetch_filter(r, place // (ND // 2), filt_hbm, held, sem) for r in range(2)]
+    generic = jnp.where(place % (ND // 2) == 0, 0.0, 1.0)
+    out_ref[12:14] = cross_base_ref[...]
+    out_ref[14, 0:128, 0:128] = base_ref[0]
+    out_ref[14, 128:256, 0:128] = base_ref[1]
+    out_ref[14, :, 128:256] = jnp.zeros((F, 128), f32)
+    for copy in (*copies[0], *copies[1]):
+        copy.wait()
     for r, got_ref in enumerate((got0_ref, got1_ref)):
-        for ri in range(2):
-            for c in range(2):
-                got = decode_filter(got_ref[ri * 2 + c].astype(f32))
-                if r == 0:
-                    other_ref[ri, c] = got
-                    got = got * generic_ref[0]
-                hi, lo = split(filt_ref[ri, c, r])
-                out_ref[r, ri, c] = dot(hi, order_ref[1]) + dot(lo, order_ref[1]) + got
-
-
-def transform(re, im, table, mf_ref, mi_ref, cross_ref, turn_ref, fwd_ref, inv_ref, filt, arrive):
+        for i in range(4):
+            got = decode_filter(got_ref[i].astype(f32))
+            if r == 0:
+                out_ref[8 + i] = got
+                got = got * generic
+            hi, lo = split(held[r, i])
+            out_ref[r * 4 + i] = dot(hi, order_ref[1]) + dot(lo, order_ref[1]) + got
+
+
+def transform(re, im, table, mf_ref, mi_ref, cross_ref, turn_ref, inner_ref, filt, arrive):
     tc, ts = (jnp.concatenate([turn_ref[table, i]] * 2, axis=1) for i in range(2))
     if im is None:
         hi, lo = split(re)
@@ -238,14 +259,13 @@
             zr, zi = zr * cosine + zi * sine, zi * cosine - zr * sine
             sums.append(jnp.concatenate([zr[:, :128] + zr[:, 128:], zi[:, :128] + zi[:, 128:]], axis=1))
             diffs.append(jnp.concatenate([zr[:, :128] - zr[:, 128:], zi[:, :128] - zi[:, 128:]], axis=1))
-    arrive("fwd")
+    arrive("inner")
     spectra = []
     for odd, rows in enumerate((sums, diffs)):
         hi, lo = split(jnp.concatenate(rows, axis=0))
-        spectra.append(dot(twice(hi, lo, 1), wide_table(fwd_ref[odd], 0)))
+        spectra.append(dot(twice(hi, lo, 1), wide_table(inner_ref[0, odd], 0)))
     yield
     arrive(("filt", table))
-    arrive("inv")
     back = []
     for odd, z in enumerate(spectra):
         rows = []
@@ -254,7 +274,7 @@
             fr, fi = filt(0, c, odd), filt(1, c, odd)
             rows.append(jnp.concatenate([zr * fr - zi * fi, zi * fr + zr * fi], axis=1))
         hi, lo = split(jnp.concatenate(rows, axis=0))
-        back.append(dot(twice(hi, lo, 1), wide_table(inv_ref[odd], 0)))
+        back.append(dot(twice(hi, lo, 1), wide_table(inner_ref[1, odd], 0)))
     yield
     even, odd = back
     tops, bottoms = [], []
@@ -278,22 +298,20 @@
     yield dot(wide_table(t, 1), twice(hi, lo, 0))
 
 
-def middle_kernel(
-    y_hbm, base_hbm, cross_base_hbm, fwd_hbm, inv_hbm, filt_hbm, other_hbm, peak_ref, wave_ref, generic_ref, out_hbm, buf, obuf, *held
-):
-    y_ref, base_ref, cross_base_ref, fwd_ref, inv_ref, filt_ref, other_ref = held[:7]
-    mf_ref, mi_ref, cross_ref, turn_ref, out_ref, sem = held[7:]
+def middle_kernel(y_ref, inner_hbm, bundle_hbm, peak_ref, wave_ref, out_hbm, buf, obuf, *held):
+    inner_ref, base_ref, cross_base_ref, filt_ref, other_ref = held[:5]
+    mf_ref, mi_ref, cross_ref, turn_ref, out_ref, sem = held[5:]
+    special = place_of() % (ND // 2) == 0
     blocks = [pl.ds(m * ROWS, ROWS) for m in range(STEPS)]
-    sources = {"base": (base_hbm, base_ref), "cross": (cross_base_hbm, cross_base_ref)}
-    for m, b in enumerate(blocks):
-        sources["y", m] = (y_hbm.at[b], y_ref.at[b])
-    sources["fwd"] = (fwd_hbm, fwd_ref)
-    for ri in range(2):
-        sources["filt", 0, ri] = (filt_hbm.at[0, ri], filt_ref.at[0, ri])
-    sources["inv"] = (inv_hbm, inv_ref)
-    for ri in range(2):
-        sources["filt", 1, ri] = (filt_hbm.at[1, ri], filt_ref.at[1, ri])
-    sources["filt", 2, 0] = (other_hbm, other_ref)
+    sources = {
+        "base": (bundle_hbm.at[14], base_ref),
+        "cross": (bundle_hbm.at[pl.ds(12, 2)], cross_base_ref),
+        "inner": (inner_hbm, inner_ref),
+    }
+    for r in range(2):
+        for ri in range(2):
+            sources["filt", r, ri] = (bundle_hbm.at[pl.ds(r * 4 + ri * 2, 2)], filt_ref.at[r, ri])
+    sources["filt", 2] = (bundle_hbm.at[pl.ds(8, 4)], other_ref)
     copies = {k: pltpu.make_async_copy(*v, sem.at[i]) for i, (k, v) in enumerate(sources.items())}
     waiting = set(copies)
 
@@ -306,16 +324,15 @@
     for copy in copies.values():
         copy.start()
     peak = peak_ref[0:1, 0:1]
-    tables = (mf_ref, mi_ref, cross_ref, turn_ref, fwd_ref, inv_ref)
+    tables = (mf_ref, mi_ref, cross_ref, turn_ref, inner_ref)
+    for m in range(STEPS):
+        y = decode(y_ref[blocks[m]].astype(f32), peak, FIELD_CODE).reshape(ROWS * 16, F)
+        for g in range(2):
+            buf[g, pl.ds(m * ROWS * 16, ROWS * 16), :] = y[:, g * 128 : (g + 1) * 128]
     arrive("base")
     arrive("cross")
     for r in range(2):
         fill_tables(r, base_ref, cross_base_ref, wave_ref, *tables[:4])
-    for m in range(STEPS):
-        arrive(("y", m))
-        y = decode(y_ref[blocks[m]].astype(f32), peak, FIELD_CODE).reshape(ROWS * 16, F)
-        for g in range(2):
-            buf[g, pl.ds(m * ROWS * 16, ROWS * 16), :] = y[:, g * 128 : (g + 1) * 128]
 
     def field(r, ri):
         return jnp.concatenate(
@@ -344,7 +361,7 @@
     for r in range(2):
         im = field(r, 1)
         if r == 0:
-            im = im * generic_ref[0]
+            im = im * jnp.where(special, 0.0, 1.0)
         running.append(transform(field(r, 0), im, r, *tables, filt_of(r), arrive))
     for stage in range(4):
         for r in range(2):
@@ -355,7 +372,7 @@
 
     arrive(("filt", 2))
 
-    @pl.when(generic_ref[0] < 0.5)
+    @pl.when(special)
     def _():
         fill_tables(2, base_ref, cross_base_ref, wave_ref, *tables[:4])
         *_, z = transform(
@@ -363,7 +380,7 @@
             None,
             2,
             *tables,
-            lambda ri, c, odd: other_ref[ri, c, :, odd * 128 : (odd + 1) * 128],
+            lambda ri, c, odd: other_ref[ri * 2 + c, :, odd * 128 : (odd + 1) * 128],
             arrive,
         )
         put(z, 0, 1, 0)
@@ -415,20 +432,19 @@
 
 
 VMEM = pl.BlockSpec(memory_space=pltpu.VMEM)
-SMEM = pl.BlockSpec(memory_space=pltpu.SMEM)
 ANY = pl.BlockSpec(memory_space=pl.ANY)
 
 
-def call(kernel, ins, outs, scratch, name, flops=0, limit=16, grid=(), in_specs=None, out_specs=None, scalars=0):
+def call(kernel, ins, outs, scratch, name, flops=0, limit=16, grid=(), in_specs=None, out_specs=None):
     size = sum(int(np.prod(x.shape)) * x.dtype.itemsize for x in (*ins, *outs))
     return pl.pallas_call(
         kernel,
         grid_spec=pltpu.PrefetchScalarGridSpec(
-            num_scalar_prefetch=scalars,
+            num_scalar_prefetch=0,
             grid=grid,
             in_specs=in_specs or [VMEM] * len(ins),
             out_specs=out_specs or [VMEM] * len(outs),
-            scratch_shapes=[d(s) if d is pltpu.SemaphoreType.DMA else pltpu.VMEM(s, d) for s, d in scratch],
+            scratch_shapes=[pltpu.VMEM(s, d) if s else d for s, d in scratch],
         ),
         out_shape=outs,
         compiler_params=pltpu.CompilerParams(vmem_limit_bytes=limit * 2**20),
@@ -446,28 +462,23 @@
 
 
 def per_device(signal, gate, skip, spectrum):
-    place = lax.axis_index("wide") * lax.axis_size("narrow") + lax.axis_index("narrow")
     (packed,) = call(pack_kernel, (signal,), [shape(ND, 4, 640)], [], "pack")
     spread = exchange(packed)
 
-    upper = (place >= ND // 2).astype(jnp.int32)
-    special = place % (ND // 2) == 0
-    generic = jnp.where(special, 0.0, 1.0).astype(f32)[None]
     plain, back = order_tables()
-    block = (2, 2, 2, F, F)
-    given = call(
-        give_kernel,
-        (jnp.stack([1 - upper, (place == 0).astype(jnp.int32)]), spectrum, jnp.asarray(np.stack([back, plain]))),
-        [shape(4, F, F)] * 2,
-        [],
-        "give",
-        limit=58,
-        flops=2**30,
-        grid=(1,),
-        in_specs=[pl.BlockSpec(block, lambda i, flag: (0, flag[0], 0, 0, 0)), VMEM],
-        out_specs=[pl.BlockSpec((4, F, F), lambda i, flag: (0, 0, 0))] * 2,
-        scalars=1,
-    )
+    held = [((2, 4, F, F), f32), (None, pltpu.SemaphoreType.DMA((2, 4)))]
+    given = []
+    for r, orders in enumerate(([back, plain], [back])):
+        given += call(
+            lambda *refs, r=r: give_kernel(r, *refs),
+            (jnp.asarray(np.stack(orders)), spectrum),
+            [shape(4, F, F)],
+            held,
+            "give",
+            limit=58,
+            flops=2**29,
+            in_specs=[VMEM, ANY],
+        )
     spread, *_ = lax.optimization_barrier((spread, *given))
     mirror = [(p, (ND // 2 - p) if p % (ND // 2) == 0 else ND - p) for p in range(ND)]
     got = [
@@ -475,13 +486,12 @@
         lax.ppermute(given[1], AXES, [(p, ND - 1 - p) for p in range(ND)]),
     ]
 
+    place = place_of()
     k1 = jnp.stack([place * 2, place * 2 + 1, ND - place * 2])[:, None] % F
     lane = jnp.arange(F, dtype=jnp.int32)
     turns = jnp.stack([k1 * lane % (F * ND) * (F * 2), k1 * lane, (k1 + F * lane) % (F * F) * F], axis=1)
     angle = (2 * np.pi / F**3) * turns.astype(f32)
     wave = jnp.stack([jnp.cos(angle), jnp.sin(angle)], axis=2).reshape(3, 6, F)
-    base, cross_base = (jnp.asarray(t) for t in base_tables())
-    inner_fwd, inner_inv = (jnp.asarray(t) for t in inner_tables())
 
     field, peak = call(
         outer_kernel,
@@ -495,36 +505,30 @@
         out_specs=[pl.BlockSpec((ROWS, 16, F), lambda i: (i, 0, 0)), pl.BlockSpec((8, 128), lambda i: (0, 0))],
     )
     field = exchange(field)
-    filt, other = call(
+    base, cross_base = (jnp.asarray(t) for t in base_tables())
+    (bundle,) = call(
         combine_kernel,
-        (upper[None], spectrum, jnp.asarray(plain), *got, generic),
-        [shape(2, 2, 2, F, F, dtype=f32), shape(2, 2, F, F, dtype=f32)],
-        [],
+        (spectrum, jnp.asarray(plain), cross_base, base, *got),
+        [shape(15, F, F, dtype=f32)],
+        held,
         "combine",
         limit=58,
         flops=2**34,
-        grid=(1,),
-        in_specs=[pl.BlockSpec(block, lambda i, half: (0, half[0], 0, 0, 0)), VMEM, VMEM, VMEM, SMEM],
-        out_specs=[
-            pl.BlockSpec((2, 2, 2, F, F), lambda i, half: (0, 0, 0, 0, 0)),
-            pl.BlockSpec((2, 2, F, F), lambda i, half: (0, 0, 0, 0)),
-        ],
-        scalars=1,
-    )
-    loads = (field, base, cross_base, inner_fwd, inner_inv, filt, other)
+        in_specs=[ANY] + [VMEM] * 5,
+    )
     (filtered,) = call(
         middle_kernel,
-        (*loads, peak, wave, generic),
+        (field, jnp.asarray(np.stack(inner_tables())), bundle, peak, wave),
         [shape(ND, 16, F)],
         [((2, ND * 16, 128), f32)] * 2
-        + [(x.shape, x.dtype) for x in loads]
+        + [((2, 2, 512, F), bf16), ((F, F), f32), ((2, F, F), f32), ((2, 2, 2, F, F), f32), ((4, F, F), f32)]
         + [((3, 256, 512), bf16)] * 2
         + [((3, 2, F, F), f32), ((3, 2, ND, ND), f32), ((ND, 16, F), bf16)]
-        + [((9 + 2 * STEPS,), pltpu.SemaphoreType.DMA)],
+        + [(None, pltpu.SemaphoreType.DMA((8 + STEPS,)))],
         "middle",
         flops=4 * 2**30,
-        limit=58,
-        in_specs=[ANY] * 7 + [VMEM, VMEM, SMEM],
+        limit=51,
+        in_specs=[VMEM, ANY, ANY, VMEM, VMEM],
         out_specs=[ANY],
     )
     filtered = exchange(filtered)

time: 131 us -> 126 us (0.962)
  waiting for transfers between devices: 37.1 us -> 28.1 us
  Pallas kernels: 31.6 us -> 33.8 us
  local copies, waits for them, and re-layouts: 4.39 us -> 2.26 us
  starting transfers between devices: 28.3 us -> 30.4 us
  blocking collectives: 28.4 us -> 29.9 us
    all_to_all x3, waiting for transfers between devices: 23.2 us -> 17.8 us  [exchange(): return lax.all_to_all(x, AXES, split_axis=0, concat_axis=0, tiled=True)]
    ppermute x1, waiting for transfers between devices: 2.86 us -> 0.01 us  [per_device(): lax.ppermute(given[0], AXES, mirror)]
    pallas_call x7 -> x8, Pallas kernels: 31.6 us -> 33.8 us  [call(): pl.pallas_call(kernel, grid_spec=pltpu.PrefetchScalarGridSpec(num_scalar_...]
    all_to_all x3, starting transfers between devices: 20.3 us -> 22.3 us  [exchange(): return lax.all_to_all(x, AXES, split_axis=0, concat_axis=0, tiled=True)]
    unnamed x22 -> x16, local copies, waits for them, and re-layouts: 3.42 us -> 1.9 us
    all_to_all x1, blocking collectives: 28.4 us -> 29.9 us  [exchange(): return lax.all_to_all(x, AXES, split_axis=0, concat_axis=0, tiled=True)]
  transfers between devices with their start and end apart: 5 -> 5, of which waited for: 5 -> 4; matrix products, arithmetic and copies ran while one was open for 2% -> 1% of each run, Pallas kernels for 10% -> 14%
where the time goes in v5:
time: 126 us; the launch traced here: 125 us
  Pallas kernels  33.8 us (27%)
  starting transfers between devices  30.4 us (24%)
  blocking collectives  29.9 us (24%)
  waiting for transfers between devices  28.1 us (22%)
  local copies, waits for them, and re-layouts  2.26 us (2%)
    pallas_call x8, Pallas kernels, call(): pl.pallas_call(kernel, grid_spec=pltpu.PrefetchScalarGridSpec(num_scalar_...  33.8 us
    all_to_all x1, blocking collectives, exchange(): return lax.all_to_all(x, AXES, split_axis=0, concat_axis=0, tiled=True)  29.9 us
    all_to_all x3, starting transfers between devices, exchange(): return lax.all_to_all(x, AXES, split_axis=0, concat_axis=0, tiled=True)  22.3 us
    all_to_all x3, waiting for transfers between devices, exchange(): return lax.all_to_all(x, AXES, split_axis=0, concat_axis=0, tiled=True)  17.8 us
    ppermute x1, waiting for transfers between devices, per_device(): lax.ppermute(given[1], AXES, [(p, ND - 1 - p) for p in range(ND)])  10.3 us
    ppermute x1, starting transfers between devices, per_device(): lax.ppermute(given[0], AXES, mirror)  4.25 us
    ppermute x1, starting transfers between devices, per_device(): lax.ppermute(given[1], AXES, [(p, ND - 1 - p) for p in range(ND)])  3.9 us
  transfers between devices with their start and end apart: 5, of which 4 were waited for; matrix products, arithmetic and copies ran while one was open for 1% of the time, Pallas kernels for 14%

profile of v5, /device:TPU:1, one launch (start us, length us, event | category | flops | bytes accessed | tf_op | source)
XLA Modules:
  0.0 125.1 jit_solution(2200137434336426188)
XLA Ops:
  0.0 0.0 copy-start
  0.0 1.0 copy-done
  1.0 1.4 %pack.1 = bf16[128,4,640]{2,1,0:T(4,128)(2,1)} custom-call(bf16[4,65536]{1,0:T(4,128)(2,1)S(1)} %copy-done), custom_call_target="tpu_custom_call" | custom-call | bytes 1179648 | tf_op jit(solution)/shard_map/pack/pallas_call | solution.py:440
  2.5 11.5 %all-to-all-start = ((bf16[128,4,640]{2,1,0:T(4,128)(2,1)}), bf16[128,4,640]{2,1,0:T(4,128)(2,1)S(1)}, u32[]{:S(2)}, u32[]{:S(2)}) async-start(bf16[128,4,640]{2,1,0:T(4,128)(2,1)} %pack.1), calls=%async_computation | async-start | bytes 1310720 | tf_op jit(solution)/shard_map/all_to_all | solution.py:457
  14.0 0.0 copy-start.4
  14.0 4.2 %give.2 = bf16[4,256,256]{2,1,0:T(8,128)(2,1)} custom-call(bf16[2,2,256,256]{3,2,1,0:T(8,128)(2,1)} %constant.79.clone.refs_0_, f32[2,4,2,256,256]{4,3,2,1,0:T(8,128)} %filt_hbm.1), custom_call_target="tpu_custom_call" | custom-call | flops 536870912 | bytes 5242880 | tf_op jit(solution)/shard_map/give/pallas_call | solution.py:440
  18.2 4.3 %collective-permute-start = (bf16[4,256,256]{2,1,0:T(8,128)(2,1)}, bf16[4,256,256]{2,1,0:T(8,128)(2,1)S(1)}, u32[]{:S(2)}, u32[]{:S(2)}) collective-permute-start(bf16[4,256,256]{2,1,0:T(8,128)(2,1)} %give.2), channel_id=1, source_target_pairs={{0,64},{1,127},{2,126},{3,125},{4,124},{5,123},{6,122},{7,121},{8,... | collective-permute-start | bytes 1572872 | tf_op jit(solution)/shard_map/ppermute | solution.py:485
  22.4 4.0 %give.3 = bf16[4,256,256]{2,1,0:T(8,128)(2,1)} custom-call(bf16[1,2,256,256]{3,2,1,0:T(8,128)(2,1)} %constant.80.clone.refs_0_, f32[2,4,2,256,256]{4,3,2,1,0:T(8,128)} %filt_hbm.1), custom_call_target="tpu_custom_call" | custom-call | flops 536870912 | bytes 4980736 | tf_op jit(solution)/shard_map/give/pallas_call | solution.py:440
  26.4 3.9 %collective-permute-start.1 = (bf16[4,256,256]{2,1,0:T(8,128)(2,1)}, bf16[4,256,256]{2,1,0:T(8,128)(2,1)S(1)}, u32[]{:S(2)}, u32[]{:S(2)}) collective-permute-start(bf16[4,256,256]{2,1,0:T(8,128)(2,1)} %give.3), channel_id=1, source_target_pairs={{0,127},{1,126},{2,125},{3,124},{4,123},{5,122},{6,121},{7,120},{8... | collective-permute-start | bytes 1572872 | tf_op jit(solution)/shard_map/ppermute | solution.py:486
  30.3 0.1 and_select_fusion.2
  30.4 0.1 fusion.5
  30.5 0.3 fusion.9
  30.8 0.2 sin.10
  31.1 0.2 all-to-all-done.x_ref
  31.2 0.0 copy-done.4
  31.2 3.3 %outer.1 = (bf16[128,16,256]{2,1,0:T(8,128)(2,1)}, f32[8,128]{1,0:T(8,128)S(1)}) custom-call(bf16[128,4,640]{2,1,0:T(4,128)(2,1)S(1)} %all-to-all-done.x_ref, bf16[1024,512]{1,0:T(8,128)(2,1)S(1)} %copy-done.4), custom_call_target="tpu_custom_call" | custom-call | flops 536870912 | bytes 2756608 | tf_op jit(solution)/shard_map/outer/pallas_call | solution.py:440
  34.5 6.8 %all-to-all-start.1 = ((bf16[128,16,256]{2,1,0:T(8,128)(2,1)}), bf16[128,16,256]{2,1,0:T(8,128)(2,1)S(1)}, u32[]{:S(2)}, u32[]{:S(2)}) async-start(bf16[128,16,256]{2,1,0:T(8,128)(2,1)} %get-tuple-element.9), calls=%async_computation.1 | async-start | bytes 2097152 | tf_op jit(solution)/shard_map/all_to_all | solution.py:457
  41.3 0.0 collective-permute-done.got0_ref
  41.3 0.0 copy-start.6
  41.3 10.3 %collective-permute-done.1.got1_ref = bf16[4,256,256]{2,1,0:T(8,128)(2,1)S(1)} collective-permute-done((bf16[4,256,256]{2,1,0:T(8,128)(2,1)}, bf16[4,256,256]{2,1,0:T(8,128)(2,1)S(1)}, u32[]{:S(2)}, u32[]{:S(2)}) %collective-permute-start.1) | collective-permute-done | bytes 524320 | tf_op jit(solution)/shard_map/ppermute | solution.py:486
  51.6 0.0 copy-done.6
  51.6 0.0 copy-start.7
  51.6 0.8 copy-done.7
  52.5 6.1 %combine.1.bundle_hbm = f32[15,256,256]{2,1,0:T(8,128)} custom-call(f32[2,4,2,256,256]{4,3,2,1,0:T(8,128)} %filt_hbm.1, bf16[2,256,256]{2,1,0:T(8,128)(2,1)} %constant.84.clone.order_ref, f32[2,256,256]{2,1,0:T(8,128)} %constant.83.clone.cross_base_ref, f32[2,128,128]{2,1,0:T(8,128)} %constant.82.clone.base_ref, bf16[4,256,256]{2,1,0:T(8,128)(2,1)} %copy-done.6, ...), custom_call_target="tpu_custom_call" | custom-call | flops 17179869184 | bytes 10092544 | tf_op jit(solution)/shard_map/combine/pallas_call | solution.py:440
  58.5 3.7 %all-to-all-done.1.y_ref = bf16[128,16,256]{2,1,0:T(8,128)(2,1)S(1)} async-done(((bf16[128,16,256]{2,1,0:T(8,128)(2,1)}), bf16[128,16,256]{2,1,0:T(8,128)(2,1)S(1)}, u32[]{:S(2)}, u32[]{:S(2)}) %all-to-all-start.1) | async-done | bytes 1048608 | tf_op jit(solution)/shard_map/all_to_all | solution.py:457
  62.2 0.0 copy-start.2
  62.2 8.3 %middle.1 = bf16[128,16,256]{2,1,0:T(8,128)(2,1)S(1)} custom-call(bf16[128,16,256]{2,1,0:T(8,128)(2,1)S(1)} %all-to-all-done.1.y_ref, bf16[2,2,512,256]{3,2,1,0:T(8,128)(2,1)} %constant.85.clone.inner_hbm, f32[15,256,256]{2,1,0:T(8,128)} %combine.1.bundle_hbm, f32[8,128]{1,0:T(8,128)S(1)} %get-tuple-element.10.peak_ref, f32[3,6,256]{2,1,0:T(8,128)S(1)} %reshape.294.wave_ref), custom_call_target="tpu_custom_call" | custom-call | flops 4294967296 | bytes 7100416 | tf_op jit(solution)/shard_map/middle/pallas_call | solution.py:440
  70.6 0.0 copy-start.5
  70.6 0.0 copy-start.1
  70.6 0.0 copy-start.3
  70.6 29.9 %all_to_all.20.y_ref = bf16[128,16,256]{2,1,0:T(8,128)(2,1)S(1)} all-to-all(bf16[128,16,256]{2,1,0:T(8,128)(2,1)S(1)} %middle.1), channel_id=1, replica_groups=mesh['wide'=16,'narrow'=8] {'wide','narrow'}, dimensions={0} | all-to-all | bytes 2097152 | tf_op jit(solution)/shard_map/all_to_all | solution.py:457
  100.4 0.0 copy-done.2
  100.4 4.6 %last.1 = bf16[128,16,128]{2,1,0:T(8,128)(2,1)} custom-call(bf16[128,16,256]{2,1,0:T(8,128)(2,1)S(1)} %all_to_all.20.y_ref, bf16[4,256,768]{2,1,0:T(8,128)(2,1)S(1)} %copy-done.2, f32[8,128]{1,0:T(8,128)S(1)} %get-tuple-element.10.peak_ref), custom_call_target="tpu_custom_call" | custom-call | flops 536870912 | bytes 3149824 | tf_op jit(solution)/shard_map/last/pallas_call | solution.py:440
  105.0 4.0 %all-to-all-start.3 = ((bf16[128,16,128]{2,1,0:T(8,128)(2,1)}), bf16[128,16,128]{2,1,0:T(8,128)(2,1)S(1)}, u32[]{:S(2)}, u32[]{:S(2)}) async-start(bf16[128,16,128]{2,1,0:T(8,128)(2,1)} %last.1), calls=%async_computation.3 | async-start | bytes 1048576 | tf_op jit(solution)/shard_map/all_to_all | solution.py:457
  109.0 0.0 copy-done.5
  109.0 0.1 copy.15.skip_ref
  109.1 13.9 %all-to-all-done.3.y_ref = bf16[128,16,128]{2,1,0:T(8,128)(2,1)S(1)} async-done(((bf16[128,16,128]{2,1,0:T(8,128)(2,1)}), bf16[128,16,128]{2,1,0:T(8,128)(2,1)S(1)}, u32[]{:S(2)}, u32[]{:S(2)}) %all-to-all-start.3) | async-done | bytes 524320 | tf_op jit(solution)/shard_map/all_to_all | solution.py:457
  123.1 0.0 copy-done.1
  123.1 0.0 copy-done.3
  123.1 2.0 %finish.1 = bf16[4,65536]{1,0:T(4,128)(2,1)} custom-call(bf16[128,16,128]{2,1,0:T(8,128)(2,1)S(1)} %all-to-all-done.3.y_ref, bf16[4,65536]{1,0:T(4,128)(2,1)S(1)} %copy-done.1, bf16[4,65536]{1,0:T(4,128)(2,1)S(1)} %copy-done.3, f32[4,1]{1,0:T(4,128)S(1)} %copy.15.skip_ref, f32[8,128]{1,0:T(8,128)S(1)} %get-tuple-element.10.peak_ref), custom_call_target="tpu_custom_call" | custom-call | bytes 2101264 | tf_op jit(solution)/shard_map/finish/pallas_call | solution.py:440
  (3 shorter events, 0.0 us)
Async XLA Ops:
  0.0 1.0 copy-start
  2.5 28.8 %all-to-all-start = ((bf16[128,4,640]{2,1,0:T(4,128)(2,1)}), bf16[128,4,640]{2,1,0:T(4,128)(2,1)S(1)}, u32[]{:S(2)}, u32[]{:S(2)}) async-start(bf16[128,4,640]{2,1,0:T(4,128)(2,1)} %pack.1), calls=%async_computation | async-start | bytes 1310720 | tf_op jit(solution)/shard_map/all_to_all | solution.py:457
  14.0 17.3 %copy-start.4 = (bf16[1024,512]{1,0:T(8,128)(2,1)S(1)}, bf16[1024,512]{1,0:T(8,128)(2,1)}, u32[]{:S(2)}) copy-start(bf16[1024,512]{1,0:T(8,128)(2,1)} %constant.81.clone.table_ref) | copy-start | bytes 3145732
  18.2 23.1 %collective-permute-start = (bf16[4,256,256]{2,1,0:T(8,128)(2,1)}, bf16[4,256,256]{2,1,0:T(8,128)(2,1)S(1)}, u32[]{:S(2)}, u32[]{:S(2)}) collective-permute-start(bf16[4,256,256]{2,1,0:T(8,128)(2,1)} %give.2), channel_id=1, source_target_pairs={{0,64},{1,127},{2,126},{3,125},{4,124},{5,123},{6,122},{7,121},{8,... | collective-permute-start | bytes 1572872 | tf_op jit(solution)/shard_map/ppermute | solution.py:485
  26.4 25.2 %collective-permute-start.1 = (bf16[4,256,256]{2,1,0:T(8,128)(2,1)}, bf16[4,256,256]{2,1,0:T(8,128)(2,1)S(1)}, u32[]{:S(2)}, u32[]{:S(2)}) collective-permute-start(bf16[4,256,256]{2,1,0:T(8,128)(2,1)} %give.3), channel_id=1, source_target_pairs={{0,127},{1,126},{2,125},{3,124},{4,123},{5,122},{6,121},{7,120},{8... | collective-permute-start | bytes 1572872 | tf_op jit(solution)/shard_map/ppermute | solution.py:486
  34.5 27.7 %all-to-all-start.1 = ((bf16[128,16,256]{2,1,0:T(8,128)(2,1)}), bf16[128,16,256]{2,1,0:T(8,128)(2,1)S(1)}, u32[]{:S(2)}, u32[]{:S(2)}) async-start(bf16[128,16,256]{2,1,0:T(8,128)(2,1)} %get-tuple-element.9), calls=%async_computation.1 | async-start | bytes 2097152 | tf_op jit(solution)/shard_map/all_to_all | solution.py:457
  41.3 10.4 %copy-start.6 = (bf16[4,256,256]{2,1,0:T(8,128)(2,1)}, bf16[4,256,256]{2,1,0:T(8,128)(2,1)S(1)}, u32[]{:S(2)}) copy-start(bf16[4,256,256]{2,1,0:T(8,128)(2,1)S(1)} %collective-permute-done.got0_ref) | copy-start | bytes 1572868
  51.6 0.8 copy-start.7
  62.2 38.2 %copy-start.2 = (bf16[4,256,768]{2,1,0:T(8,128)(2,1)S(1)}, bf16[4,256,768]{2,1,0:T(8,128)(2,1)}, u32[]{:S(2)}) copy-start(bf16[4,256,768]{2,1,0:T(8,128)(2,1)} %constant.86.clone.table_ref) | copy-start | bytes 4718596
  70.6 38.5 %copy-start.5 = (f32[4]{0:T(128)S(1)}, f32[4]{0:T(128)}, u32[]{:S(2)}) copy-start(f32[4]{0:T(128)} %param.14) | copy-start | bytes 52
  70.6 52.5 %copy-start.1 = (bf16[4,65536]{1,0:T(4,128)(2,1)S(1)}, bf16[4,65536]{1,0:T(4,128)(2,1)}, u32[]{:S(2)}) copy-start(bf16[4,65536]{1,0:T(4,128)(2,1)} %sig_ref.3) | copy-start | bytes 1572868
  70.6 52.5 %copy-start.3 = (bf16[4,65536]{1,0:T(4,128)(2,1)S(1)}, bf16[4,65536]{1,0:T(4,128)(2,1)}, u32[]{:S(2)}) copy-start(bf16[4,65536]{1,0:T(4,128)(2,1)} %gate_ref.1) | copy-start | bytes 1572868
  105.0 18.0 %all-to-all-start.3 = ((bf16[128,16,128]{2,1,0:T(8,128)(2,1)}), bf16[128,16,128]{2,1,0:T(8,128)(2,1)S(1)}, u32[]{:S(2)}, u32[]{:S(2)}) async-start(bf16[128,16,128]{2,1,0:T(8,128)(2,1)} %last.1), calls=%async_computation.3 | async-start | bytes 1048576 | tf_op jit(solution)/shard_map/all_to_all | solution.py:457

commit v6 on v5

--- a/solution.py
+++ b/solution.py
@@ -132,37 +132,68 @@
     return jnp.concatenate([hi, hi, lo], axis=axis)
 
 
-def pack_kernel(sig_ref, out_ref):
+def block(m):
+    return pl.ds(m * ROWS, ROWS)
+
+
+def send_block(out_ref, out_hbm, sem, m):
+    copy = pltpu.make_async_copy(out_ref.at[block(m)], out_hbm.at[block(m)], sem.at[m])
+    copy.start()
+    return copy
+
+
+def pack_kernel(sig_hbm, out_hbm, held, out_ref, sem):
+    reads = []
+    for m in range(STEPS):
+        at = pl.ds(m * ROWS * 512, ROWS * 512)
+        reads.append(pltpu.make_async_copy(sig_hbm.at[:, at], held.at[:, at], sem.at[m]))
+        reads[-1].start()
+    writes = []
     top = jnp.zeros((4, 128), f32)
-    for q in range(ND):
-        x = sig_ref[:, pl.ds(q * 512, 512)]
-        out_ref[q, :, pl.ds(0, 512)] = x
-        x = jnp.abs(x.astype(f32))
-        for i in range(4):
-            top = jnp.maximum(top, x[:, i * 128 : (i + 1) * 128])
+    for m in range(STEPS):
+        reads[m].wait()
+        for q in range(m * ROWS, (m + 1) * ROWS):
+            x = held[:, pl.ds(q * 512, 512)]
+            out_ref[q, :, pl.ds(0, 512)] = x
+            x = jnp.abs(x.astype(f32))
+            for i in range(4):
+                top = jnp.maximum(top, x[:, i * 128 : (i + 1) * 128])
+        at = (block(m), slice(None), pl.ds(0, 512))
+        writes.append(pltpu.make_async_copy(out_ref.at[at], out_hbm.at[at], sem.at[STEPS + m]))
+        writes[-1].start()
     top = top.astype(bf16)
     for q in range(ND):
         out_ref[q, :, pl.ds(512, 128)] = top
-
-
-def outer_kernel(x_ref, table_ref, out_ref, peak_ref, buf, xs):
-    @pl.when(pl.program_id(0) == 0)
-    def _():
-        top = jnp.zeros((4, 128), f32)
-        for n in range(ND):
-            x = x_ref[n].astype(f32)
-            top = jnp.maximum(top, x[:, 512:640])
-            for i in range(4):
-                buf[i, pl.ds(n * 8, 4), :] = x[:, i * 128 : (i + 1) * 128]
-        peak_ref[...] = jnp.broadcast_to(jnp.maximum(jnp.max(top, keepdims=True), 1e-30), (8, 128))
-        for c in range(4):
-            parts = [buf[i, pl.ds(c, ND, stride=8), :] for i in range(4)]
-            xs[pl.ds(c * ND, ND), :] = jnp.concatenate(parts, axis=1).astype(bf16)
-
-    x = xs[pl.ds(pl.program_id(0) // (STEPS // 2) * 256, 256), :]
-    res = encode(dot(table_ref[...], jnp.concatenate([x, x], axis=0)), peak_ref[0:1, 0:1], FIELD_CODE)
-    parts = [res[:, h * F : (h + 1) * F].reshape(ROWS, 8, F) for h in range(2)]
-    out_ref[...] = jnp.concatenate(parts, axis=1).astype(bf16)
+    at = (slice(None), slice(None), pl.ds(512, 128))
+    writes.append(pltpu.make_async_copy(out_ref.at[at], out_hbm.at[at], sem.at[2 * STEPS]))
+    writes[-1].start()
+    for copy in writes:
+        copy.wait()
+
+
+def outer_kernel(x_ref, table_ref, out_hbm, peak_ref, buf, out_ref, sem):
+    top = jnp.zeros((4, 128), f32)
+    for n in range(ND):
+        x = x_ref[n].astype(f32)
+        top = jnp.maximum(top, x[:, 512:640])
+        for i in range(4):
+            buf[i, pl.ds(n * 8, 4), :] = x[:, i * 128 : (i + 1) * 128]
+    peak = jnp.maximum(jnp.max(top, keepdims=True), 1e-30)
+    peak_ref[...] = jnp.broadcast_to(peak, (8, 128))
+    writes = []
+    for pair in range(2):
+        rows = []
+        for c in range(2):
+            parts = [buf[i, pl.ds(pair * 2 + c, ND, stride=8), :] for i in range(4)]
+            rows.append(jnp.concatenate(parts, axis=1).astype(bf16))
+        x = jnp.concatenate(rows + rows, axis=0)
+        for m in range(pair * STEPS // 2, (pair + 1) * STEPS // 2):
+            res = encode(dot(table_ref[pl.ds(m * ROWS * 8, ROWS * 8), :], x), peak, FIELD_CODE)
+            parts = [res[:, h * F : (h + 1) * F].reshape(ROWS, 8, F) for h in range(2)]
+            out_ref[block(m)] = jnp.concatenate(parts, axis=1).astype(bf16)
+            writes.append(send_block(out_ref, out_hbm, sem, m))
+    for copy in writes:
+        copy.wait()
 
 
 def fill_tables(table, base_ref, cross_base_ref, wave_ref, mf_ref, mi_ref, cross_ref, turn_ref):
@@ -192,35 +223,43 @@
     return lax.axis_index("wide") * lax.axis_size("narrow") + lax.axis_index("narrow")
 
 
-def fetch_filter(r, pair, filt_hbm, held, sem):
+def fetch_filter(slot, r, pair, filt_hbm, held, sem):
     copies = []
     for i in range(4):
         source = filt_hbm.at[i // 2, pair * 2 + i % 2, r]
-        copies.append(pltpu.make_async_copy(source, held.at[r, i], sem.at[r, i]))
+        copies.append(pltpu.make_async_copy(source, held.at[slot, i], sem.at[slot, i]))
         copies[-1].start()
     return copies
 
 
-def give_kernel(r, order_ref, filt_hbm, out_ref, held, sem):
+def give_kernel(r, order_hbm, filt_hbm, out_hbm, held, order_ref, out_ref, sem, more):
     place = place_of()
-    copies = fetch_filter(r, 1 - place // (ND // 2), filt_hbm, held, sem)
     kind = jnp.where(place == 0, 1, 0) if r == 0 else 0
-    left, right = order_ref[kind, 0], order_ref[kind, 1]
+    order = pltpu.make_async_copy(order_hbm.at[kind], order_ref, more.at[4])
+    order.start()
+    copies = fetch_filter(0, r, 1 - place // (ND // 2), filt_hbm, held, sem)
     sign = (2 * kind - 1) * jnp.float32(1.0)
+    order.wait()
     for copy in copies:
         copy.wait()
+    left, right = order_ref[0], order_ref[1]
+    writes = []
     for i in range(4):
-        hi, lo = split(held[r, i])
+        hi, lo = split(held[0, i])
         hi, lo = split(dot(hi, right) + dot(lo, right))
         x = dot(left, hi) + dot(left, lo)
         if i >= 2:
             x = x * sign
         out_ref[i] = encode_filter(x).astype(bf16)
+        writes.append(pltpu.make_async_copy(out_ref.at[i], out_hbm.at[i], more.at[i]))
+        writes[-1].start()
+    for copy in writes:
+        copy.wait()
 
 
 def combine_kernel(filt_hbm, order_ref, cross_base_ref, base_ref, got0_ref, got1_ref, out_ref, held, sem):
     place = place_of()
-    copies = [fetch_filter(r, place // (ND // 2), filt_hbm, held, sem) for r in range(2)]
+    copies = [fetch_filter(r, r, place // (ND // 2), filt_hbm, held, sem) for r in range(2)]
     generic = jnp.where(place % (ND // 2) == 0, 0.0, 1.0)
     out_ref[12:14] = cross_base_ref[...]
     out_ref[14, 0:128, 0:128] = base_ref[0]
@@ -395,29 +434,29 @@
         copy.wait()
 
 
-def last_kernel(y_ref, table_ref, peak_ref, out_ref, acc, buf):
+def last_kernel(y_ref, table_ref, peak_ref, out_hbm, buf, out_ref, sem):
     peak = peak_ref[0:1, 0:1]
-    step = pl.program_id(0)
-
-    y = decode(y_ref[...].astype(f32), peak, FILTERED_CODE)
-    t = table_ref[0]
-    pair = step // (STEPS // 2)
-    first = step % (STEPS // 2) == 0
-    for h in range(2):
-        hi, lo = split(y[:, h * 8 : h * 8 + 8, :].reshape(ROWS * 8, F))
-        res = dot(t, twice(hi, lo, 0))
-        acc[pair, h] = jnp.where(first, res, acc[pair, h] + res)
-
-    @pl.when(step == STEPS - 1)
-    def _():
-        for pair in range(2):
+    for pair in range(2):
+        acc = [None, None]
+        for step in range(pair * STEPS // 2, (pair + 1) * STEPS // 2):
+            y = decode(y_ref[block(step)].astype(f32), peak, FILTERED_CODE)
             for h in range(2):
-                for c in range(2):
-                    for g in range(2):
-                        buf[pl.ds(h * 8 + g * 4 + pair * 2 + c, ND, stride=16), :] = acc[
-                            pair, h, c * ND : (c + 1) * ND, g * 128 : (g + 1) * 128
-                        ]
-        out_ref[...] = encode(buf[...], peak, CONV_CODE).reshape(ND, 16, 128).astype(bf16)
+                hi, lo = split(y[:, h * 8 : h * 8 + 8, :].reshape(ROWS * 8, F))
+                res = dot(table_ref[step], twice(hi, lo, 0))
+                acc[h] = res if acc[h] is None else acc[h] + res
+        for h in range(2):
+            for c in range(2):
+                for g in range(2):
+                    buf[pl.ds(h * 8 + g * 4 + pair * 2 + c, ND, stride=16), :] = acc[h][
+                        c * ND : (c + 1) * ND, g * 128 : (g + 1) * 128
+                    ]
+    writes = []
+    for m in range(STEPS):
+        y = encode(buf[pl.ds(m * ROWS * 16, ROWS * 16), :], peak, CONV_CODE)
+        out_ref[block(m)] = y.reshape(ROWS, 16, 128).astype(bf16)
+        writes.append(send_block(out_ref, out_hbm, sem, m))
+    for copy in writes:
+        copy.wait()
 
 
 def finish_kernel(y_ref, sig_ref, gate_ref, skip_ref, peak_ref, out_ref, buf):
@@ -462,7 +501,16 @@
 
 
 def per_device(signal, gate, skip, spectrum):
-    (packed,) = call(pack_kernel, (signal,), [shape(ND, 4, 640)], [], "pack")
+    (packed,) = call(
+        pack_kernel,
+        (signal,),
+        [shape(ND, 4, 640)],
+        [(signal.shape, bf16), ((ND, 4, 640), bf16), (None, pltpu.SemaphoreType.DMA((2 * STEPS + 1,)))],
+        "pack",
+        limit=58,
+        in_specs=[ANY],
+        out_specs=[ANY],
+    )
     spread = exchange(packed)
 
     plain, back = order_tables()
@@ -473,11 +521,13 @@
             lambda *refs, r=r: give_kernel(r, *refs),
             (jnp.asarray(np.stack(orders)), spectrum),
             [shape(4, F, F)],
-            held,
+            [((1, 4, F, F), f32), ((2, F, F), bf16), ((4, F, F), bf16)]
+            + [(None, pltpu.SemaphoreType.DMA((1, 4))), (None, pltpu.SemaphoreType.DMA((5,)))],
             "give",
             limit=58,
             flops=2**29,
-            in_specs=[VMEM, ANY],
+            in_specs=[ANY, ANY],
+            out_specs=[ANY],
         )
     spread, *_ = lax.optimization_barrier((spread, *given))
     mirror = [(p, (ND // 2 - p) if p % (ND // 2) == 0 else ND - p) for p in range(ND)]
@@ -497,12 +547,10 @@
         outer_kernel,
         (spread, jnp.asarray(outer_forward_table())),
         [shape(ND, 16, F), shape(8, 128, dtype=f32)],
-        [((4, ND * 8, 128), f32), ((ND * 4, 512), bf16)],
+        [((4, ND * 8, 128), f32), ((ND, 16, F), bf16), (None, pltpu.SemaphoreType.DMA((STEPS,)))],
         "outer",
         flops=2**29,
-        grid=(STEPS,),
-        in_specs=[VMEM, pl.BlockSpec((ROWS * 8, 512), lambda i: (i, 0))],
-        out_specs=[pl.BlockSpec((ROWS, 16, F), lambda i: (i, 0, 0)), pl.BlockSpec((8, 128), lambda i: (0, 0))],
+        out_specs=[ANY, VMEM],
     )
     field = exchange(field)
     base, cross_base = (jnp.asarray(t) for t in base_tables())
@@ -536,16 +584,10 @@
         last_kernel,
         (filtered, jnp.asarray(outer_inverse_table()), peak),
         [shape(ND, 16, 128)],
-        [((2, 2, 2 * ND, F), f32), ((ND * 16, 128), f32)],
+        [((ND * 16, 128), f32), ((ND, 16, 128), bf16), (None, pltpu.SemaphoreType.DMA((STEPS,)))],
         "last",
         flops=2**29,
-        grid=(STEPS,),
-        in_specs=[
-            pl.BlockSpec((ROWS, 16, F), lambda i: (i, 0, 0)),
-            pl.BlockSpec((1, 2 * ND, ROWS * 24), lambda i: (i, 0, 0)),
-            VMEM,
-        ],
-        out_specs=[VMEM],
+        out_specs=[ANY],
     )
     conv = exchange(conv)
     (mixed,) = call(

time: 126 us -> 122 us (0.968)
  waiting for transfers between devices: 28.1 us -> 32.9 us
  Pallas kernels: 33.8 us -> 30.1 us
  starting transfers between devices: 30.4 us -> 28.3 us
    pallas_call x8, Pallas kernels: 33.8 us -> 30.1 us  [call(): pl.pallas_call(kernel, grid_spec=pltpu.PrefetchScalarGridSpec(num_scalar_...]
    ppermute x1, waiting for transfers between devices: 0.01 us -> 3.37 us  [per_device(): lax.ppermute(given[0], AXES, mirror)]
    ppermute x1, waiting for transfers between devices: 10.3 us -> 13.2 us  [per_device(): lax.ppermute(given[1], AXES, [(p, ND - 1 - p) for p in range(ND)])]
    all_to_all x3, starting transfers between devices: 22.3 us -> 20.2 us  [exchange(): return lax.all_to_all(x, AXES, split_axis=0, concat_axis=0, tiled=True)]
    all_to_all x3, waiting for transfers between devices: 17.8 us -> 16.4 us  [exchange(): return lax.all_to_all(x, AXES, split_axis=0, concat_axis=0, tiled=True)]
  transfers between devices with their start and end apart: 5 -> 5, of which waited for: 4 -> 5; matrix products, arithmetic and copies ran while one was open for 1% -> 1% of each run, Pallas kernels for 14% -> 12%
where the time goes in v6:
time: 122 us
  waiting for transfers between devices  32.9 us (27%)
  Pallas kernels  30.1 us (25%)
  blocking collectives  28.7 us (24%)
  starting transfers between devices  28.3 us (23%)
    pallas_call x8, Pallas kernels, call(): pl.pallas_call(kernel, grid_spec=pltpu.PrefetchScalarGridSpec(num_scalar_...  30.1 us
    all_to_all x1, blocking collectives, exchange(): return lax.all_to_all(x, AXES, split_axis=0, concat_axis=0, tiled=True)  28.7 us
    all_to_all x3, starting transfers between devices, exchange(): return lax.all_to_all(x, AXES, split_axis=0, concat_axis=0, tiled=True)  20.2 us
    all_to_all x3, waiting for transfers between devices, exchange(): return lax.all_to_all(x, AXES, split_axis=0, concat_axis=0, tiled=True)  16.4 us
    ppermute x1, waiting for transfers between devices, per_device(): lax.ppermute(given[1], AXES, [(p, ND - 1 - p) for p in range(ND)])  13.2 us
    ppermute x1, starting transfers between devices, per_device(): lax.ppermute(given[0], AXES, mirror)  4.25 us
    ppermute x1, starting transfers between devices, per_device(): lax.ppermute(given[1], AXES, [(p, ND - 1 - p) for p in range(ND)])  3.9 us
    ppermute x1, waiting for transfers between devices, per_device(): lax.ppermute(given[0], AXES, mirror)  3.37 us
  transfers between devices with their start and end apart: 5, of which 5 were waited for; matrix products, arithmetic and copies ran while one was open for 1% of the time, Pallas kernels for 12%

profile of v6, /device:TPU:1, one launch (start us, length us, event | category | flops | bytes accessed | tf_op | source)
XLA Modules:
  0.0 121.9 jit_solution(8162524274694072222)
XLA Ops:
  0.0 2.2 %pack.1 = bf16[128,4,640]{2,1,0:T(4,128)(2,1)} custom-call(bf16[4,65536]{1,0:T(4,128)(2,1)} %sig_ref.1), custom_call_target="tpu_custom_call" | custom-call | bytes 1179648 | tf_op jit(solution)/shard_map/pack/pallas_call | solution.py:479
  2.2 11.5 %all-to-all-start = ((bf16[128,4,640]{2,1,0:T(4,128)(2,1)}), bf16[128,4,640]{2,1,0:T(4,128)(2,1)S(1)}, u32[]{:S(2)}, u32[]{:S(2)}) async-start(bf16[128,4,640]{2,1,0:T(4,128)(2,1)} %pack.1), calls=%async_computation | async-start | bytes 1310720 | tf_op jit(solution)/shard_map/all_to_all | solution.py:496
  13.8 0.0 copy-start.3
  13.8 3.1 %give.2 = bf16[4,256,256]{2,1,0:T(8,128)(2,1)} custom-call(bf16[2,2,256,256]{3,2,1,0:T(8,128)(2,1)} %constant.79.clone.refs_0_, f32[2,4,2,256,256]{4,3,2,1,0:T(8,128)} %filt_hbm.1), custom_call_target="tpu_custom_call" | custom-call | flops 536870912 | bytes 5242880 | tf_op jit(solution)/shard_map/give/pallas_call | solution.py:479
  16.9 4.3 %collective-permute-start = (bf16[4,256,256]{2,1,0:T(8,128)(2,1)}, bf16[4,256,256]{2,1,0:T(8,128)(2,1)S(1)}, u32[]{:S(2)}, u32[]{:S(2)}) collective-permute-start(bf16[4,256,256]{2,1,0:T(8,128)(2,1)} %give.2), channel_id=1, source_target_pairs={{0,64},{1,127},{2,126},{3,125},{4,124},{5,123},{6,122},{7,121},{8,... | collective-permute-start | bytes 1572872 | tf_op jit(solution)/shard_map/ppermute | solution.py:535
  21.1 3.0 %give.3 = bf16[4,256,256]{2,1,0:T(8,128)(2,1)} custom-call(bf16[1,2,256,256]{3,2,1,0:T(8,128)(2,1)} %constant.80.clone.refs_0_, f32[2,4,2,256,256]{4,3,2,1,0:T(8,128)} %filt_hbm.1), custom_call_target="tpu_custom_call" | custom-call | flops 536870912 | bytes 4980736 | tf_op jit(solution)/shard_map/give/pallas_call | solution.py:479
  24.1 3.9 %collective-permute-start.1 = (bf16[4,256,256]{2,1,0:T(8,128)(2,1)}, bf16[4,256,256]{2,1,0:T(8,128)(2,1)S(1)}, u32[]{:S(2)}, u32[]{:S(2)}) collective-permute-start(bf16[4,256,256]{2,1,0:T(8,128)(2,1)} %give.3), channel_id=1, source_target_pairs={{0,127},{1,126},{2,125},{3,124},{4,123},{5,122},{6,121},{7,120},{8... | collective-permute-start | bytes 1572872 | tf_op jit(solution)/shard_map/ppermute | solution.py:536
  28.0 0.1 and_select_fusion.2
  28.1 0.1 fusion.5
  28.2 0.3 fusion.9
  28.5 0.2 sin.10
  28.8 2.2 %all-to-all-done.x_ref = bf16[128,4,640]{2,1,0:T(4,128)(2,1)S(1)} async-done(((bf16[128,4,640]{2,1,0:T(4,128)(2,1)}), bf16[128,4,640]{2,1,0:T(4,128)(2,1)S(1)}, u32[]{:S(2)}, u32[]{:S(2)}) %all-to-all-start) | async-done | bytes 655392 | tf_op jit(solution)/shard_map/all_to_all | solution.py:496
  31.0 0.0 copy-done.3
  31.0 2.4 %outer.1 = (bf16[128,16,256]{2,1,0:T(8,128)(2,1)}, f32[8,128]{1,0:T(8,128)S(1)}) custom-call(bf16[128,4,640]{2,1,0:T(4,128)(2,1)S(1)} %all-to-all-done.x_ref, bf16[1024,512]{1,0:T(8,128)(2,1)S(1)} %copy-done.3), custom_call_target="tpu_custom_call" | custom-call | flops 536870912 | bytes 2756608 | tf_op jit(solution)/shard_map/outer/pallas_call | solution.py:479
  33.4 4.6 %all-to-all-start.1 = ((bf16[128,16,256]{2,1,0:T(8,128)(2,1)}), bf16[128,16,256]{2,1,0:T(8,128)(2,1)S(1)}, u32[]{:S(2)}, u32[]{:S(2)}) async-start(bf16[128,16,256]{2,1,0:T(8,128)(2,1)} %get-tuple-element.9), calls=%async_computation.1 | async-start | bytes 2097152 | tf_op jit(solution)/shard_map/all_to_all | solution.py:496
  38.1 3.4 %collective-permute-done.got0_ref = bf16[4,256,256]{2,1,0:T(8,128)(2,1)S(1)} collective-permute-done((bf16[4,256,256]{2,1,0:T(8,128)(2,1)}, bf16[4,256,256]{2,1,0:T(8,128)(2,1)S(1)}, u32[]{:S(2)}, u32[]{:S(2)}) %collective-permute-start) | collective-permute-done | bytes 524320 | tf_op jit(solution)/shard_map/ppermute | solution.py:535
  41.4 0.0 copy-start.5
  41.4 13.2 %collective-permute-done.1.got1_ref = bf16[4,256,256]{2,1,0:T(8,128)(2,1)S(1)} collective-permute-done((bf16[4,256,256]{2,1,0:T(8,128)(2,1)}, bf16[4,256,256]{2,1,0:T(8,128)(2,1)S(1)}, u32[]{:S(2)}, u32[]{:S(2)}) %collective-permute-start.1) | collective-permute-done | bytes 524320 | tf_op jit(solution)/shard_map/ppermute | solution.py:536
  54.6 0.0 copy-done.5
  54.6 0.0 copy-start.6
  54.6 0.8 copy-done.6
  55.4 6.1 %combine.1.bundle_hbm = f32[15,256,256]{2,1,0:T(8,128)} custom-call(f32[2,4,2,256,256]{4,3,2,1,0:T(8,128)} %filt_hbm.1, bf16[2,256,256]{2,1,0:T(8,128)(2,1)} %constant.84.clone.order_ref, f32[2,256,256]{2,1,0:T(8,128)} %constant.83.clone.cross_base_ref, f32[2,128,128]{2,1,0:T(8,128)} %constant.82.clone.base_ref, bf16[4,256,256]{2,1,0:T(8,128)(2,1)} %copy-done.5, ...), custom_call_target="tpu_custom_call" | custom-call | flops 17179869184 | bytes 10092544 | tf_op jit(solution)/shard_map/combine/pallas_call | solution.py:479
  61.5 0.2 all-to-all-done.1.y_ref
  61.7 0.0 copy-start.1
  61.7 8.3 %middle.1 = bf16[128,16,256]{2,1,0:T(8,128)(2,1)S(1)} custom-call(bf16[128,16,256]{2,1,0:T(8,128)(2,1)S(1)} %all-to-all-done.1.y_ref, bf16[2,2,512,256]{3,2,1,0:T(8,128)(2,1)} %constant.85.clone.inner_hbm, f32[15,256,256]{2,1,0:T(8,128)} %combine.1.bundle_hbm, f32[8,128]{1,0:T(8,128)S(1)} %get-tuple-element.10.peak_ref, f32[3,6,256]{2,1,0:T(8,128)S(1)} %reshape.294.wave_ref), custom_call_target="tpu_custom_call" | custom-call | flops 4294967296 | bytes 7100416 | tf_op jit(solution)/shard_map/middle/pallas_call | solution.py:479
  70.0 0.0 copy-start.4
  70.0 0.0 copy-start
  70.1 0.0 copy-start.2
  70.1 28.7 %all_to_all.20.y_ref = bf16[128,16,256]{2,1,0:T(8,128)(2,1)S(1)} all-to-all(bf16[128,16,256]{2,1,0:T(8,128)(2,1)S(1)} %middle.1), channel_id=1, replica_groups=mesh['wide'=16,'narrow'=8] {'wide','narrow'}, dimensions={0} | all-to-all | bytes 2097152 | tf_op jit(solution)/shard_map/all_to_all | solution.py:496
  98.8 0.0 copy-done.1
  98.8 3.0 %last.1 = bf16[128,16,128]{2,1,0:T(8,128)(2,1)} custom-call(bf16[128,16,256]{2,1,0:T(8,128)(2,1)S(1)} %all_to_all.20.y_ref, bf16[4,256,768]{2,1,0:T(8,128)(2,1)S(1)} %copy-done.1, f32[8,128]{1,0:T(8,128)S(1)} %get-tuple-element.10.peak_ref), custom_call_target="tpu_custom_call" | custom-call | flops 536870912 | bytes 3149824 | tf_op jit(solution)/shard_map/last/pallas_call | solution.py:479
  101.9 4.0 %all-to-all-start.3 = ((bf16[128,16,128]{2,1,0:T(8,128)(2,1)}), bf16[128,16,128]{2,1,0:T(8,128)(2,1)S(1)}, u32[]{:S(2)}, u32[]{:S(2)}) async-start(bf16[128,16,128]{2,1,0:T(8,128)(2,1)} %last.1), calls=%async_computation.3 | async-start | bytes 1048576 | tf_op jit(solution)/shard_map/all_to_all | solution.py:496
  105.9 0.0 copy-done.4
  105.9 0.1 copy.15.skip_ref
  106.0 13.9 %all-to-all-done.3.y_ref = bf16[128,16,128]{2,1,0:T(8,128)(2,1)S(1)} async-done(((bf16[128,16,128]{2,1,0:T(8,128)(2,1)}), bf16[128,16,128]{2,1,0:T(8,128)(2,1)S(1)}, u32[]{:S(2)}, u32[]{:S(2)}) %all-to-all-start.3) | async-done | bytes 524320 | tf_op jit(solution)/shard_map/all_to_all | solution.py:496
  119.9 0.0 copy-done
  119.9 0.0 copy-done.2
  119.9 2.0 %finish.1 = bf16[4,65536]{1,0:T(4,128)(2,1)} custom-call(bf16[128,16,128]{2,1,0:T(8,128)(2,1)S(1)} %all-to-all-done.3.y_ref, bf16[4,65536]{1,0:T(4,128)(2,1)S(1)} %copy-done, bf16[4,65536]{1,0:T(4,128)(2,1)S(1)} %copy-done.2, f32[4,1]{1,0:T(4,128)S(1)} %copy.15.skip_ref, f32[8,128]{1,0:T(8,128)S(1)} %get-tuple-element.10.peak_ref), custom_call_target="tpu_custom_call" | custom-call | bytes 2101264 | tf_op jit(solution)/shard_map/finish/pallas_call | solution.py:479
  (3 shorter events, 0.0 us)
Async XLA Ops:
  2.2 28.8 %all-to-all-start = ((bf16[128,4,640]{2,1,0:T(4,128)(2,1)}), bf16[128,4,640]{2,1,0:T(4,128)(2,1)S(1)}, u32[]{:S(2)}, u32[]{:S(2)}) async-start(bf16[128,4,640]{2,1,0:T(4,128)(2,1)} %pack.1), calls=%async_computation | async-start | bytes 1310720 | tf_op jit(solution)/shard_map/all_to_all | solution.py:496
  13.8 17.3 %copy-start.3 = (bf16[1024,512]{1,0:T(8,128)(2,1)S(1)}, bf16[1024,512]{1,0:T(8,128)(2,1)}, u32[]{:S(2)}) copy-start(bf16[1024,512]{1,0:T(8,128)(2,1)} %constant.81.clone.table_ref) | copy-start | bytes 3145732
  16.9 24.6 %collective-permute-start = (bf16[4,256,256]{2,1,0:T(8,128)(2,1)}, bf16[4,256,256]{2,1,0:T(8,128)(2,1)S(1)}, u32[]{:S(2)}, u32[]{:S(2)}) collective-permute-start(bf16[4,256,256]{2,1,0:T(8,128)(2,1)} %give.2), channel_id=1, source_target_pairs={{0,64},{1,127},{2,126},{3,125},{4,124},{5,123},{6,122},{7,121},{8,... | collective-permute-start | bytes 1572872 | tf_op jit(solution)/shard_map/ppermute | solution.py:535
  24.1 30.5 %collective-permute-start.1 = (bf16[4,256,256]{2,1,0:T(8,128)(2,1)}, bf16[4,256,256]{2,1,0:T(8,128)(2,1)S(1)}, u32[]{:S(2)}, u32[]{:S(2)}) collective-permute-start(bf16[4,256,256]{2,1,0:T(8,128)(2,1)} %give.3), channel_id=1, source_target_pairs={{0,127},{1,126},{2,125},{3,124},{4,123},{5,122},{6,121},{7,120},{8... | collective-permute-start | bytes 1572872 | tf_op jit(solution)/shard_map/ppermute | solution.py:536
  33.4 28.3 %all-to-all-start.1 = ((bf16[128,16,256]{2,1,0:T(8,128)(2,1)}), bf16[128,16,256]{2,1,0:T(8,128)(2,1)S(1)}, u32[]{:S(2)}, u32[]{:S(2)}) async-start(bf16[128,16,256]{2,1,0:T(8,128)(2,1)} %get-tuple-element.9), calls=%async_computation.1 | async-start | bytes 2097152 | tf_op jit(solution)/shard_map/all_to_all | solution.py:496
  41.4 13.2 %copy-start.5 = (bf16[4,256,256]{2,1,0:T(8,128)(2,1)}, bf16[4,256,256]{2,1,0:T(8,128)(2,1)S(1)}, u32[]{:S(2)}) copy-start(bf16[4,256,256]{2,1,0:T(8,128)(2,1)S(1)} %collective-permute-done.got0_ref) | copy-start | bytes 1572868
  54.6 0.8 copy-start.6
  61.7 37.1 %copy-start.1 = (bf16[4,256,768]{2,1,0:T(8,128)(2,1)S(1)}, bf16[4,256,768]{2,1,0:T(8,128)(2,1)}, u32[]{:S(2)}) copy-start(bf16[4,256,768]{2,1,0:T(8,128)(2,1)} %constant.86.clone.table_ref) | copy-start | bytes 4718596
  70.0 35.9 %copy-start.4 = (f32[4]{0:T(128)S(1)}, f32[4]{0:T(128)}, u32[]{:S(2)}) copy-start(f32[4]{0:T(128)} %param.14) | copy-start | bytes 52
  70.0 49.9 %copy-start = (bf16[4,65536]{1,0:T(4,128)(2,1)S(1)}, bf16[4,65536]{1,0:T(4,128)(2,1)}, u32[]{:S(2)}) copy-start(bf16[4,65536]{1,0:T(4,128)(2,1)} %sig_ref.1) | copy-start | bytes 1572868
  70.1 49.9 %copy-start.2 = (bf16[4,65536]{1,0:T(4,128)(2,1)S(1)}, bf16[4,65536]{1,0:T(4,128)(2,1)}, u32[]{:S(2)}) copy-start(bf16[4,65536]{1,0:T(4,128)(2,1)} %gate_ref.1) | copy-start | bytes 1572868
  101.9 18.1 %all-to-all-start.3 = ((bf16[128,16,128]{2,1,0:T(8,128)(2,1)}), bf16[128,16,128]{2,1,0:T(8,128)(2,1)S(1)}, u32[]{:S(2)}, u32[]{:S(2)}) async-start(bf16[128,16,128]{2,1,0:T(8,128)(2,1)} %last.1), calls=%async_computation.3 | async-start | bytes 1048576 | tf_op jit(solution)/shard_map/all_to_all | solution.py:496

commit v7 on v6

--- a/solution.py
+++ b/solution.py
@@ -257,7 +257,7 @@
         copy.wait()
 
 
-def combine_kernel(filt_hbm, order_ref, cross_base_ref, base_ref, got0_ref, got1_ref, out_ref, held, sem):
+def combine_kernel(filt_hbm, order_ref, cross_base_ref, base_ref, got0_ref, got1_ref, out_hbm, held, out_ref, sem, out_sem):
     place = place_of()
     copies = [fetch_filter(r, r, place // (ND // 2), filt_hbm, held, sem) for r in range(2)]
     generic = jnp.where(place % (ND // 2) == 0, 0.0, 1.0)
@@ -265,6 +265,14 @@
     out_ref[14, 0:128, 0:128] = base_ref[0]
     out_ref[14, 128:256, 0:128] = base_ref[1]
     out_ref[14, :, 128:256] = jnp.zeros((F, 128), f32)
+    writes = []
+
+    def write(i):
+        writes.append(pltpu.make_async_copy(out_ref.at[i], out_hbm.at[i], out_sem.at[i]))
+        writes[-1].start()
+
+    for i in (12, 13, 14):
+        write(i)
     for copy in (*copies[0], *copies[1]):
         copy.wait()
     for r, got_ref in enumerate((got0_ref, got1_ref)):
@@ -272,9 +280,13 @@
             got = decode_filter(got_ref[i].astype(f32))
             if r == 0:
                 out_ref[8 + i] = got
+                write(8 + i)
                 got = got * generic
             hi, lo = split(held[r, i])
             out_ref[r * 4 + i] = dot(hi, order_ref[1]) + dot(lo, order_ref[1]) + got
+            write(r * 4 + i)
+    for copy in writes:
+        copy.wait()
 
 
 def transform(re, im, table, mf_ref, mi_ref, cross_ref, turn_ref, inner_ref, filt, arrive):
@@ -514,7 +526,6 @@
     spread = exchange(packed)
 
     plain, back = order_tables()
-    held = [((2, 4, F, F), f32), (None, pltpu.SemaphoreType.DMA((2, 4)))]
     given = []
     for r, orders in enumerate(([back, plain], [back])):
         given += call(
@@ -558,11 +569,13 @@
         combine_kernel,
         (spectrum, jnp.asarray(plain), cross_base, base, *got),
         [shape(15, F, F, dtype=f32)],
-        held,
+        [((2, 4, F, F), f32), ((15, F, F), f32)]
+        + [(None, pltpu.SemaphoreType.DMA((2, 4))), (None, pltpu.SemaphoreType.DMA((15,)))],
         "combine",
-        limit=58,
+        limit=51,
         flops=2**34,
         in_specs=[ANY] + [VMEM] * 5,
+        out_specs=[ANY],
     )
     (filtered,) = call(
         middle_kernel,

time: 122 us -> 120 us (0.984)
  blocking collectives: 28.7 us -> 26.5 us
  Pallas kernels: 30.1 us -> 28.3 us
    all_to_all x3, waiting for transfers between devices: 16.4 us -> 19.6 us  [exchange(): return lax.all_to_all(x, AXES, split_axis=0, concat_axis=0, tiled=True)]
    all_to_all x1, blocking collectives: 28.7 us -> 26.5 us  [exchange(): return lax.all_to_all(x, AXES, split_axis=0, concat_axis=0, tiled=True)]
    pallas_call x8, Pallas kernels: 30.1 us -> 28.3 us  [call(): pl.pallas_call(kernel, grid_spec=pltpu.PrefetchScalarGridSpec(num_scalar_...]
  transfers between devices with their start and end apart: 5 -> 5, of which waited for: 5 -> 5; matrix products, arithmetic and copies ran while one was open for 1% -> 1% of each run, Pallas kernels for 12% -> 11%
where the time goes in v7:
time: 120 us; the launch traced here: 119 us
  waiting for transfers between devices  34.1 us (28%)
  Pallas kernels  28.3 us (24%)
  starting transfers between devices  28.3 us (24%)
  blocking collectives  26.5 us (22%)
  local copies, waits for them, and re-layouts  1.63 us (1%)
    pallas_call x8, Pallas kernels, call(): pl.pallas_call(kernel, grid_spec=pltpu.PrefetchScalarGridSpec(num_scalar_...  28.3 us
    all_to_all x1, blocking collectives, exchange(): return lax.all_to_all(x, AXES, split_axis=0, concat_axis=0, tiled=True)  26.5 us
    all_to_all x3, starting transfers between devices, exchange(): return lax.all_to_all(x, AXES, split_axis=0, concat_axis=0, tiled=True)  20.1 us
    all_to_all x3, waiting for transfers between devices, exchange(): return lax.all_to_all(x, AXES, split_axis=0, concat_axis=0, tiled=True)  19.6 us
    ppermute x1, waiting for transfers between devices, per_device(): lax.ppermute(given[1], AXES, [(p, ND - 1 - p) for p in range(ND)])  12.2 us
    ppermute x1, starting transfers between devices, per_device(): lax.ppermute(given[0], AXES, mirror)  4.25 us
    ppermute x1, starting transfers between devices, per_device(): lax.ppermute(given[1], AXES, [(p, ND - 1 - p) for p in range(ND)])  3.96 us
  transfers between devices with their start and end apart: 5, of which 5 were waited for; matrix products, arithmetic and copies ran while one was open for 1% of the time, Pallas kernels for 11%

profile of v7, /device:TPU:1, one launch (start us, length us, event | category | flops | bytes accessed | tf_op | source)
XLA Modules:
  0.0 119.4 jit_solution(7127799424108923880)
XLA Ops:
  0.0 2.2 %pack.1 = bf16[128,4,640]{2,1,0:T(4,128)(2,1)} custom-call(bf16[4,65536]{1,0:T(4,128)(2,1)} %sig_ref.1), custom_call_target="tpu_custom_call" | custom-call | bytes 1179648 | tf_op jit(solution)/shard_map/pack/pallas_call | solution.py:491
  2.2 11.5 %all-to-all-start = ((bf16[128,4,640]{2,1,0:T(4,128)(2,1)}), bf16[128,4,640]{2,1,0:T(4,128)(2,1)S(1)}, u32[]{:S(2)}, u32[]{:S(2)}) async-start(bf16[128,4,640]{2,1,0:T(4,128)(2,1)} %pack.1), calls=%async_computation | async-start | bytes 1310720 | tf_op jit(solution)/shard_map/all_to_all | solution.py:508
  13.8 3.0 %give.2 = bf16[4,256,256]{2,1,0:T(8,128)(2,1)} custom-call(bf16[2,2,256,256]{3,2,1,0:T(8,128)(2,1)} %constant.79.clone.refs_0_, f32[2,4,2,256,256]{4,3,2,1,0:T(8,128)} %filt_hbm.1), custom_call_target="tpu_custom_call" | custom-call | flops 536870912 | bytes 5242880 | tf_op jit(solution)/shard_map/give/pallas_call | solution.py:491
  16.8 0.0 copy-start.4
  16.8 0.0 copy-start.5
  16.8 0.0 copy-start.6
  16.8 4.3 %collective-permute-start = (bf16[4,256,256]{2,1,0:T(8,128)(2,1)}, bf16[4,256,256]{2,1,0:T(8,128)(2,1)S(1)}, u32[]{:S(2)}, u32[]{:S(2)}) collective-permute-start(bf16[4,256,256]{2,1,0:T(8,128)(2,1)} %give.2), channel_id=1, source_target_pairs={{0,64},{1,127},{2,126},{3,125},{4,124},{5,123},{6,122},{7,121},{8,... | collective-permute-start | bytes 1572872 | tf_op jit(solution)/shard_map/ppermute | solution.py:546
  21.1 3.0 %give.3 = bf16[4,256,256]{2,1,0:T(8,128)(2,1)} custom-call(bf16[1,2,256,256]{3,2,1,0:T(8,128)(2,1)} %constant.80.clone.refs_0_, f32[2,4,2,256,256]{4,3,2,1,0:T(8,128)} %filt_hbm.1), custom_call_target="tpu_custom_call" | custom-call | flops 536870912 | bytes 4980736 | tf_op jit(solution)/shard_map/give/pallas_call | solution.py:491
  24.1 4.0 %collective-permute-start.1 = (bf16[4,256,256]{2,1,0:T(8,128)(2,1)}, bf16[4,256,256]{2,1,0:T(8,128)(2,1)S(1)}, u32[]{:S(2)}, u32[]{:S(2)}) collective-permute-start(bf16[4,256,256]{2,1,0:T(8,128)(2,1)} %give.3), channel_id=1, source_target_pairs={{0,127},{1,126},{2,125},{3,124},{4,123},{5,122},{6,121},{7,120},{8... | collective-permute-start | bytes 1572872 | tf_op jit(solution)/shard_map/ppermute | solution.py:547
  28.0 0.1 and_select_fusion.2
  28.1 0.1 fusion.5
  28.2 0.3 fusion.9
  28.5 0.2 sin.10
  28.8 2.2 %all-to-all-done.x_ref = bf16[128,4,640]{2,1,0:T(4,128)(2,1)S(1)} async-done(((bf16[128,4,640]{2,1,0:T(4,128)(2,1)}), bf16[128,4,640]{2,1,0:T(4,128)(2,1)S(1)}, u32[]{:S(2)}, u32[]{:S(2)}) %all-to-all-start) | async-done | bytes 655392 | tf_op jit(solution)/shard_map/all_to_all | solution.py:508
  31.0 0.0 copy-start.3
  31.0 1.2 %copy-done.3 = bf16[1024,512]{1,0:T(8,128)(2,1)S(1)} copy-done((bf16[1024,512]{1,0:T(8,128)(2,1)S(1)}, bf16[1024,512]{1,0:T(8,128)(2,1)}, u32[]{:S(2)}) %copy-start.3) | copy-done | bytes 1048600
  32.2 2.4 %outer.1 = (bf16[128,16,256]{2,1,0:T(8,128)(2,1)}, f32[8,128]{1,0:T(8,128)S(1)}) custom-call(bf16[128,4,640]{2,1,0:T(4,128)(2,1)S(1)} %all-to-all-done.x_ref, bf16[1024,512]{1,0:T(8,128)(2,1)S(1)} %copy-done.3), custom_call_target="tpu_custom_call" | custom-call | flops 536870912 | bytes 2756608 | tf_op jit(solution)/shard_map/outer/pallas_call | solution.py:491
  34.6 4.6 %all-to-all-start.1 = ((bf16[128,16,256]{2,1,0:T(8,128)(2,1)}), bf16[128,16,256]{2,1,0:T(8,128)(2,1)S(1)}, u32[]{:S(2)}, u32[]{:S(2)}) async-start(bf16[128,16,256]{2,1,0:T(8,128)(2,1)} %get-tuple-element.9), calls=%async_computation.1 | async-start | bytes 2097152 | tf_op jit(solution)/shard_map/all_to_all | solution.py:508
  39.2 2.3 %collective-permute-done.got0_ref = bf16[4,256,256]{2,1,0:T(8,128)(2,1)S(1)} collective-permute-done((bf16[4,256,256]{2,1,0:T(8,128)(2,1)}, bf16[4,256,256]{2,1,0:T(8,128)(2,1)S(1)}, u32[]{:S(2)}, u32[]{:S(2)}) %collective-permute-start) | collective-permute-done | bytes 524320 | tf_op jit(solution)/shard_map/ppermute | solution.py:546
  41.5 12.2 %collective-permute-done.1.got1_ref = bf16[4,256,256]{2,1,0:T(8,128)(2,1)S(1)} collective-permute-done((bf16[4,256,256]{2,1,0:T(8,128)(2,1)}, bf16[4,256,256]{2,1,0:T(8,128)(2,1)S(1)}, u32[]{:S(2)}, u32[]{:S(2)}) %collective-permute-start.1) | collective-permute-done | bytes 524320 | tf_op jit(solution)/shard_map/ppermute | solution.py:547
  53.7 0.0 copy-done.4
  53.7 0.0 copy-done.5
  53.7 0.0 copy-done.6
  53.7 4.2 %combine.1.bundle_hbm = f32[15,256,256]{2,1,0:T(8,128)} custom-call(f32[2,4,2,256,256]{4,3,2,1,0:T(8,128)} %filt_hbm.1, bf16[2,256,256]{2,1,0:T(8,128)(2,1)S(1)} %copy-done.5, f32[2,256,256]{2,1,0:T(8,128)S(1)} %copy-done.4, f32[2,128,128]{2,1,0:T(8,128)S(1)} %copy-done.6, bf16[4,256,256]{2,1,0:T(8,128)(2,1)S(1)} %collective-permute-done.got0_ref, ...), custom_call_target="tpu_custom_call" | custom-call | flops 17179869184 | bytes 10092544 | tf_op jit(solution)/shard_map/combine/pallas_call | solution.py:491
  57.9 3.5 %all-to-all-done.1.y_ref = bf16[128,16,256]{2,1,0:T(8,128)(2,1)S(1)} async-done(((bf16[128,16,256]{2,1,0:T(8,128)(2,1)}), bf16[128,16,256]{2,1,0:T(8,128)(2,1)S(1)}, u32[]{:S(2)}, u32[]{:S(2)}) %all-to-all-start.1) | async-done | bytes 1048608 | tf_op jit(solution)/shard_map/all_to_all | solution.py:508
  61.4 0.0 copy-start.1
  61.4 8.3 %middle.1 = bf16[128,16,256]{2,1,0:T(8,128)(2,1)S(1)} custom-call(bf16[128,16,256]{2,1,0:T(8,128)(2,1)S(1)} %all-to-all-done.1.y_ref, bf16[2,2,512,256]{3,2,1,0:T(8,128)(2,1)} %constant.85.clone.inner_hbm, f32[15,256,256]{2,1,0:T(8,128)} %combine.1.bundle_hbm, f32[8,128]{1,0:T(8,128)S(1)} %get-tuple-element.10.peak_ref, f32[3,6,256]{2,1,0:T(8,128)S(1)} %reshape.294.wave_ref), custom_call_target="tpu_custom_call" | custom-call | flops 4294967296 | bytes 7100416 | tf_op jit(solution)/shard_map/middle/pallas_call | solution.py:491
  69.7 0.0 copy-start.7
  69.8 0.0 copy-start
  69.8 0.0 copy-start.2
  69.8 26.5 %all_to_all.20.y_ref = bf16[128,16,256]{2,1,0:T(8,128)(2,1)S(1)} all-to-all(bf16[128,16,256]{2,1,0:T(8,128)(2,1)S(1)} %middle.1), channel_id=1, replica_groups=mesh['wide'=16,'narrow'=8] {'wide','narrow'}, dimensions={0} | all-to-all | bytes 2097152 | tf_op jit(solution)/shard_map/all_to_all | solution.py:508
  96.3 0.0 copy-done.1
  96.3 3.0 %last.1 = bf16[128,16,128]{2,1,0:T(8,128)(2,1)} custom-call(bf16[128,16,256]{2,1,0:T(8,128)(2,1)S(1)} %all_to_all.20.y_ref, bf16[4,256,768]{2,1,0:T(8,128)(2,1)S(1)} %copy-done.1, f32[8,128]{1,0:T(8,128)S(1)} %get-tuple-element.10.peak_ref), custom_call_target="tpu_custom_call" | custom-call | flops 536870912 | bytes 3149824 | tf_op jit(solution)/shard_map/last/pallas_call | solution.py:491
  99.4 4.0 %all-to-all-start.3 = ((bf16[128,16,128]{2,1,0:T(8,128)(2,1)}), bf16[128,16,128]{2,1,0:T(8,128)(2,1)S(1)}, u32[]{:S(2)}, u32[]{:S(2)}) async-start(bf16[128,16,128]{2,1,0:T(8,128)(2,1)} %last.1), calls=%async_computation.3 | async-start | bytes 1048576 | tf_op jit(solution)/shard_map/all_to_all | solution.py:508
  103.4 0.0 copy-done.7
  103.4 0.1 copy.15.skip_ref
  103.5 13.9 %all-to-all-done.3.y_ref = bf16[128,16,128]{2,1,0:T(8,128)(2,1)S(1)} async-done(((bf16[128,16,128]{2,1,0:T(8,128)(2,1)}), bf16[128,16,128]{2,1,0:T(8,128)(2,1)S(1)}, u32[]{:S(2)}, u32[]{:S(2)}) %all-to-all-start.3) | async-done | bytes 524320 | tf_op jit(solution)/shard_map/all_to_all | solution.py:508
  117.4 0.0 copy-done
  117.4 0.0 copy-done.2
  117.4 2.0 %finish.1 = bf16[4,65536]{1,0:T(4,128)(2,1)} custom-call(bf16[128,16,128]{2,1,0:T(8,128)(2,1)S(1)} %all-to-all-done.3.y_ref, bf16[4,65536]{1,0:T(4,128)(2,1)S(1)} %copy-done, bf16[4,65536]{1,0:T(4,128)(2,1)S(1)} %copy-done.2, f32[4,1]{1,0:T(4,128)S(1)} %copy.15.skip_ref, f32[8,128]{1,0:T(8,128)S(1)} %get-tuple-element.10.peak_ref), custom_call_target="tpu_custom_call" | custom-call | bytes 2101264 | tf_op jit(solution)/shard_map/finish/pallas_call | solution.py:491
  (3 shorter events, 0.0 us)
Async XLA Ops:
  2.2 28.8 %all-to-all-start = ((bf16[128,4,640]{2,1,0:T(4,128)(2,1)}), bf16[128,4,640]{2,1,0:T(4,128)(2,1)S(1)}, u32[]{:S(2)}, u32[]{:S(2)}) async-start(bf16[128,4,640]{2,1,0:T(4,128)(2,1)} %pack.1), calls=%async_computation | async-start | bytes 1310720 | tf_op jit(solution)/shard_map/all_to_all | solution.py:508
  16.8 36.9 %copy-start.4 = (f32[2,256,256]{2,1,0:T(8,128)S(1)}, f32[2,256,256]{2,1,0:T(8,128)}, u32[]{:S(2)}) copy-start(f32[2,256,256]{2,1,0:T(8,128)} %constant.83.clone.cross_base_ref) | copy-start | bytes 1572868
  16.8 36.9 %copy-start.5 = (bf16[2,256,256]{2,1,0:T(8,128)(2,1)S(1)}, bf16[2,256,256]{2,1,0:T(8,128)(2,1)}, u32[]{:S(2)}) copy-start(bf16[2,256,256]{2,1,0:T(8,128)(2,1)} %constant.84.clone.order_ref) | copy-start | bytes 786436
  16.8 36.9 %copy-start.6 = (f32[2,128,128]{2,1,0:T(8,128)S(1)}, f32[2,128,128]{2,1,0:T(8,128)}, u32[]{:S(2)}) copy-start(f32[2,128,128]{2,1,0:T(8,128)} %constant.82.clone.base_ref) | copy-start | bytes 393220
  16.8 24.7 %collective-permute-start = (bf16[4,256,256]{2,1,0:T(8,128)(2,1)}, bf16[4,256,256]{2,1,0:T(8,128)(2,1)S(1)}, u32[]{:S(2)}, u32[]{:S(2)}) collective-permute-start(bf16[4,256,256]{2,1,0:T(8,128)(2,1)} %give.2), channel_id=1, source_target_pairs={{0,64},{1,127},{2,126},{3,125},{4,124},{5,123},{6,122},{7,121},{8,... | collective-permute-start | bytes 1572872 | tf_op jit(solution)/shard_map/ppermute | solution.py:546
  24.1 29.6 %collective-permute-start.1 = (bf16[4,256,256]{2,1,0:T(8,128)(2,1)}, bf16[4,256,256]{2,1,0:T(8,128)(2,1)S(1)}, u32[]{:S(2)}, u32[]{:S(2)}) collective-permute-start(bf16[4,256,256]{2,1,0:T(8,128)(2,1)} %give.3), channel_id=1, source_target_pairs={{0,127},{1,126},{2,125},{3,124},{4,123},{5,122},{6,121},{7,120},{8... | collective-permute-start | bytes 1572872 | tf_op jit(solution)/shard_map/ppermute | solution.py:547
  31.0 1.2 %copy-start.3 = (bf16[1024,512]{1,0:T(8,128)(2,1)S(1)}, bf16[1024,512]{1,0:T(8,128)(2,1)}, u32[]{:S(2)}) copy-start(bf16[1024,512]{1,0:T(8,128)(2,1)} %constant.81.clone.table_ref) | copy-start | bytes 3145732
  34.6 26.8 %all-to-all-start.1 = ((bf16[128,16,256]{2,1,0:T(8,128)(2,1)}), bf16[128,16,256]{2,1,0:T(8,128)(2,1)S(1)}, u32[]{:S(2)}, u32[]{:S(2)}) async-start(bf16[128,16,256]{2,1,0:T(8,128)(2,1)} %get-tuple-element.9), calls=%async_computation.1 | async-start | bytes 2097152 | tf_op jit(solution)/shard_map/all_to_all | solution.py:508
  61.4 34.9 %copy-start.1 = (bf16[4,256,768]{2,1,0:T(8,128)(2,1)S(1)}, bf16[4,256,768]{2,1,0:T(8,128)(2,1)}, u32[]{:S(2)}) copy-start(bf16[4,256,768]{2,1,0:T(8,128)(2,1)} %constant.86.clone.table_ref) | copy-start | bytes 4718596
  69.7 33.6 %copy-start.7 = (f32[4]{0:T(128)S(1)}, f32[4]{0:T(128)}, u32[]{:S(2)}) copy-start(f32[4]{0:T(128)} %param.14) | copy-start | bytes 52
  69.8 47.7 %copy-start = (bf16[4,65536]{1,0:T(4,128)(2,1)S(1)}, bf16[4,65536]{1,0:T(4,128)(2,1)}, u32[]{:S(2)}) copy-start(bf16[4,65536]{1,0:T(4,128)(2,1)} %sig_ref.1) | copy-start | bytes 1572868
  69.8 47.7 %copy-start.2 = (bf16[4,65536]{1,0:T(4,128)(2,1)S(1)}, bf16[4,65536]{1,0:T(4,128)(2,1)}, u32[]{:S(2)}) copy-start(bf16[4,65536]{1,0:T(4,128)(2,1)} %gate_ref.1) | copy-start | bytes 1572868
  99.4 18.1 %all-to-all-start.3 = ((bf16[128,16,128]{2,1,0:T(8,128)(2,1)}), bf16[128,16,128]{2,1,0:T(8,128)(2,1)S(1)}, u32[]{:S(2)}, u32[]{:S(2)}) async-start(bf16[128,16,128]{2,1,0:T(8,128)(2,1)} %last.1), calls=%async_computation.3 | async-start | bytes 1048576 | tf_op jit(solution)/shard_map/all_to_all | solution.py:508

commit v8 on v7

--- a/solution.py
+++ b/solution.py
@@ -171,7 +171,9 @@
         copy.wait()
 
 
-def outer_kernel(x_ref, table_ref, out_hbm, peak_ref, buf, out_ref, sem):
+def outer_kernel(x_ref, table_hbm, out_hbm, peak_ref, buf, out_ref, table_ref, sem):
+    load = pltpu.make_async_copy(table_hbm, table_ref, sem.at[STEPS])
+    load.start()
     top = jnp.zeros((4, 128), f32)
     for n in range(ND):
         x = x_ref[n].astype(f32)
@@ -180,6 +182,7 @@
             buf[i, pl.ds(n * 8, 4), :] = x[:, i * 128 : (i + 1) * 128]
     peak = jnp.maximum(jnp.max(top, keepdims=True), 1e-30)
     peak_ref[...] = jnp.broadcast_to(peak, (8, 128))
+    load.wait()
     writes = []
     for pair in range(2):
         rows = []
@@ -558,9 +561,12 @@
         outer_kernel,
         (spread, jnp.asarray(outer_forward_table())),
         [shape(ND, 16, F), shape(8, 128, dtype=f32)],
-        [((4, ND * 8, 128), f32), ((ND, 16, F), bf16), (None, pltpu.SemaphoreType.DMA((STEPS,)))],
+        [((4, ND * 8, 128), f32), ((ND, 16, F), bf16), ((ND * 8, 512), bf16)]
+        + [(None, pltpu.SemaphoreType.DMA((STEPS + 1,)))],
         "outer",
+        limit=53,
         flops=2**29,
+        in_specs=[VMEM, ANY],
         out_specs=[ANY, VMEM],
     )
     field = exchange(field)

time: 120 us -> 120 us (level)
  local copies, waits for them, and re-layouts: 1.63 us -> 0.4 us
    unnamed x16 -> x14, local copies, waits for them, and re-layouts: 1.27 us -> 0.04 us
where the time goes in v8:
time: 120 us; the launch traced here: 119 us
  waiting for transfers between devices  34.3 us (29%)
  Pallas kernels  29.3 us (24%)
  starting transfers between devices  28.3 us (24%)
  blocking collectives  26.4 us (22%)
    pallas_call x8, Pallas kernels, call(): pl.pallas_call(kernel, grid_spec=pltpu.PrefetchScalarGridSpec(num_scalar_...  29.3 us
    all_to_all x1, blocking collectives, exchange(): return lax.all_to_all(x, AXES, split_axis=0, concat_axis=0, tiled=True)  26.4 us
    all_to_all x3, starting transfers between devices, exchange(): return lax.all_to_all(x, AXES, split_axis=0, concat_axis=0, tiled=True)  20.1 us
    all_to_all x3, waiting for transfers between devices, exchange(): return lax.all_to_all(x, AXES, split_axis=0, concat_axis=0, tiled=True)  19.3 us
    ppermute x1, waiting for transfers between devices, per_device(): lax.ppermute(given[1], AXES, [(p, ND - 1 - p) for p in range(ND)])  12.6 us
    ppermute x1, starting transfers between devices, per_device(): lax.ppermute(given[0], AXES, mirror)  4.25 us
    ppermute x1, starting transfers between devices, per_device(): lax.ppermute(given[1], AXES, [(p, ND - 1 - p) for p in range(ND)])  3.96 us
    ppermute x1, waiting for transfers between devices, per_device(): lax.ppermute(given[0], AXES, mirror)  2.47 us
  transfers between devices with their start and end apart: 5, of which 5 were waited for; matrix products, arithmetic and copies ran while one was open for 1% of the time, Pallas kernels for 11%

profile of v8, /device:TPU:1, one launch (start us, length us, event | category | flops | bytes accessed | tf_op | source)
XLA Modules:
  0.0 119.4 jit_solution(15193652278288263719)
XLA Ops:
  0.0 2.2 %pack.1 = bf16[128,4,640]{2,1,0:T(4,128)(2,1)} custom-call(bf16[4,65536]{1,0:T(4,128)(2,1)} %sig_ref.1), custom_call_target="tpu_custom_call" | custom-call | bytes 1179648 | tf_op jit(solution)/shard_map/pack/pallas_call | solution.py:494
  2.2 11.5 %all-to-all-start = ((bf16[128,4,640]{2,1,0:T(4,128)(2,1)}), bf16[128,4,640]{2,1,0:T(4,128)(2,1)S(1)}, u32[]{:S(2)}, u32[]{:S(2)}) async-start(bf16[128,4,640]{2,1,0:T(4,128)(2,1)} %pack.1), calls=%async_computation | async-start | bytes 1310720 | tf_op jit(solution)/shard_map/all_to_all | solution.py:511
  13.8 3.0 %give.2 = bf16[4,256,256]{2,1,0:T(8,128)(2,1)} custom-call(bf16[2,2,256,256]{3,2,1,0:T(8,128)(2,1)} %constant.79.clone.refs_0_, f32[2,4,2,256,256]{4,3,2,1,0:T(8,128)} %filt_hbm.1), custom_call_target="tpu_custom_call" | custom-call | flops 536870912 | bytes 5242880 | tf_op jit(solution)/shard_map/give/pallas_call | solution.py:494
  16.8 0.0 copy-start.3
  16.8 0.0 copy-start.4
  16.8 0.0 copy-start.5
  16.8 4.3 %collective-permute-start = (bf16[4,256,256]{2,1,0:T(8,128)(2,1)}, bf16[4,256,256]{2,1,0:T(8,128)(2,1)S(1)}, u32[]{:S(2)}, u32[]{:S(2)}) collective-permute-start(bf16[4,256,256]{2,1,0:T(8,128)(2,1)} %give.2), channel_id=1, source_target_pairs={{0,64},{1,127},{2,126},{3,125},{4,124},{5,123},{6,122},{7,121},{8,... | collective-permute-start | bytes 1572872 | tf_op jit(solution)/shard_map/ppermute | solution.py:549
  21.1 3.0 %give.3 = bf16[4,256,256]{2,1,0:T(8,128)(2,1)} custom-call(bf16[1,2,256,256]{3,2,1,0:T(8,128)(2,1)} %constant.80.clone.refs_0_, f32[2,4,2,256,256]{4,3,2,1,0:T(8,128)} %filt_hbm.1), custom_call_target="tpu_custom_call" | custom-call | flops 536870912 | bytes 4980736 | tf_op jit(solution)/shard_map/give/pallas_call | solution.py:494
  24.1 4.0 %collective-permute-start.1 = (bf16[4,256,256]{2,1,0:T(8,128)(2,1)}, bf16[4,256,256]{2,1,0:T(8,128)(2,1)S(1)}, u32[]{:S(2)}, u32[]{:S(2)}) collective-permute-start(bf16[4,256,256]{2,1,0:T(8,128)(2,1)} %give.3), channel_id=1, source_target_pairs={{0,127},{1,126},{2,125},{3,124},{4,123},{5,122},{6,121},{7,120},{8... | collective-permute-start | bytes 1572872 | tf_op jit(solution)/shard_map/ppermute | solution.py:550
  28.0 0.1 and_select_fusion.2
  28.1 0.1 fusion.5
  28.2 0.3 fusion.9
  28.5 0.2 sin.10
  28.8 2.2 %all-to-all-done.x_ref = bf16[128,4,640]{2,1,0:T(4,128)(2,1)S(1)} async-done(((bf16[128,4,640]{2,1,0:T(4,128)(2,1)}), bf16[128,4,640]{2,1,0:T(4,128)(2,1)S(1)}, u32[]{:S(2)}, u32[]{:S(2)}) %all-to-all-start) | async-done | bytes 655392 | tf_op jit(solution)/shard_map/all_to_all | solution.py:511
  31.0 3.4 %outer.1 = (bf16[128,16,256]{2,1,0:T(8,128)(2,1)}, f32[8,128]{1,0:T(8,128)S(1)}) custom-call(bf16[128,4,640]{2,1,0:T(4,128)(2,1)S(1)} %all-to-all-done.x_ref, bf16[1024,512]{1,0:T(8,128)(2,1)} %constant.81.clone.table_hbm), custom_call_target="tpu_custom_call" | custom-call | flops 536870912 | bytes 2756608 | tf_op jit(solution)/shard_map/outer/pallas_call | solution.py:494
  34.4 4.6 %all-to-all-start.1 = ((bf16[128,16,256]{2,1,0:T(8,128)(2,1)}), bf16[128,16,256]{2,1,0:T(8,128)(2,1)S(1)}, u32[]{:S(2)}, u32[]{:S(2)}) async-start(bf16[128,16,256]{2,1,0:T(8,128)(2,1)} %get-tuple-element.9), calls=%async_computation.1 | async-start | bytes 2097152 | tf_op jit(solution)/shard_map/all_to_all | solution.py:511
  39.0 2.5 %collective-permute-done.got0_ref = bf16[4,256,256]{2,1,0:T(8,128)(2,1)S(1)} collective-permute-done((bf16[4,256,256]{2,1,0:T(8,128)(2,1)}, bf16[4,256,256]{2,1,0:T(8,128)(2,1)S(1)}, u32[]{:S(2)}, u32[]{:S(2)}) %collective-permute-start) | collective-permute-done | bytes 524320 | tf_op jit(solution)/shard_map/ppermute | solution.py:549
  41.5 12.6 %collective-permute-done.1.got1_ref = bf16[4,256,256]{2,1,0:T(8,128)(2,1)S(1)} collective-permute-done((bf16[4,256,256]{2,1,0:T(8,128)(2,1)}, bf16[4,256,256]{2,1,0:T(8,128)(2,1)S(1)}, u32[]{:S(2)}, u32[]{:S(2)}) %collective-permute-start.1) | collective-permute-done | bytes 524320 | tf_op jit(solution)/shard_map/ppermute | solution.py:550
  54.1 0.0 copy-done.3
  54.1 0.0 copy-done.4
  54.1 0.0 copy-done.5
  54.1 4.3 %combine.1.bundle_hbm = f32[15,256,256]{2,1,0:T(8,128)} custom-call(f32[2,4,2,256,256]{4,3,2,1,0:T(8,128)} %filt_hbm.1, bf16[2,256,256]{2,1,0:T(8,128)(2,1)S(1)} %copy-done.4, f32[2,256,256]{2,1,0:T(8,128)S(1)} %copy-done.3, f32[2,128,128]{2,1,0:T(8,128)S(1)} %copy-done.5, bf16[4,256,256]{2,1,0:T(8,128)(2,1)S(1)} %collective-permute-done.got0_ref, ...), custom_call_target="tpu_custom_call" | custom-call | flops 17179869184 | bytes 10092544 | tf_op jit(solution)/shard_map/combine/pallas_call | solution.py:494
  58.4 3.1 %all-to-all-done.1.y_ref = bf16[128,16,256]{2,1,0:T(8,128)(2,1)S(1)} async-done(((bf16[128,16,256]{2,1,0:T(8,128)(2,1)}), bf16[128,16,256]{2,1,0:T(8,128)(2,1)S(1)}, u32[]{:S(2)}, u32[]{:S(2)}) %all-to-all-start.1) | async-done | bytes 1048608 | tf_op jit(solution)/shard_map/all_to_all | solution.py:511
  61.5 0.0 copy-start.1
  61.5 8.3 %middle.1 = bf16[128,16,256]{2,1,0:T(8,128)(2,1)S(1)} custom-call(bf16[128,16,256]{2,1,0:T(8,128)(2,1)S(1)} %all-to-all-done.1.y_ref, bf16[2,2,512,256]{3,2,1,0:T(8,128)(2,1)} %constant.85.clone.inner_hbm, f32[15,256,256]{2,1,0:T(8,128)} %combine.1.bundle_hbm, f32[8,128]{1,0:T(8,128)S(1)} %get-tuple-element.10.peak_ref, f32[3,6,256]{2,1,0:T(8,128)S(1)} %reshape.294.wave_ref), custom_call_target="tpu_custom_call" | custom-call | flops 4294967296 | bytes 7100416 | tf_op jit(solution)/shard_map/middle/pallas_call | solution.py:494
  69.8 0.0 copy-start.6
  69.8 0.0 copy-start
  69.8 0.0 copy-start.2
  69.8 26.4 %all_to_all.20.y_ref = bf16[128,16,256]{2,1,0:T(8,128)(2,1)S(1)} all-to-all(bf16[128,16,256]{2,1,0:T(8,128)(2,1)S(1)} %middle.1), channel_id=1, replica_groups=mesh['wide'=16,'narrow'=8] {'wide','narrow'}, dimensions={0} | all-to-all | bytes 2097152 | tf_op jit(solution)/shard_map/all_to_all | solution.py:511
  96.3 0.0 copy-done.1
  96.3 3.0 %last.1 = bf16[128,16,128]{2,1,0:T(8,128)(2,1)} custom-call(bf16[128,16,256]{2,1,0:T(8,128)(2,1)S(1)} %all_to_all.20.y_ref, bf16[4,256,768]{2,1,0:T(8,128)(2,1)S(1)} %copy-done.1, f32[8,128]{1,0:T(8,128)S(1)} %get-tuple-element.10.peak_ref), custom_call_target="tpu_custom_call" | custom-call | flops 536870912 | bytes 3149824 | tf_op jit(solution)/shard_map/last/pallas_call | solution.py:494
  99.3 4.0 %all-to-all-start.3 = ((bf16[128,16,128]{2,1,0:T(8,128)(2,1)}), bf16[128,16,128]{2,1,0:T(8,128)(2,1)S(1)}, u32[]{:S(2)}, u32[]{:S(2)}) async-start(bf16[128,16,128]{2,1,0:T(8,128)(2,1)} %last.1), calls=%async_computation.3 | async-start | bytes 1048576 | tf_op jit(solution)/shard_map/all_to_all | solution.py:511
  103.4 0.0 copy-done.6
  103.4 0.1 copy.15.skip_ref
  103.5 13.9 %all-to-all-done.3.y_ref = bf16[128,16,128]{2,1,0:T(8,128)(2,1)S(1)} async-done(((bf16[128,16,128]{2,1,0:T(8,128)(2,1)}), bf16[128,16,128]{2,1,0:T(8,128)(2,1)S(1)}, u32[]{:S(2)}, u32[]{:S(2)}) %all-to-all-start.3) | async-done | bytes 524320 | tf_op jit(solution)/shard_map/all_to_all | solution.py:511
  117.4 0.0 copy-done
  117.4 0.0 copy-done.2
  117.4 2.0 %finish.1 = bf16[4,65536]{1,0:T(4,128)(2,1)} custom-call(bf16[128,16,128]{2,1,0:T(8,128)(2,1)S(1)} %all-to-all-done.3.y_ref, bf16[4,65536]{1,0:T(4,128)(2,1)S(1)} %copy-done, bf16[4,65536]{1,0:T(4,128)(2,1)S(1)} %copy-done.2, f32[4,1]{1,0:T(4,128)S(1)} %copy.15.skip_ref, f32[8,128]{1,0:T(8,128)S(1)} %get-tuple-element.10.peak_ref), custom_call_target="tpu_custom_call" | custom-call | bytes 2101264 | tf_op jit(solution)/shard_map/finish/pallas_call | solution.py:494
  (3 shorter events, 0.0 us)
Async XLA Ops:
  2.2 28.8 %all-to-all-start = ((bf16[128,4,640]{2,1,0:T(4,128)(2,1)}), bf16[128,4,640]{2,1,0:T(4,128)(2,1)S(1)}, u32[]{:S(2)}, u32[]{:S(2)}) async-start(bf16[128,4,640]{2,1,0:T(4,128)(2,1)} %pack.1), calls=%async_computation | async-start | bytes 1310720 | tf_op jit(solution)/shard_map/all_to_all | solution.py:511
  16.8 37.3 %copy-start.3 = (f32[2,256,256]{2,1,0:T(8,128)S(1)}, f32[2,256,256]{2,1,0:T(8,128)}, u32[]{:S(2)}) copy-start(f32[2,256,256]{2,1,0:T(8,128)} %constant.83.clone.cross_base_ref) | copy-start | bytes 1572868
  16.8 37.3 %copy-start.4 = (bf16[2,256,256]{2,1,0:T(8,128)(2,1)S(1)}, bf16[2,256,256]{2,1,0:T(8,128)(2,1)}, u32[]{:S(2)}) copy-start(bf16[2,256,256]{2,1,0:T(8,128)(2,1)} %constant.84.clone.order_ref) | copy-start | bytes 786436
  16.8 37.3 %copy-start.5 = (f32[2,128,128]{2,1,0:T(8,128)S(1)}, f32[2,128,128]{2,1,0:T(8,128)}, u32[]{:S(2)}) copy-start(f32[2,128,128]{2,1,0:T(8,128)} %constant.82.clone.base_ref) | copy-start | bytes 393220
  16.8 24.7 %collective-permute-start = (bf16[4,256,256]{2,1,0:T(8,128)(2,1)}, bf16[4,256,256]{2,1,0:T(8,128)(2,1)S(1)}, u32[]{:S(2)}, u32[]{:S(2)}) collective-permute-start(bf16[4,256,256]{2,1,0:T(8,128)(2,1)} %give.2), channel_id=1, source_target_pairs={{0,64},{1,127},{2,126},{3,125},{4,124},{5,123},{6,122},{7,121},{8,... | collective-permute-start | bytes 1572872 | tf_op jit(solution)/shard_map/ppermute | solution.py:549
  24.1 30.0 %collective-permute-start.1 = (bf16[4,256,256]{2,1,0:T(8,128)(2,1)}, bf16[4,256,256]{2,1,0:T(8,128)(2,1)S(1)}, u32[]{:S(2)}, u32[]{:S(2)}) collective-permute-start(bf16[4,256,256]{2,1,0:T(8,128)(2,1)} %give.3), channel_id=1, source_target_pairs={{0,127},{1,126},{2,125},{3,124},{4,123},{5,122},{6,121},{7,120},{8... | collective-permute-start | bytes 1572872 | tf_op jit(solution)/shard_map/ppermute | solution.py:550
  34.4 27.0 %all-to-all-start.1 = ((bf16[128,16,256]{2,1,0:T(8,128)(2,1)}), bf16[128,16,256]{2,1,0:T(8,128)(2,1)S(1)}, u32[]{:S(2)}, u32[]{:S(2)}) async-start(bf16[128,16,256]{2,1,0:T(8,128)(2,1)} %get-tuple-element.9), calls=%async_computation.1 | async-start | bytes 2097152 | tf_op jit(solution)/shard_map/all_to_all | solution.py:511
  61.5 34.8 %copy-start.1 = (bf16[4,256,768]{2,1,0:T(8,128)(2,1)S(1)}, bf16[4,256,768]{2,1,0:T(8,128)(2,1)}, u32[]{:S(2)}) copy-start(bf16[4,256,768]{2,1,0:T(8,128)(2,1)} %constant.86.clone.table_ref) | copy-start | bytes 4718596
  69.8 33.6 %copy-start.6 = (f32[4]{0:T(128)S(1)}, f32[4]{0:T(128)}, u32[]{:S(2)}) copy-start(f32[4]{0:T(128)} %param.14) | copy-start | bytes 52
  69.8 47.6 %copy-start = (bf16[4,65536]{1,0:T(4,128)(2,1)S(1)}, bf16[4,65536]{1,0:T(4,128)(2,1)}, u32[]{:S(2)}) copy-start(bf16[4,65536]{1,0:T(4,128)(2,1)} %sig_ref.1) | copy-start | bytes 1572868
  69.8 47.6 %copy-start.2 = (bf16[4,65536]{1,0:T(4,128)(2,1)S(1)}, bf16[4,65536]{1,0:T(4,128)(2,1)}, u32[]{:S(2)}) copy-start(bf16[4,65536]{1,0:T(4,128)(2,1)} %gate_ref.1) | copy-start | bytes 1572868
  99.3 18.1 %all-to-all-start.3 = ((bf16[128,16,128]{2,1,0:T(8,128)(2,1)}), bf16[128,16,128]{2,1,0:T(8,128)(2,1)S(1)}, u32[]{:S(2)}, u32[]{:S(2)}) async-start(bf16[128,16,128]{2,1,0:T(8,128)(2,1)} %last.1), calls=%async_computation.3 | async-start | bytes 1048576 | tf_op jit(solution)/shard_map/all_to_all | solution.py:511

commit v9 on v7

--- a/solution.py
+++ b/solution.py
@@ -471,15 +471,22 @@
         copy.wait()
 
 
-def finish_kernel(y_ref, sig_ref, gate_ref, skip_ref, peak_ref, out_ref, buf):
+def finish_kernel(y_ref, sig_ref, gate_ref, skip_ref, peak_ref, out_hbm, buf, out_ref, sem):
     peak = peak_ref[0:1, 0:1]
     buf[...] = decode(y_ref[...].astype(f32).reshape(ND * 16, 128), peak, CONV_CODE)
     skip = skip_ref[...]
+    writes = []
     for q in range(ND):
         at = pl.ds(q * 512, 512)
         conv = jnp.concatenate([buf[pl.ds(q * 16 + i * 4, 4), :] for i in range(4)], axis=1)
         total = conv + skip * sig_ref[:, at].astype(f32)
         out_ref[:, at] = (gate_ref[:, at].astype(f32) * total).astype(bf16)
+        if q % ROWS == ROWS - 1:
+            at = pl.ds((q + 1 - ROWS) * 512, ROWS * 512)
+            writes.append(pltpu.make_async_copy(out_ref.at[:, at], out_hbm.at[:, at], sem.at[q // ROWS]))
+            writes[-1].start()
+    for copy in writes:
+        copy.wait()
 
 
 VMEM = pl.BlockSpec(memory_space=pltpu.VMEM)
@@ -607,8 +614,9 @@
         finish_kernel,
         (conv, signal, gate, skip[:, None], peak),
         [shape(4, 65536)],
-        [((ND * 16, 128), f32)],
+        [((ND * 16, 128), f32), (signal.shape, bf16), (None, pltpu.SemaphoreType.DMA((STEPS,)))],
         "finish",
+        out_specs=[ANY],
     )
     return mixed
 

time: 120 us -> 120 us (level)
  no operation moved by 1% of the time
where the time goes in v9:
time: 120 us
  waiting for transfers between devices  34.1 us (28%)
  starting transfers between devices  28.3 us (24%)
  Pallas kernels  28.2 us (24%)
  blocking collectives  26.5 us (22%)
  local copies, waits for them, and re-layouts  1.63 us (1%)
    pallas_call x8, Pallas kernels, call(): pl.pallas_call(kernel, grid_spec=pltpu.PrefetchScalarGridSpec(num_scalar_...  28.2 us
    all_to_all x1, blocking collectives, exchange(): return lax.all_to_all(x, AXES, split_axis=0, concat_axis=0, tiled=True)  26.5 us
    all_to_all x3, starting transfers between devices, exchange(): return lax.all_to_all(x, AXES, split_axis=0, concat_axis=0, tiled=True)  20.1 us
    all_to_all x3, waiting for transfers between devices, exchange(): return lax.all_to_all(x, AXES, split_axis=0, concat_axis=0, tiled=True)  19.6 us
    ppermute x1, waiting for transfers between devices, per_device(): lax.ppermute(given[1], AXES, [(p, ND - 1 - p) for p in range(ND)])  12.2 us
    ppermute x1, starting transfers between devices, per_device(): lax.ppermute(given[0], AXES, mirror)  4.25 us
    ppermute x1, starting transfers between devices, per_device(): lax.ppermute(given[1], AXES, [(p, ND - 1 - p) for p in range(ND)])  3.96 us
  transfers between devices with their start and end apart: 5, of which 5 were waited for; matrix products, arithmetic and copies ran while one was open for 1% of the time, Pallas kernels for 11%

profile of v9, /device:TPU:1, one launch (start us, length us, event | category | flops | bytes accessed | tf_op | source)
XLA Modules:
  0.0 119.5 jit_solution(4094469174112222173)
XLA Ops:
  0.0 2.2 %pack.1 = bf16[128,4,640]{2,1,0:T(4,128)(2,1)} custom-call(bf16[4,65536]{1,0:T(4,128)(2,1)} %sig_ref.1), custom_call_target="tpu_custom_call" | custom-call | bytes 1179648 | tf_op jit(solution)/shard_map/pack/pallas_call | solution.py:498
  2.2 11.5 %all-to-all-start = ((bf16[128,4,640]{2,1,0:T(4,128)(2,1)}), bf16[128,4,640]{2,1,0:T(4,128)(2,1)S(1)}, u32[]{:S(2)}, u32[]{:S(2)}) async-start(bf16[128,4,640]{2,1,0:T(4,128)(2,1)} %pack.1), calls=%async_computation | async-start | bytes 1310720 | tf_op jit(solution)/shard_map/all_to_all | solution.py:515
  13.8 3.0 %give.2 = bf16[4,256,256]{2,1,0:T(8,128)(2,1)} custom-call(bf16[2,2,256,256]{3,2,1,0:T(8,128)(2,1)} %constant.79.clone.refs_0_, f32[2,4,2,256,256]{4,3,2,1,0:T(8,128)} %filt_hbm.1), custom_call_target="tpu_custom_call" | custom-call | flops 536870912 | bytes 5242880 | tf_op jit(solution)/shard_map/give/pallas_call | solution.py:498
  16.8 0.0 copy-start.4
  16.8 0.0 copy-start.5
  16.8 0.0 copy-start.6
  16.8 4.3 %collective-permute-start = (bf16[4,256,256]{2,1,0:T(8,128)(2,1)}, bf16[4,256,256]{2,1,0:T(8,128)(2,1)S(1)}, u32[]{:S(2)}, u32[]{:S(2)}) collective-permute-start(bf16[4,256,256]{2,1,0:T(8,128)(2,1)} %give.2), channel_id=1, source_target_pairs={{0,64},{1,127},{2,126},{3,125},{4,124},{5,123},{6,122},{7,121},{8,... | collective-permute-start | bytes 1572872 | tf_op jit(solution)/shard_map/ppermute | solution.py:553
  21.1 3.0 %give.3 = bf16[4,256,256]{2,1,0:T(8,128)(2,1)} custom-call(bf16[1,2,256,256]{3,2,1,0:T(8,128)(2,1)} %constant.80.clone.refs_0_, f32[2,4,2,256,256]{4,3,2,1,0:T(8,128)} %filt_hbm.1), custom_call_target="tpu_custom_call" | custom-call | flops 536870912 | bytes 4980736 | tf_op jit(solution)/shard_map/give/pallas_call | solution.py:498
  24.1 4.0 %collective-permute-start.1 = (bf16[4,256,256]{2,1,0:T(8,128)(2,1)}, bf16[4,256,256]{2,1,0:T(8,128)(2,1)S(1)}, u32[]{:S(2)}, u32[]{:S(2)}) collective-permute-start(bf16[4,256,256]{2,1,0:T(8,128)(2,1)} %give.3), channel_id=1, source_target_pairs={{0,127},{1,126},{2,125},{3,124},{4,123},{5,122},{6,121},{7,120},{8... | collective-permute-start | bytes 1572872 | tf_op jit(solution)/shard_map/ppermute | solution.py:554
  28.0 0.1 and_select_fusion.2
  28.1 0.1 fusion.5
  28.2 0.3 fusion.9
  28.5 0.2 sin.10
  28.8 2.2 %all-to-all-done.x_ref = bf16[128,4,640]{2,1,0:T(4,128)(2,1)S(1)} async-done(((bf16[128,4,640]{2,1,0:T(4,128)(2,1)}), bf16[128,4,640]{2,1,0:T(4,128)(2,1)S(1)}, u32[]{:S(2)}, u32[]{:S(2)}) %all-to-all-start) | async-done | bytes 655392 | tf_op jit(solution)/shard_map/all_to_all | solution.py:515
  31.0 0.0 copy-start.3
  31.0 1.2 %copy-done.3 = bf16[1024,512]{1,0:T(8,128)(2,1)S(1)} copy-done((bf16[1024,512]{1,0:T(8,128)(2,1)S(1)}, bf16[1024,512]{1,0:T(8,128)(2,1)}, u32[]{:S(2)}) %copy-start.3) | copy-done | bytes 1048600
  32.2 2.4 %outer.1 = (bf16[128,16,256]{2,1,0:T(8,128)(2,1)}, f32[8,128]{1,0:T(8,128)S(1)}) custom-call(bf16[128,4,640]{2,1,0:T(4,128)(2,1)S(1)} %all-to-all-done.x_ref, bf16[1024,512]{1,0:T(8,128)(2,1)S(1)} %copy-done.3), custom_call_target="tpu_custom_call" | custom-call | flops 536870912 | bytes 2756608 | tf_op jit(solution)/shard_map/outer/pallas_call | solution.py:498
  34.6 4.6 %all-to-all-start.1 = ((bf16[128,16,256]{2,1,0:T(8,128)(2,1)}), bf16[128,16,256]{2,1,0:T(8,128)(2,1)S(1)}, u32[]{:S(2)}, u32[]{:S(2)}) async-start(bf16[128,16,256]{2,1,0:T(8,128)(2,1)} %get-tuple-element.9), calls=%async_computation.1 | async-start | bytes 2097152 | tf_op jit(solution)/shard_map/all_to_all | solution.py:515
  39.2 2.3 %collective-permute-done.got0_ref = bf16[4,256,256]{2,1,0:T(8,128)(2,1)S(1)} collective-permute-done((bf16[4,256,256]{2,1,0:T(8,128)(2,1)}, bf16[4,256,256]{2,1,0:T(8,128)(2,1)S(1)}, u32[]{:S(2)}, u32[]{:S(2)}) %collective-permute-start) | collective-permute-done | bytes 524320 | tf_op jit(solution)/shard_map/ppermute | solution.py:553
  41.5 12.2 %collective-permute-done.1.got1_ref = bf16[4,256,256]{2,1,0:T(8,128)(2,1)S(1)} collective-permute-done((bf16[4,256,256]{2,1,0:T(8,128)(2,1)}, bf16[4,256,256]{2,1,0:T(8,128)(2,1)S(1)}, u32[]{:S(2)}, u32[]{:S(2)}) %collective-permute-start.1) | collective-permute-done | bytes 524320 | tf_op jit(solution)/shard_map/ppermute | solution.py:554
  53.7 0.0 copy-done.4
  53.7 0.0 copy-done.5
  53.7 0.0 copy-done.6
  53.7 4.2 %combine.1.bundle_hbm = f32[15,256,256]{2,1,0:T(8,128)} custom-call(f32[2,4,2,256,256]{4,3,2,1,0:T(8,128)} %filt_hbm.1, bf16[2,256,256]{2,1,0:T(8,128)(2,1)S(1)} %copy-done.5, f32[2,256,256]{2,1,0:T(8,128)S(1)} %copy-done.4, f32[2,128,128]{2,1,0:T(8,128)S(1)} %copy-done.6, bf16[4,256,256]{2,1,0:T(8,128)(2,1)S(1)} %collective-permute-done.got0_ref, ...), custom_call_target="tpu_custom_call" | custom-call | flops 17179869184 | bytes 10092544 | tf_op jit(solution)/shard_map/combine/pallas_call | solution.py:498
  57.9 3.5 %all-to-all-done.1.y_ref = bf16[128,16,256]{2,1,0:T(8,128)(2,1)S(1)} async-done(((bf16[128,16,256]{2,1,0:T(8,128)(2,1)}), bf16[128,16,256]{2,1,0:T(8,128)(2,1)S(1)}, u32[]{:S(2)}, u32[]{:S(2)}) %all-to-all-start.1) | async-done | bytes 1048608 | tf_op jit(solution)/shard_map/all_to_all | solution.py:515
  61.4 0.0 copy-start.1
  61.4 8.3 %middle.1 = bf16[128,16,256]{2,1,0:T(8,128)(2,1)S(1)} custom-call(bf16[128,16,256]{2,1,0:T(8,128)(2,1)S(1)} %all-to-all-done.1.y_ref, bf16[2,2,512,256]{3,2,1,0:T(8,128)(2,1)} %constant.85.clone.inner_hbm, f32[15,256,256]{2,1,0:T(8,128)} %combine.1.bundle_hbm, f32[8,128]{1,0:T(8,128)S(1)} %get-tuple-element.10.peak_ref, f32[3,6,256]{2,1,0:T(8,128)S(1)} %reshape.294.wave_ref), custom_call_target="tpu_custom_call" | custom-call | flops 4294967296 | bytes 7100416 | tf_op jit(solution)/shard_map/middle/pallas_call | solution.py:498
  69.7 0.0 copy-start.7
  69.8 0.0 copy-start
  69.8 0.0 copy-start.2
  69.8 26.5 %all_to_all.20.y_ref = bf16[128,16,256]{2,1,0:T(8,128)(2,1)S(1)} all-to-all(bf16[128,16,256]{2,1,0:T(8,128)(2,1)S(1)} %middle.1), channel_id=1, replica_groups=mesh['wide'=16,'narrow'=8] {'wide','narrow'}, dimensions={0} | all-to-all | bytes 2097152 | tf_op jit(solution)/shard_map/all_to_all | solution.py:515
  96.3 0.0 copy-done.1
  96.3 3.0 %last.1 = bf16[128,16,128]{2,1,0:T(8,128)(2,1)} custom-call(bf16[128,16,256]{2,1,0:T(8,128)(2,1)S(1)} %all_to_all.20.y_ref, bf16[4,256,768]{2,1,0:T(8,128)(2,1)S(1)} %copy-done.1, f32[8,128]{1,0:T(8,128)S(1)} %get-tuple-element.10.peak_ref), custom_call_target="tpu_custom_call" | custom-call | flops 536870912 | bytes 3149824 | tf_op jit(solution)/shard_map/last/pallas_call | solution.py:498
  99.4 4.0 %all-to-all-start.3 = ((bf16[128,16,128]{2,1,0:T(8,128)(2,1)}), bf16[128,16,128]{2,1,0:T(8,128)(2,1)S(1)}, u32[]{:S(2)}, u32[]{:S(2)}) async-start(bf16[128,16,128]{2,1,0:T(8,128)(2,1)} %last.1), calls=%async_computation.3 | async-start | bytes 1048576 | tf_op jit(solution)/shard_map/all_to_all | solution.py:515
  103.4 0.0 copy-done.7
  103.4 0.1 copy.15.skip_ref
  103.5 13.9 %all-to-all-done.3.y_ref = bf16[128,16,128]{2,1,0:T(8,128)(2,1)S(1)} async-done(((bf16[128,16,128]{2,1,0:T(8,128)(2,1)}), bf16[128,16,128]{2,1,0:T(8,128)(2,1)S(1)}, u32[]{:S(2)}, u32[]{:S(2)}) %all-to-all-start.3) | async-done | bytes 524320 | tf_op jit(solution)/shard_map/all_to_all | solution.py:515
  117.4 0.0 copy-done
  117.4 0.0 copy-done.2
  117.4 1.9 %finish.1 = bf16[4,65536]{1,0:T(4,128)(2,1)} custom-call(bf16[128,16,128]{2,1,0:T(8,128)(2,1)S(1)} %all-to-all-done.3.y_ref, bf16[4,65536]{1,0:T(4,128)(2,1)S(1)} %copy-done, bf16[4,65536]{1,0:T(4,128)(2,1)S(1)} %copy-done.2, f32[4,1]{1,0:T(4,128)S(1)} %copy.15.skip_ref, f32[8,128]{1,0:T(8,128)S(1)} %get-tuple-element.10.peak_ref), custom_call_target="tpu_custom_call" | custom-call | bytes 2101264 | tf_op jit(solution)/shard_map/finish/pallas_call | solution.py:498
  (3 shorter events, 0.0 us)
Async XLA Ops:
  2.2 28.8 %all-to-all-start = ((bf16[128,4,640]{2,1,0:T(4,128)(2,1)}), bf16[128,4,640]{2,1,0:T(4,128)(2,1)S(1)}, u32[]{:S(2)}, u32[]{:S(2)}) async-start(bf16[128,4,640]{2,1,0:T(4,128)(2,1)} %pack.1), calls=%async_computation | async-start | bytes 1310720 | tf_op jit(solution)/shard_map/all_to_all | solution.py:515
  16.8 36.9 %copy-start.4 = (f32[2,256,256]{2,1,0:T(8,128)S(1)}, f32[2,256,256]{2,1,0:T(8,128)}, u32[]{:S(2)}) copy-start(f32[2,256,256]{2,1,0:T(8,128)} %constant.83.clone.cross_base_ref) | copy-start | bytes 1572868
  16.8 36.9 %copy-start.5 = (bf16[2,256,256]{2,1,0:T(8,128)(2,1)S(1)}, bf16[2,256,256]{2,1,0:T(8,128)(2,1)}, u32[]{:S(2)}) copy-start(bf16[2,256,256]{2,1,0:T(8,128)(2,1)} %constant.84.clone.order_ref) | copy-start | bytes 786436
  16.8 36.9 %copy-start.6 = (f32[2,128,128]{2,1,0:T(8,128)S(1)}, f32[2,128,128]{2,1,0:T(8,128)}, u32[]{:S(2)}) copy-start(f32[2,128,128]{2,1,0:T(8,128)} %constant.82.clone.base_ref) | copy-start | bytes 393220
  16.8 24.7 %collective-permute-start = (bf16[4,256,256]{2,1,0:T(8,128)(2,1)}, bf16[4,256,256]{2,1,0:T(8,128)(2,1)S(1)}, u32[]{:S(2)}, u32[]{:S(2)}) collective-permute-start(bf16[4,256,256]{2,1,0:T(8,128)(2,1)} %give.2), channel_id=1, source_target_pairs={{0,64},{1,127},{2,126},{3,125},{4,124},{5,123},{6,122},{7,121},{8,... | collective-permute-start | bytes 1572872 | tf_op jit(solution)/shard_map/ppermute | solution.py:553
  24.1 29.6 %collective-permute-start.1 = (bf16[4,256,256]{2,1,0:T(8,128)(2,1)}, bf16[4,256,256]{2,1,0:T(8,128)(2,1)S(1)}, u32[]{:S(2)}, u32[]{:S(2)}) collective-permute-start(bf16[4,256,256]{2,1,0:T(8,128)(2,1)} %give.3), channel_id=1, source_target_pairs={{0,127},{1,126},{2,125},{3,124},{4,123},{5,122},{6,121},{7,120},{8... | collective-permute-start | bytes 1572872 | tf_op jit(solution)/shard_map/ppermute | solution.py:554
  31.0 1.2 %copy-start.3 = (bf16[1024,512]{1,0:T(8,128)(2,1)S(1)}, bf16[1024,512]{1,0:T(8,128)(2,1)}, u32[]{:S(2)}) copy-start(bf16[1024,512]{1,0:T(8,128)(2,1)} %constant.81.clone.table_ref) | copy-start | bytes 3145732
  34.6 26.8 %all-to-all-start.1 = ((bf16[128,16,256]{2,1,0:T(8,128)(2,1)}), bf16[128,16,256]{2,1,0:T(8,128)(2,1)S(1)}, u32[]{:S(2)}, u32[]{:S(2)}) async-start(bf16[128,16,256]{2,1,0:T(8,128)(2,1)} %get-tuple-element.9), calls=%async_computation.1 | async-start | bytes 2097152 | tf_op jit(solution)/shard_map/all_to_all | solution.py:515
  61.4 34.9 %copy-start.1 = (bf16[4,256,768]{2,1,0:T(8,128)(2,1)S(1)}, bf16[4,256,768]{2,1,0:T(8,128)(2,1)}, u32[]{:S(2)}) copy-start(bf16[4,256,768]{2,1,0:T(8,128)(2,1)} %constant.86.clone.table_ref) | copy-start | bytes 4718596
  69.7 33.6 %copy-start.7 = (f32[4]{0:T(128)S(1)}, f32[4]{0:T(128)}, u32[]{:S(2)}) copy-start(f32[4]{0:T(128)} %param.14) | copy-start | bytes 52
  69.8 47.7 %copy-start = (bf16[4,65536]{1,0:T(4,128)(2,1)S(1)}, bf16[4,65536]{1,0:T(4,128)(2,1)}, u32[]{:S(2)}) copy-start(bf16[4,65536]{1,0:T(4,128)(2,1)} %sig_ref.1) | copy-start | bytes 1572868
  69.8 47.7 %copy-start.2 = (bf16[4,65536]{1,0:T(4,128)(2,1)S(1)}, bf16[4,65536]{1,0:T(4,128)(2,1)}, u32[]{:S(2)}) copy-start(bf16[4,65536]{1,0:T(4,128)(2,1)} %gate_ref.1) | copy-start | bytes 1572868
  99.4 18.1 %all-to-all-start.3 = ((bf16[128,16,128]{2,1,0:T(8,128)(2,1)}), bf16[128,16,128]{2,1,0:T(8,128)(2,1)S(1)}, u32[]{:S(2)}, u32[]{:S(2)}) async-start(bf16[128,16,128]{2,1,0:T(8,128)(2,1)} %last.1), calls=%async_computation.3 | async-start | bytes 1048576 | tf_op jit(solution)/shard_map/all_to_all | solution.py:515
